TPU v7x, 32 devices: a whole 2x2x4 slice. The times are simulated.
32 devices in a mesh: fsdp: 8 (over y, x, core), seq: 4 (over z).
Axes of the slice: x: 2, y: 2, z: 4, core: 2. Of those that a mesh axis runs over, the one named last changes fastest.
Arguments:
- tokens: bfloat16 [16384, 768], P(('fsdp', 'seq')), may hold values from -6 to 6
- doc_lengths: int32 [8, 3], P('fsdp'), may hold values from 1 to 1024, 2048 in all within a row
- gain_attn: bfloat16 [768], P('fsdp'), may hold values from 0.5 to 1.5
- query_weight: bfloat16 [768, 768], P('fsdp'), may hold values from -0.02734375 to 0.02734375
- key_weight: bfloat16 [768, 768], P('fsdp'), may hold values from -0.21875 to 0.21875
- value_weight: bfloat16 [768, 768], P('fsdp'), may hold values from -0.21875 to 0.21875
- out_weight: bfloat16 [768, 768], P('fsdp'), may hold values from -0.875 to 0.875
- bias_table: bfloat16 [384], P('fsdp'), may hold values from -4 to 4
- gain_ff: bfloat16 [768], P('fsdp'), may hold values from 0.5 to 1.5
- ff_in: bfloat16 [768, 3072], P('fsdp'), may hold values from -0.21875 to 0.21875
- ff_out: bfloat16 [3072, 768], P('fsdp'), may hold values from -0.109375 to 0.109375
- gain_self: bfloat16 [768], P('fsdp'), may hold values from 0.5 to 1.5
- self_value: bfloat16 [768, 768], P('fsdp'), may hold values from -0.21875 to 0.21875
- self_out: bfloat16 [768, 768], P('fsdp'), may hold values from -0.21875 to 0.21875
- gain_cross: bfloat16 [768], P('fsdp'), may hold values from 0.5 to 1.5
- cross_query: bfloat16 [768, 768], P('fsdp'), may hold values from -0.02734375 to 0.02734375
- cross_key: bfloat16 [768, 768], P('fsdp'), may hold values from -0.21875 to 0.21875
- cross_value: bfloat16 [768, 768], P('fsdp'), may hold values from -0.21875 to 0.21875
- cross_out: bfloat16 [768, 768], P('fsdp'), may hold values from -0.875 to 0.875
- gain_dff: bfloat16 [768], P('fsdp'), may hold values from 0.5 to 1.5
- dff_in: bfloat16 [768, 3072], P('fsdp'), may hold values from -0.21875 to 0.21875
- dff_out: bfloat16 [3072, 768], P('fsdp'), may hold values from -0.109375 to 0.109375
- enc_cot: bfloat16 [16384, 768], P(('fsdp', 'seq')), may hold values from -6 to 6
- dec_cot: bfloat16 [24, 768], P('fsdp'), may hold values from -6 to 6
Outputs:
- enc_hidden: float32 [16384, 768], P(('fsdp', 'seq'))
- dec_hidden: float32 [24, 768], P('fsdp')
- tokens_grad: float32 [16384, 768], P(('fsdp', 'seq'))
- gain_attn_grad: float32 [768], P('fsdp')
- query_weight_grad: float32 [768, 768], P('fsdp')
- key_weight_grad: float32 [768, 768], P('fsdp')
- value_weight_grad: float32 [768, 768], P('fsdp')
- out_weight_grad: float32 [768, 768], P('fsdp')
- bias_table_grad: float32 [384], P('fsdp')
- gain_ff_grad: float32 [768], P('fsdp')
- ff_in_grad: float32 [768, 3072], P('fsdp')
- ff_out_grad: float32 [3072, 768], P('fsdp')
- gain_self_grad: float32 [768], P('fsdp')
- self_value_grad: float32 [768, 768], P('fsdp')
- self_out_grad: float32 [768, 768], P('fsdp')
- gain_cross_grad: float32 [768], P('fsdp')
- cross_query_grad: float32 [768, 768], P('fsdp')
- cross_key_grad: float32 [768, 768], P('fsdp')
- cross_value_grad: float32 [768, 768], P('fsdp')
- cross_out_grad: float32 [768, 768], P('fsdp')
- gain_dff_grad: float32 [768], P('fsdp')
- dff_in_grad: float32 [768, 3072], P('fsdp')
- dff_out_grad: float32 [3072, 768], P('fsdp')
Inputs may be any that keep to these rules, and one draw needn't show every extreme that they name: `doc_lengths`: row g gives, in order, the lengths of the 3 documents that make up tokens g * 2048 to (g + 1) * 2048 - 1; every row sums to 2048, and in every row the longest is exactly 1024.
All inputs are finite; a program needn't handle non-finite values.
Results may differ from a plain program's by a relative error of at most 0.022.
Values may be sent and summed in bfloat16 or wider, within the bound.
A program may use at most 256 MiB of HBM per device.

v0:
```python
import functools, math
import jax, jax.numpy as jnp
from jax import lax
from jax.experimental import pallas as pl
from jax.experimental.pallas import tpu as pltpu
from jax.sharding import PartitionSpec as P

HEADS=12; HEAD=64; BUCKETS=32
LIMITS = (12, 16, 23, 32, 46, 64, 91)
BLK=256
SUB=128
BAND=512
NEG=-1e30

def bucket_of(relative):
    distance = jnp.abs(relative)
    bucket = jnp.minimum(distance, 8)
    for bound_value in LIMITS:
        bucket = bucket + (distance >= bound_value).astype(jnp.int32)
    return bucket + 16 * (relative > 0).astype(jnp.int32)

def nt(a,b):
    return lax.dot_general(a,b,(((1,),(1,)),((),())),preferred_element_type=jnp.float32)
def tn(a,b):
    return lax.dot_general(a,b,(((0,),(0,)),((),())),preferred_element_type=jnp.float32)
def nn(a,b):
    return lax.dot_general(a,b,(((1,),(0,)),((),())),preferred_element_type=jnp.float32)

def band_offsets(sign):
    c = jnp.arange(BAND, dtype=jnp.int32)
    t = jnp.where(c < 3*SUB, c, c - BAND) - SUB
    return sign * t

def seg_of(pos, e0, e1):
    return (pos >= e0).astype(jnp.int32) + (pos >= e1).astype(jnp.int32)

def build_tiles(band_ref, tiles, hh, flip):
    row = band_ref[hh:hh+1, :]
    x = jnp.broadcast_to(row, (SUB, BAND))
    x = pltpu.roll(x, 0, 1, stride=1, stride_axis=0)
    last, first = row[0:1, 3*SUB-1:3*SUB], row[0:1, 3*SUB:3*SUB+1]
    near = [x[:, n*SUB:(n+1)*SUB] for n in range(3)]
    if flip:
        near = near[::-1]
        last, first = first, last
    low = jnp.broadcast_to(first, (SUB, SUB))
    high = jnp.broadcast_to(last, (SUB, SUB))
    for d in range(5):
        for r in range(2):
            for c in range(2):
                off = ((r - c) if flip else (c - r)) + 2*(d-2)
                tiles[hh, d, r*SUB:(r+1)*SUB, c*SUB:(c+1)*SUB] = low if off < -1 else high if off > 1 else near[off+1]

def fwd_kernel(info, band_ref, q_ref, k_ref, v_ref, ctx_ref, lse_ref, tiles, s_scr):
    p0, e0, e1 = info[0], info[1], info[2]
    T = q_ref.shape[0]; G = k_ref.shape[0]
    lane = lax.broadcasted_iota(jnp.int32, (1,128), 1)
    left = lane < HEAD
    for hh in range(2):
        build_tiles(band_ref, tiles, hh, False)
    for i in range(T//BLK):
        a = p0 + i*BLK; b = a + BLK - 1
        lo = jnp.where(a >= e1, e1, jnp.where(a >= e0, e0, 0))
        hi = jnp.where(b >= e1, G, jnp.where(b >= e0, e1, e0))
        j0 = lo // BLK; j1 = (hi + BLK - 1)//BLK
        ib = a // BLK
        qb = q_ref[i*BLK:(i+1)*BLK, :]
        row_pos = a + lax.broadcasted_iota(jnp.int32, (BLK,1), 0)
        row_seg = jnp.broadcast_to(seg_of(row_pos, e0, e1),(BLK,128))
        zero = jnp.zeros_like(qb)
        qh = [jnp.where(left, qb, zero), jnp.where(left, zero, qb)]
        def score(j, carry):
            koff = pl.multiple_of(lax.rem(j*BLK + G - p0, G), BLK)
            kb = k_ref[pl.ds(koff, BLK), :]
            kpos = j*BLK + lax.broadcasted_iota(jnp.int32, (1,BLK), 1)
            kseg = seg_of(kpos, e0, e1)
            same = jnp.concatenate([row_seg == kseg[:, :128], row_seg == kseg[:,128:]],axis=1)
            d = jnp.clip(j - ib, -2, 2) + 2
            out = []
            for hh in range(2):
                s = nt(qh[hh], kb) + tiles[hh, d]
                s = jnp.where(same, s, NEG)
                s_scr[hh, j] = s
                out.append(jnp.maximum(carry[hh], jnp.maximum(s[:, :128], s[:, 128:])))
            return tuple(out)
        init = jnp.full((BLK,128), NEG, jnp.float32)
        mx = lax.fori_loop(j0, j1, score, (init, init))
        top = [jnp.max(m, axis=1, keepdims=True) for m in mx]
        def weigh(j, carry):
            koff = pl.multiple_of(lax.rem(j*BLK + G - p0, G), BLK)
            vb = v_ref[pl.ds(koff, BLK), :]
            one = jnp.ones_like(vb)
            vh = [jnp.where(left, vb, one), jnp.where(left, one, vb)]
            out = []
            for hh in range(2):
                p = jnp.exp(s_scr[hh, j] - top[hh]).astype(jnp.bfloat16)
                out.append(carry[hh] + nn(p, vh[hh]))
            return tuple(out)
        zf = jnp.zeros((BLK,128), jnp.float32)
        acc = lax.fori_loop(j0, j1, weigh, (zf, zf))
        tot = [jnp.where(left, pltpu.roll(acc[0], HEAD, 1), pltpu.roll(acc[1], HEAD, 1))]
        num = jnp.where(left, acc[0], acc[1])
        total = tot[0]
        ctx_ref[i*BLK:(i+1)*BLK, :] = (num / total).astype(jnp.bfloat16)
        lse_ref[i*BLK:(i+1)*BLK, :] = jnp.where(left, top[0], top[1]) + jnp.log(total)

def attn_fwd(info, band, q, k, v):
    T=q.shape[0]; G=k.shape[0]; W=q.shape[1]
    pairs=W//128
    return pl.pallas_call(
        fwd_kernel,
        grid=(pairs,),
        in_specs=[pl.BlockSpec(memory_space=pltpu.SMEM),
                  pl.BlockSpec((None,2,BAND), lambda p:(p,0,0)),
                  pl.BlockSpec((T,128), lambda p:(0,p)),
                  pl.BlockSpec((G,128), lambda p:(0,p)),
                  pl.BlockSpec((G,128), lambda p:(0,p))],
        out_specs=[pl.BlockSpec((T,128), lambda p:(0,p)), pl.BlockSpec((T,128), lambda p:(0,p))],
        out_shape=[jax.ShapeDtypeStruct((T,W), jnp.bfloat16), jax.ShapeDtypeStruct((T,W), jnp.float32)],
        scratch_shapes=[pltpu.VMEM((2,5,BLK,BLK), jnp.float32), pltpu.VMEM((2,G//BLK,BLK,BLK), jnp.float32)],
        compiler_params=pltpu.CompilerParams(vmem_limit_bytes=24<<20),
        cost_estimate=pl.CostEstimate(flops=4*HEADS*T*1280*128, bytes_accessed=4*G*W+8*T*W, transcendentals=HEADS*T*1280),
    )(info, band, q, k, v)

def bwd_kernel(info, band_ref, q_ref, k_ref, v_ref, g_ref, ctx_ref, lse_ref, gq_ref, gk_ref, gv_ref, gb_ref, gf_ref, tiles, gt, gk_acc, gv_acc):
    p0, e0, e1 = info[0], info[1], info[2]
    T = q_ref.shape[0]; G = k_ref.shape[0]
    lane = lax.broadcasted_iota(jnp.int32, (1,128), 1)
    left = lane < HEAD
    sub_left = lax.broadcasted_iota(jnp.int32, (128,1), 0) < HEAD
    for hh in range(2):
        build_tiles(band_ref, tiles, hh, True)
    gt[...] = jnp.zeros_like(gt)
    gk_acc[...] = jnp.zeros_like(gk_acc)
    gv_acc[...] = jnp.zeros_like(gv_acc)
    for i in range(T//BLK):
        a = p0 + i*BLK; b = a + BLK - 1
        lo = jnp.where(a >= e1, e1, jnp.where(a >= e0, e0, 0))
        hi = jnp.where(b >= e1, G, jnp.where(b >= e0, e1, e0))
        j0 = lo // BLK; j1 = (hi + BLK - 1)//BLK
        ib = a // BLK
        rows = slice(i*BLK,(i+1)*BLK)
        qb = q_ref[rows, :]; gb = g_ref[rows, :]
        zero = jnp.zeros_like(qb)
        qh = [jnp.where(left, qb, zero), jnp.where(left, zero, qb)]
        gh = [jnp.where(left, gb, zero), jnp.where(left, zero, gb)]
        prod = (gb.astype(jnp.float32) * ctx_ref[rows,:].astype(jnp.float32)).T
        lse_t = lse_ref[rows,:].T
        dot = [jnp.sum(prod[hh*HEAD:(hh+1)*HEAD], axis=0, keepdims=True) for hh in range(2)]
        lse = [lse_t[hh*HEAD:hh*HEAD+1] for hh in range(2)]
        q_pos = a + lax.broadcasted_iota(jnp.int32, (1,BLK), 1)
        q_seg = seg_of(q_pos, e0, e1)
        def step(j, carry):
            koff = pl.multiple_of(lax.rem(j*BLK + G - p0, G), BLK)
            kb = k_ref[pl.ds(koff, BLK), :]
            vb = v_ref[pl.ds(koff, BLK), :]
            kpos = j*BLK + lax.broadcasted_iota(jnp.int32, (BLK,1), 0)
            same = jnp.broadcast_to(seg_of(kpos, e0, e1), (BLK,BLK)) == jnp.broadcast_to(q_seg, (BLK,BLK))
            d = jnp.clip(j - ib, -2, 2) + 2
            gqs=[]
            gk = None; gv=None
            for hh in range(2):
                s = nt(kb, qh[hh]) + tiles[hh, d]
                s = jnp.where(same, s, NEG)
                p = jnp.exp(s - lse[hh])
                gp = nt(vb, gh[hh])
                gs = p * (gp - dot[hh])
                gt[hh, d] += gs
                pb = p.astype(jnp.bfloat16); gsb = gs.astype(jnp.bfloat16)
                tk = nn(gsb, qh[hh]); tv = nn(pb, gh[hh])
                gk = tk if gk is None else gk + tk
                gv = tv if gv is None else gv + tv
                gqs.append(carry[hh] + tn(gsb, kb))
            gk_acc[pl.ds(koff,BLK), :] += gk
            gv_acc[pl.ds(koff,BLK), :] += gv
            return tuple(gqs)
        zf = jnp.zeros((BLK,128), jnp.float32)
        gq = lax.fori_loop(j0, j1, step, (zf, zf))
        gq_ref[rows,:] = jnp.where(left, gq[0], gq[1]).astype(jnp.bfloat16)
    gk_ref[...] = gk_acc[...].astype(jnp.bfloat16)
    gv_ref[...] = gv_acc[...].astype(jnp.bfloat16)
    for hh in range(2):
        near = [None]*3; low = None; high = None
        for d in range(5):
            for r in range(2):
                for c in range(2):
                    off = r - c + 2*(d-2)
                    x = gt[hh, d, r*SUB:(r+1)*SUB, c*SUB:(c+1)*SUB]
                    if off < -1: low = x if low is None else low + x
                    elif off > 1: high = x if high is None else high + x
                    else: near[off+1] = x if near[off+1] is None else near[off+1] + x
        x = jnp.concatenate([near[2], near[1], near[0], jnp.zeros((SUB,SUB),jnp.float32)], axis=1)
        rows_left = SUB
        while rows_left > 1:
            rows_left //= 2
            x = x[:rows_left] + pltpu.roll(x[rows_left:], BAND - rows_left, 1)
        gb_ref[hh:hh+1,:] = x
        gf_ref[hh:hh+1,:] = jnp.concatenate([jnp.sum(low, axis=0, keepdims=True), jnp.sum(high, axis=0, keepdims=True)], axis=1)

def attn_bwd(info, band, q, k, v, g, ctx, lse, first_pair, count, into):
    T=q.shape[0]; G=k.shape[0]; W=q.shape[1]
    at = lambda rows: pl.BlockSpec((rows,128), lambda p:(0,p+first_pair))
    kernel = bwd_kernel
    if into is not None:
        kernel = lambda *refs: bwd_kernel(*refs[:8], *refs[13:])
    extra = [] if into is None else list(into)
    small = lambda n: pl.BlockSpec((None,2,n), lambda p:(p+first_pair,0,0))
    pairs=W//128
    return pl.pallas_call(
        kernel,
        grid=(count,),
        in_specs=[pl.BlockSpec(memory_space=pltpu.SMEM), small(BAND),
                  at(T), at(G), at(G), at(T), at(T), at(T)] + [pl.BlockSpec(memory_space=pl.ANY)]*len(extra),
        out_specs=[at(T), at(G), at(G), small(BAND), small(2*SUB)],
        out_shape=[jax.ShapeDtypeStruct((T,W), jnp.bfloat16), jax.ShapeDtypeStruct((G,W), jnp.bfloat16), jax.ShapeDtypeStruct((G,W), jnp.bfloat16),
                   jax.ShapeDtypeStruct((pairs,2,BAND), jnp.float32), jax.ShapeDtypeStruct((pairs,2,2*SUB), jnp.float32)],
        scratch_shapes=[pltpu.VMEM((2,5,BLK,BLK), jnp.float32), pltpu.VMEM((2,5,BLK,BLK), jnp.float32),
                        pltpu.VMEM((G,128), jnp.float32), pltpu.VMEM((G,128), jnp.float32)],
        input_output_aliases={8+n: n for n in range(len(extra))},
        compiler_params=pltpu.CompilerParams(vmem_limit_bytes=24<<20),
        cost_estimate=pl.CostEstimate(flops=count*10*2*T*1280*128*4, bytes_accessed=(8*G*W+12*T*W)*count//pairs, transcendentals=2*count*T*1280),
    )(info, band, q, k, v, g, ctx, lse, *extra)

def make_band(table, sign):
    off = band_offsets(sign)
    oh = (bucket_of(off)[None,:] == jnp.arange(BUCKETS, dtype=jnp.int32)[:,None]).astype(jnp.bfloat16)
    return jnp.dot(table, oh, preferred_element_type=jnp.float32).reshape(HEADS//2, 2, BAND)

def table_grad(gb, gf):
    oh = (bucket_of(band_offsets(-1))[:,None] == jnp.arange(BUCKETS, dtype=jnp.int32)[None,:]).astype(jnp.float32)
    t = jnp.dot(gb.reshape(HEADS,BAND), oh, precision=lax.Precision.HIGHEST)
    f = gf.reshape(HEADS, 2, SUB).sum(axis=2)
    return t.at[:,15].add(f[:,0]).at[:,31].add(f[:,1])


DOC_MAX = 1024


def swap(values, axis, bit):
    count = lax.axis_size(axis)
    return lax.ppermute(values, axis, [(n, n ^ bit) for n in range(count)])


def shift(values, axis, step):
    count = lax.axis_size(axis)
    return lax.ppermute(values, axis, [(n, n + step) for n in range(count) if 0 <= n + step < count])


def bits_of(axis):
    bits = []
    while 1 << len(bits) < lax.axis_size(axis):
        bits.append(1 << len(bits))
    return bits


def pick_at(values, index, dim):
    return lax.dynamic_index_in_dim(values, index, dim, keepdims=False)


def add_low(left, right):
    return (left.astype(jnp.float32) + right.astype(jnp.float32)).astype(jnp.bfloat16)


def scatter_core(pieces):
    index = lax.axis_index("fsdp")
    core = index % 2
    halves = [piece.reshape((piece.shape[0] // 2, 2) + piece.shape[1:]) for piece in pieces]
    send = jnp.concatenate([pick_at(half, 1 - core, 1) for half in halves], axis=2)
    keep = jnp.concatenate([pick_at(half, core, 1) for half in halves], axis=2)
    return add_low(keep, swap(send, "fsdp", 1))


def scatter_chips(piece):
    index = lax.axis_index("fsdp") // 2
    done = 2
    while piece.shape[0] > 1:
        step = min(4, piece.shape[0])
        piece = piece.reshape((piece.shape[0] // step, step) + piece.shape[1:])
        place = index % step
        total = pick_at(piece, place, 1).astype(jnp.float32)
        for other in range(1, step):
            total = total + swap(pick_at(piece, place ^ other, 1), "fsdp", other * done).astype(jnp.float32)
        piece = total.astype(jnp.bfloat16)
        index = index // step
        done = done * step
    return piece[0]


def halve_seq(piece, bit, dim):
    mine = lax.axis_index("seq") // bit % 2
    low, high = jnp.split(piece, 2, axis=dim)
    return add_low(jnp.where(mine == 0, low, high), swap(jnp.where(mine == 0, high, low), "seq", bit))


def whole_seq(pieces, dims, width):
    index = lax.axis_index("seq")
    for bit in bits_of("seq")[::-1]:
        mine = index // bit % 2
        shapes = [piece.shape for piece in pieces]
        flat = [jnp.concatenate(jnp.split(piece, piece.shape[1] // width, axis=1), axis=0) for piece in pieces]
        come = swap(jnp.concatenate(flat, axis=0), "seq", bit)
        at = 0
        for n, (shape, dim) in enumerate(zip(shapes, dims)):
            rows = flat[n].shape[0]
            other = come[at : at + rows]
            at += rows
            other = jnp.concatenate(jnp.split(other, shape[1] // width, axis=0), axis=1)
            pieces[n] = jnp.concatenate([jnp.where(mine == 0, pieces[n], other), jnp.where(mine == 0, other, pieces[n])], axis=dim)
    return pieces


def sum_seq(piece, dim):
    for bit in bits_of("seq"):
        piece = halve_seq(piece, bit, dim)
    return whole_seq([piece], [dim], piece.shape[1])[0]


def gather_seq(values):
    index = lax.axis_index("seq")
    count = lax.axis_size("seq")
    turn = lambda step: lax.ppermute(values, "seq", [(n, (n + step) % count) for n in range(count)])
    found = jnp.stack([values] + [turn(step) for step in range(count - 1, 0, -1)])
    order = (jnp.arange(count) - index) % count
    return jnp.stack([pick_at(found, order[n], 0) for n in range(count)])


def window_blocks(rows):
    return min(lax.axis_size("seq") - 1, -(-(DOC_MAX - 1) // rows))


def gather_window(values, beside):
    rows = values.shape[0]
    count, reach = lax.axis_size("seq"), window_blocks(rows)
    left, right = [values], [values]
    for far in range(reach):
        left.append(shift(left[-1], "seq", 1))
        right.append(shift(right[-1], "seq", -1))
        if far == 0:
            left[1], right[1], beside = lax.optimization_barrier((left[1], right[1], beside))
    slots = [values]
    for place in range(1, count):
        found = [right[place]] if place <= reach else []
        found += [left[count - place]] if count - place <= reach else []
        slots.append(sum(found[1:], found[0]) if found else jnp.zeros_like(values))
    return jnp.concatenate(slots, axis=0), beside


def scatter_window(block, reach):
    total = None
    carried = {}
    for far in range(reach, 0, -1):
        for sign in (1, -1):
            term = block(sign * far)
            moving = term.astype(jnp.bfloat16) if far == reach else add_low(term, carried[sign])
            carried[sign] = shift(moving, "seq", sign)
    return carried[1].astype(jnp.float32) + carried[-1].astype(jnp.float32)


eps = 1e-06
GELU_COEF = 0.044715
GELU_ROOT = math.sqrt(2.0 / math.pi)
bf16 = jnp.bfloat16
f32 = jnp.float32


def gelu_both(values):
    inner = GELU_ROOT * (values + GELU_COEF * values * values * values)
    tanh_val = jnp.tanh(inner)
    half = 0.5 * (1.0 + tanh_val)
    slope = half + 0.5 * values * (1.0 - tanh_val * tanh_val) * GELU_ROOT * (
        1.0 + 3.0 * GELU_COEF * values * values
    )
    return values * half, slope


def norm_forward(values, gain_vec):
    inverse = lax.rsqrt(jnp.mean(values * values, axis=-1, keepdims=True) + eps)
    return (values * inverse * gain_vec).astype(bf16), inverse


def norm_backward(values, inverse, gain_vec, grad_normed):
    scaled = grad_normed * gain_vec
    cubed = inverse * inverse * inverse
    grad_values = inverse * scaled - values * cubed * jnp.mean(
        scaled * values, axis=-1, keepdims=True
    )
    return grad_values


def body(
    tokens, doc_lengths, gain_attn, query_weight, key_weight, value_weight, out_weight, bias_table,
    gain_ff, ff_in, ff_out, gain_self, self_value, self_out, gain_cross, cross_query, cross_key,
    cross_value, cross_out, gain_dff, dff_in, dff_out, enc_cot, dec_cot,
):
    seq_index = lax.axis_index("seq")
    seq_count = lax.axis_size("seq")
    own = lax.axis_index("fsdp")
    fsdp = lax.axis_size("fsdp")
    rows = tokens.shape[0]
    width = tokens.shape[1]
    group_tok = rows * seq_count
    part = query_weight.shape[0]
    buckets_part = bias_table.shape[0]
    docs = doc_lengths.shape[1]

    columns = [gain_attn, gain_ff, gain_self, gain_cross, gain_dff,
               jnp.pad(bias_table, (0, part - buckets_part))]
    small = jnp.pad(jnp.stack(columns, axis=1), ((0, 0), (0, 128 - len(columns))))
    over_fsdp = lambda pieces: lax.all_gather(jnp.concatenate(pieces, axis=1), "fsdp", axis=0, tiled=True)
    held = (out_weight, ff_in, self_value, self_out, cross_query, cross_key, cross_value, cross_out, dff_in)
    group, held = gather_window(tokens, held)
    first_weights = over_fsdp([query_weight, key_weight, value_weight, small])
    out_weight_b, ff_in_b, self_value_b, self_out_b, cross_query_b, cross_key_b, cross_value_b, cross_out_b, dff_in_b = held
    wide = dff_out.shape[0] // part
    units = dff_out.shape[0] // seq_count
    dff_in_part = pick_at(dff_in_b.reshape(part, fsdp, seq_count, units), seq_index, 2).reshape(part, fsdp * units)
    dff_out_part = lax.dynamic_slice_in_dim(dff_out, seq_index * units, units, 0)
    second_weights = over_fsdp([out_weight_b, ff_in_b, self_value_b, self_out_b, cross_query_b, cross_key_b])
    ff_out_full = over_fsdp([ff_out])
    third_weights = over_fsdp([cross_value_b, cross_out_b, dff_in_part, dff_out_part])

    query_full = first_weights[:, :width]
    kv_full = first_weights[:, width : 3 * width]
    vectors = first_weights[:, 3 * width : 3 * width + len(columns)].astype(f32)
    gain_attn_f, gain_ff_f, gain_self_f, gain_cross_f, gain_dff_f = (vectors[:, n] for n in range(5))
    table = vectors[:, 5].reshape(fsdp, part)[:, :buckets_part].reshape(HEADS, BUCKETS).astype(bf16)
    span = lambda start, count: second_weights[:, start * width : (start + count) * width]
    out_full = span(0, 1)
    ff_in_full = span(1, wide)
    self_value_full, self_out_full, cross_query_full, cross_key_full = (span(1 + wide + n, 1) for n in range(4))
    cross_value_full, cross_out_full, dff_in_full, dff_out_full = (
        third_weights[:, n * width : (n + 1) * width] for n in range(4))
    lengths = doc_lengths[0]
    end_zero = lengths[0]
    end_one = lengths[0] + lengths[1]
    here = seq_index * rows
    info = jnp.stack([here.astype(jnp.int32), end_zero, end_one])
    local_seg = seg_of(here + jnp.arange(rows, dtype=jnp.int32), end_zero, end_one)
    starts = jnp.stack([jnp.zeros_like(end_zero), end_zero, end_one])

    tokens_f = tokens.astype(f32)
    normed_all, inverse_all = norm_forward(group.astype(f32), gain_attn_f)
    normed, inverse_attn = normed_all[:rows], inverse_all[:rows]
    query = nn(normed, query_full).astype(bf16)
    key = nn(normed_all, kv_full[:, :width]).astype(bf16)
    value = nn(normed_all, kv_full[:, width:]).astype(bf16)
    context, lse = attn_fwd(info, make_band(table, 1), query, key, value)
    middle = tokens_f + nn(context, out_full)
    normed_ff, inverse_ff = norm_forward(middle, gain_ff_f)
    pre_act = nn(normed_ff, ff_in_full)
    hidden_f, slope = gelu_both(pre_act)
    hidden = hidden_f.astype(bf16)
    enc_hidden = middle + nn(hidden, ff_out_full)
    memory = enc_hidden.astype(bf16)

    local_pick = starts[:, None] == here + jnp.arange(rows, dtype=jnp.int32)[None, :]
    first = jnp.sum(gather_seq(nn(local_pick.astype(bf16), tokens).astype(bf16)).astype(f32), axis=0)
    self_low, self_inv = norm_forward(first, gain_self_f)
    self_vals = nn(self_low, self_value_full).astype(bf16)
    state_one = first + nn(self_vals, self_out_full)
    cross_low, cross_inv = norm_forward(state_one, gain_cross_f)
    cross_q = nn(cross_low, cross_query_full).astype(bf16)
    head_of = jnp.arange(width, dtype=jnp.int32) // HEAD
    head_rows = -(-HEADS // 8) * 8
    head_mask = (jnp.arange(head_rows, dtype=jnp.int32)[:, None] == head_of[None, :])[None]

    def by_head(values):
        return jnp.where(head_mask, values[:, None, :], 0).reshape(-1, width)

    def from_heads(values):
        return jnp.sum(jnp.where(head_mask, values.reshape(docs, head_rows, width), 0), axis=1)

    probe = nt(by_head(cross_q), cross_key_full).astype(bf16)
    doc_rows = jnp.repeat(jnp.arange(docs, dtype=jnp.int32), head_rows)
    in_doc = doc_rows[:, None] == local_seg[None, :]
    scores = jnp.where(in_doc, nt(probe, memory), NEG)
    top = jnp.max(scores, axis=1, keepdims=True)
    powers = jnp.where(in_doc, jnp.exp(scores - top), 0.0)
    total = jnp.sum(powers, axis=1, keepdims=True)
    mixed = nn(powers.astype(bf16), memory)
    stat_lanes = jnp.where(jnp.arange(128, dtype=jnp.int32)[None, :] == 0, top, total)
    parts = gather_seq(jnp.concatenate([mixed, stat_lanes], axis=1))
    tops = parts[:, :, width : width + 1]
    top_all = jnp.max(tops, axis=0)
    scale = jnp.exp(tops - top_all[None])
    total_all = jnp.sum(scale * parts[:, :, width + 1 : width + 2], axis=0)
    mixed_f = jnp.sum(scale * parts[:, :, :width], axis=0) / total_all
    mixed_all = mixed_f.astype(bf16)
    cross_ctx = from_heads(nn(mixed_all, cross_value_full)).astype(bf16)
    state_two = state_one + nn(cross_ctx, cross_out_full)
    ffn_low, ffn_inv = norm_forward(state_two, gain_dff_f)
    dec_hid_f, dec_slope = gelu_both(nn(ffn_low, dff_in_full))
    dec_hid = dec_hid_f.astype(bf16)

    grad_dec_pre = (dec_slope * nt(dec_cot, dff_out_full)).astype(bf16)
    halves = jnp.sum(gather_seq(jnp.concatenate([nn(dec_hid, dff_out_full), nt(grad_dec_pre, dff_in_full)])), axis=0)
    dec_hidden = state_two + halves[:docs]
    back_values = norm_backward(state_two, ffn_inv, gain_dff_f, halves[docs:])
    grad_two = dec_cot.astype(f32) + back_values
    grad_two_low = grad_two.astype(bf16)
    grad_cross_ctx = nt(grad_two_low, cross_out_full).astype(bf16)
    pull = nt(by_head(grad_cross_ctx), cross_value_full).astype(bf16)
    probs = powers * (jnp.exp(top - top_all) / total_all)
    row_dot = jnp.sum(mixed_f * pull.astype(f32), axis=1, keepdims=True)
    grad_scores = (probs * (nt(pull, memory) - row_dot)).astype(bf16)
    grad_memory = tn(jnp.concatenate([grad_scores, probs.astype(bf16)], axis=0),
                     jnp.concatenate([probe, pull], axis=0))
    grad_mixed = jnp.sum(gather_seq(nn(grad_scores, memory).astype(bf16)).astype(f32), axis=0).astype(bf16)
    grad_cross_q = from_heads(nn(grad_mixed, cross_key_full)).astype(bf16)
    back_values = norm_backward(state_one, cross_inv, gain_cross_f, nt(grad_cross_q, cross_query_full))
    grad_one = grad_two + back_values
    grad_one_low = grad_one.astype(bf16)
    grad_self_vals = nt(grad_one_low, self_out_full).astype(bf16)
    back_values = norm_backward(first, self_inv, gain_self_f, nt(grad_self_vals, self_value_full))
    grad_first = grad_one + back_values

    both = gather_seq(jnp.concatenate([dec_hid, grad_dec_pre])).reshape(seq_count, 2, docs, fsdp, units)
    both = both.transpose(1, 2, 3, 0, 4).reshape(2, docs, fsdp * seq_count * units)
    pack = [self_low, grad_self_vals, self_vals, grad_one_low, cross_low, grad_cross_q, cross_q, grad_cross_ctx,
            cross_ctx, grad_two_low, ffn_low, dec_cot]
    pack += [both[0, :, n * width : (n + 1) * width] for n in range(wide)]
    pack += [both[1, :, n * width : (n + 1) * width] for n in range(wide)]
    tile = 8
    pack = [jnp.pad(rows_of, ((0, tile - docs), (0, 0))) for rows_of in pack] + [grad_mixed, mixed_all]
    pack = jnp.concatenate(pack, axis=0)

    grad_enc = enc_cot.astype(f32) + grad_memory
    grad_enc_low = grad_enc.astype(bf16)
    blocks = tn(hidden, grad_enc_low).astype(bf16).reshape(fsdp, wide, part, width)
    grad_pre = (slope * nt(grad_enc_low, ff_out_full)).astype(bf16)
    back_values = norm_backward(middle, inverse_ff, gain_ff_f, nt(grad_pre, ff_in_full))
    grad_middle = grad_enc + back_values
    grad_middle_low = grad_middle.astype(bf16)
    early = [blocks[:, n] for n in range(wide)] + [tn(context, grad_middle_low).astype(bf16).reshape(fsdp, part, width)]
    across = [tn(normed_ff, grad_pre).astype(bf16).reshape(fsdp, part, wide * width)]
    early, across = scatter_core(early), scatter_core(across)
    grad_context = nt(grad_middle_low, out_full).astype(bf16)
    band, early, across, pack = lax.optimization_barrier((make_band(table, -1), early, across, pack))
    early = scatter_chips(early)
    seq_bits = bits_of("seq")
    grads = None
    pairs = HEADS // 2
    for call, bit in enumerate(seq_bits):
        across_next = halve_seq(across, bit, 2)
        first, count = call * pairs // len(seq_bits), (call + 1) * pairs // len(seq_bits) - call * pairs // len(seq_bits)
        grads = attn_bwd(info, band, query, key, value, grad_context, context, lse, first, count, grads)
        band, across, grads = lax.optimization_barrier((band, across_next, grads))
    grads, early, pack = lax.optimization_barrier((grads, early, pack))
    packs = lax.all_gather(pack, "fsdp", axis=0)
    stack = lambda shard: jnp.concatenate(
        [shard[:, n * width : (n + 1) * width] for n in range(shard.shape[1] // width)], axis=0)
    unstack = lambda rows_of: jnp.concatenate(
        [rows_of[n * part : (n + 1) * part] for n in range(rows_of.shape[0] // part)], axis=1)
    across = scatter_chips(across)
    early = stack(early)
    for bit in seq_bits:
        early = halve_seq(early, bit, 0)
    across, early = whole_seq([across, early], [1, 0], width)
    shard_ff_out = early[: wide * part].astype(f32)
    shard_ff_in = across.astype(f32)
    shard_out = early[wide * part :].astype(f32)
    grad_query, grad_key, grad_value, grad_band, grad_far = grads
    reach = window_blocks(rows)

    def term(step):
        place = step % seq_count * rows
        block = lambda values: values[place : place + rows]
        return nt(block(grad_key), kv_full[:, :width]) + nt(block(grad_value), kv_full[:, width:])

    grad_normed = scatter_window(term, reach) + (term(0) + nt(grad_query, query_full))
    late = [tn(normed, grad_query), tn(normed_all, grad_key), tn(normed_all, grad_value)]
    late = [piece.astype(bf16).reshape(fsdp, part, width) for piece in late]
    grad_table = table_grad(grad_band, grad_far).reshape(fsdp, 1, buckets_part).astype(bf16)
    late += [jnp.pad(grad_table, ((0, 0), (0, part - 1), (0, 128 - buckets_part)))]
    late = scatter_core(late)
    rowset = lambda n: packs[:, n * tile : (n + 1) * tile].reshape(fsdp * tile, width)
    mine = lambda values: lax.dynamic_slice_in_dim(values, own * part, part, 1)
    at = 12
    hid_all = jnp.concatenate([rowset(at + n) for n in range(wide)], axis=1)
    pre_all = jnp.concatenate([rowset(at + wide + n) for n in range(wide)], axis=1)
    part_ff = dff_out.shape[0]
    at = (12 + 2 * wide) * tile
    heads_rows = head_rows * docs
    mixed_g = packs[:, at : at + heads_rows].reshape(fsdp * heads_rows, width)
    mixed_m = packs[:, at + heads_rows : at + 2 * heads_rows].reshape(fsdp * heads_rows, width)
    spread = lambda n: jnp.where(head_mask[None], packs[:, n * tile : n * tile + docs, None], 0).reshape(
        fsdp * heads_rows, width)
    dec_shards = [
        tn(mine(rowset(0)), rowset(1)), tn(mine(rowset(2)), rowset(3)), tn(mine(rowset(4)), rowset(5)),
        tn(mine(mixed_g), spread(6)), tn(mine(mixed_m), spread(7)), tn(mine(rowset(8)), rowset(9)),
        tn(mine(rowset(10)), pre_all),
        tn(lax.dynamic_slice_in_dim(hid_all, own * part_ff, part_ff, 1), rowset(11)),
    ]
    late = scatter_chips(late)
    late, dec_shards = lax.optimization_barrier((late, dec_shards))
    shard_self_value, shard_self_out, shard_cross_query, shard_cross_key = dec_shards[:4]
    shard_cross_value, shard_cross_out, shard_dff_in, shard_dff_out = dec_shards[4:]
    table_rows = jnp.pad(late[:1, 3 * width :], ((0, 31), (0, width - 128)))
    late = sum_seq(jnp.concatenate([stack(late[:, : 3 * width]), table_rows], axis=0), 0).astype(f32)
    shard_query, shard_key, shard_value = (late[n * part : (n + 1) * part] for n in range(3))
    shard_table = late[3 * part, :buckets_part]
    back_values = norm_backward(tokens_f, inverse_attn, gain_attn_f, grad_normed)
    first_back = lax.dot_general(local_pick.astype(f32), grad_first, (((0,), (0,)), ((), ())),
                                 precision=lax.Precision.HIGHEST, preferred_element_type=f32)
    tokens_grad = grad_middle + back_values + first_back

    def gain_grad(gain_vec, *pairs_of):
        return sum(jnp.sum(grad * weight.astype(f32), axis=1) for grad, weight in pairs_of) / gain_vec.astype(f32)

    grad_gain_attn = gain_grad(gain_attn, (shard_query, query_weight), (shard_key, key_weight), (shard_value, value_weight))
    grad_gain_ff = gain_grad(gain_ff, (shard_ff_in, ff_in))
    grad_gain_self = gain_grad(gain_self, (shard_self_value, self_value))
    grad_gain_cross = gain_grad(gain_cross, (shard_cross_query, cross_query))
    grad_gain_dff = gain_grad(gain_dff, (shard_dff_in, dff_in))
    return (
        enc_hidden, dec_hidden, tokens_grad, grad_gain_attn, shard_query, shard_key, shard_value, shard_out,
        shard_table, grad_gain_ff, shard_ff_in, shard_ff_out, grad_gain_self, shard_self_value, shard_self_out,
        grad_gain_cross, shard_cross_query, shard_cross_key, shard_cross_value, shard_cross_out, grad_gain_dff,
        shard_dff_in, shard_dff_out,
    )


def solution(mesh):
    tok, wide, one = P(("fsdp", "seq"), None), P("fsdp", None), P("fsdp")
    return jax.shard_map(
        body,
        mesh=mesh,
        in_specs=(tok, wide, one, wide, wide, wide, wide, one, one, wide, wide, one, wide, wide, one, wide, wide, wide,
                  wide, one, wide, wide, tok, wide),
        out_specs=(tok, wide, tok, one, wide, wide, wide, wide, one, one, wide, wide, one, wide, wide, one, wide, wide,
                   wide, wide, one, wide, wide),
        check_vma=False,
    )
```

profile of v0, /device:TPU:0, one launch (start us, length us, event | category | flops | bytes accessed | tf_op | source)
XLA Modules:
  0.0 530.5 jit_solution(10973578472345139903)
XLA Ops:
  12.2 5.6 %collective-permute-start = (bf16[512,768]{1,0:T(8,128)(2,1)}, bf16[512,768]{1,0:T(8,128)(2,1)S(1)}, u32[]{:S(2)}, u32[]{:S(2)}) collective-permute-start(bf16[512,768]{1,0:T(8,128)(2,1)} %param.28), channel_id=1, source_target_pairs={{0,1},{1,2},{2,3},{4,5},{5,6},{6,7},{8,9},{9,10},{10,11},{12,13},{... | collective-permute-start | bytes 2359304 | tf_op jit(solution)/shard_map/ppermute | solution.py:246
  17.8 15.8 %collective-permute-done.1 = bf16[512,768]{1,0:T(8,128)(2,1)S(1)} collective-permute-done((bf16[512,768]{1,0:T(8,128)(2,1)}, bf16[512,768]{1,0:T(8,128)(2,1)S(1)}, u32[]{:S(2)}, u32[]{:S(2)}) %collective-permute-start.1) | collective-permute-done | bytes 786464 | tf_op jit(solution)/shard_map/ppermute | solution.py:246
  48.1 2.8 collective-permute-start.5
  66.4 5.4 %collective-permute-start.3 = (bf16[512,768]{1,0:T(8,128)(2,1)S(1)}, bf16[512,768]{1,0:T(8,128)(2,1)}, u32[]{:S(2)}, u32[]{:S(2)}) collective-permute-start(bf16[512,768]{1,0:T(8,128)(2,1)S(1)} %collective-permute-done), channel_id=1, source_target_pairs={{0,1},{1,2},{2,3},{4,5},{5,6},{6,7},{8,9},{9,10},{10,11},{12,13},{... | collective-permute-start | bytes 2359304 | tf_op jit(solution)/shard_map/ppermute | solution.py:246
  78.4 6.1 %collective-permute-done.2 = bf16[512,768]{1,0:T(8,128)(2,1)} collective-permute-done((bf16[512,768]{1,0:T(8,128)(2,1)S(1)}, bf16[512,768]{1,0:T(8,128)(2,1)}, u32[]{:S(2)}, u32[]{:S(2)}) %collective-permute-start.2) | collective-permute-done | bytes 786464 | tf_op jit(solution)/shard_map/ppermute | solution.py:246
  92.1 6.8 %fusion.2 = bf16[2048,768]{1,0:T(8,128)(2,1)S(1)} fusion(f32[768]{0:T(1024)S(1)} %get-tuple-element.163, f32[2048]{0:T(1024)S(1)} %add_rsqrt_fusion, bf16[512,768]{1,0:T(8,128)(2,1)S(1)} %collective-permute-done, bf16[512,768]{1,0:T(8,128)(2,1)S(1)} %add.653, bf16[512,768]{1,0:T(8,128)(2,1)S(1)} %collective-permute-done.1, bf16[512,768]{1,0:T(8,128)(2,1)S(1)} %copy-done.12), kind=kLoop, calls=%fused_computation.6 | loop fusion | flops 17301504 | bytes 6302720 | tf_op jit(solution)/shard_map/convert_element_type | solution.py:378
  100.6 2.8 convolution_convert_fusion.2.v_ref.refs_4_
  103.4 2.8 convolution_convert_fusion.3.k_ref.refs_3_
  106.2 25.9 %shard_map.407 = (bf16[512,768]{1,0:T(8,128)(2,1)S(1)}, f32[512,768]{1,0:T(8,128)S(1)}) custom-call(s32[3]{0:T(128)S(1)} %add_add_fusion.info.refs_0_, f32[6,2,512]{2,1,0:T(2,128)S(1)} %copy.71.band_ref, bf16[512,768]{1,0:T(8,128)(2,1)S(1)} %convolution_convert_fusion.9.q_ref.refs_2_, bf16[2048,768]{1,0:T(8,128)(2,1)S(1)} %convolution_convert_fusion.3.k_ref.refs_3_, ...), custom_call_target="tpu_custom_call" | custom-call | flops 4026531840 | bytes 9437184 | tf_op jit(solution)/shard_map/pallas_call | solution.py:110
  138.7 2.5 multiply_reduce_fusion.1
  145.4 7.2 %fusion.13 = f32[512,3072]{1,0:T(8,128)} fusion(bf16[768,6912]{1,0:T(8,128)(2,1)} %all-gather.9.cloned.1.call-done, f32[512,768]{1,0:T(8,128)S(1)} %get-tuple-element.300, f32[768]{0:T(1024)S(1)} %get-tuple-element.162, f32[512]{0:T(512)S(1)} %get-tuple-element.286), kind=kOutput, calls=%fused_computation.23 | convolution fusion | flops 2417098752 | bytes 12588032 | tf_op jit(solution)/shard_map/dot_general | solution.py:27
  152.6 3.1 all-gather.11.cloned.1.call-done
  155.7 9.5 %fusion.197 = (bf16[512,768]{1,0:T(8,128)(2,1)S(1)}, f32[512,768]{1,0:T(8,128)}) fusion(f32[512,768]{1,0:T(8,128)} %copy-done.26, bf16[3072,768]{1,0:T(8,128)(2,1)} %all-gather.11.cloned.1.call-done, f32[512,3072]{1,0:T(8,128)} %fusion.13), kind=kOutput, calls=%fused_computation.493 | convolution fusion | flops 2430861312 | bytes 14942208 | tf_op jit(solution)/shard_map/dot_general | solution.py:27
  167.0 5.5 %collective-permute-start.8 = (f32[48,896]{1,0:T(8,128)S(1)}, f32[48,896]{1,0:T(8,128)S(1)}, u32[]{:S(2)}, u32[]{:S(2)}) collective-permute-start(f32[48,896]{1,0:T(8,128)S(1)} %get-tuple-element.261), channel_id=1, source_target_pairs={{0,2},{1,3},{2,0},{3,1},{4,6},{5,7},{6,4},{7,5},{8,10},{9,11},{10,... | collective-permute-start | bytes 516104 | tf_op jit(solution)/shard_map/ppermute | solution.py:321
  175.3 8.0 %collective-permute-done.8 = f32[48,896]{1,0:T(8,128)S(1)} collective-permute-done((f32[48,896]{1,0:T(8,128)S(1)}, f32[48,896]{1,0:T(8,128)S(1)}, u32[]{:S(2)}, u32[]{:S(2)}) %collective-permute-start.8) | collective-permute-done | bytes 172064 | tf_op jit(solution)/shard_map/ppermute | solution.py:321
  184.0 13.0 %all-gather.13.cloned.1.call-done = bf16[768,3072]{1,0:T(8,128)(2,1)} async-done(((bf16[96,3072]{1,0:T(8,128)(2,1)}), bf16[768,3072]{1,0:T(8,128)(2,1)}) %all-gather.13.cloned.1.call-update) | async-done | bytes 4718608 | tf_op jit(solution)/shard_map/all_gather | solution.py:409
  205.2 2.5 collective-permute-start.19
  211.4 2.9 collective-permute-start.10
  216.1 4.0 collective-permute-done.12
  225.6 3.4 collective-permute-start.15
  230.6 6.2 %convolution_convert_fusion.1 = bf16[3072,768]{1,0:T(8,128)(2,1)S(1)} fusion(f32[512,768]{1,0:T(8,128)S(1)} %convert_add_fusion.2, f32[512,3072]{1,0:T(8,128)} %fusion.13), kind=kOutput, calls=%fused_computation.18 | convolution fusion | flops 2432827392 | bytes 12582912 | tf_op jit(solution)/shard_map/dot_general | solution.py:25
  237.2 9.0 %fusion.9 = bf16[512,3072]{1,0:T(8,128)(2,1)S(1)} fusion(f32[512,3072]{1,0:T(8,128)} %fusion.13, bf16[3072,768]{1,0:T(8,128)(2,1)} %all-gather.11.cloned.1.call-done, f32[512,768]{1,0:T(8,128)S(1)} %convert_add_fusion.2), kind=kOutput, calls=%fused_computation.13 | convolution fusion | flops 2446196736 | bytes 15728640 | tf_op jit(solution)/shard_map/dot_general | solution.py:23
  246.2 3.1 convolution_convert_fusion
  249.4 2.7 multiply_reduce_fusion
  264.5 3.4 fusion.10
  268.0 2.6 add_convert_fusion
  275.1 21.2 %shard_map.408 = (bf16[512,768]{1,0:T(8,128)(2,1)S(1)}, bf16[2048,768]{1,0:T(8,128)(2,1)S(1)}, bf16[2048,768]{1,0:T(8,128)(2,1)S(1)}, f32[6,2,512]{2,1,0:T(2,128)S(1)}, f32[6,2,256]{2,1,0:T(2,128)S(1)}) custom-call(s32[3]{0:T(128)S(1)} %add_add_fusion.info.refs_0_, f32[6,2,512]{2,1,0:T(2,128)S(1)} %copy.93.band_ref, ...), custom_call_target="tpu_custom_call" | custom-call | flops 20132659200 | bytes 8650752 | tf_op jit(solution)/shard_map/pallas_call | solution.py:209
  296.3 10.1 %collective-permute-done.25 = bf16[1,96,3840]{2,1,0:T(8,128)(2,1)S(1)} collective-permute-done((bf16[1,96,3840]{2,1,0:T(8,128)(2,1)S(1)}, bf16[1,96,3840]{2,1,0:T(8,128)(2,1)S(1)}, u32[]{:S(2)}, u32[]{:S(2)}) %collective-permute-start.25) | collective-permute-done | bytes 737312 | tf_op jit(solution)/shard_map/ppermute | solution.py:241
  311.4 21.2 %shard_map.409 = (bf16[512,768]{1,0:T(8,128)(2,1)S(1)}, bf16[2048,768]{1,0:T(8,128)(2,1)S(1)}, bf16[2048,768]{1,0:T(8,128)(2,1)S(1)}, f32[6,2,512]{2,1,0:T(2,128)S(1)}, f32[6,2,256]{2,1,0:T(2,128)S(1)}) custom-call(s32[3]{0:T(128)S(1)} %add_add_fusion.info.refs_0_, ...), custom_call_target="tpu_custom_call", output_to_operand_aliasing={{0}: (8, {}), {1}: (9, {}), {2}: (10, {}), {3}: (11, {}), {... | custom-call | flops 20132659200 | bytes 8650752 | tf_op jit(solution)/shard_map/pallas_call | solution.py:209
  332.6 3.3 collective-permute-done.22
  336.2 2.7 convolution_convert_fusion.5
  338.9 3.7 convolution_convert_fusion.4
  346.5 5.4 %collective-permute-start.26 = (bf16[512,768]{1,0:T(8,128)(2,1)}, bf16[512,768]{1,0:T(8,128)(2,1)}, u32[]{:S(2)}, u32[]{:S(2)}) collective-permute-start(bf16[512,768]{1,0:T(8,128)(2,1)} %add_convert_fusion.5), channel_id=1, source_target_pairs={{0,1},{1,2},{2,3},{4,5},{5,6},{6,7},{8,9},{9,10},{10,11},{12,13},{... | collective-permute-start | bytes 2359304 | tf_op jit(solution)/shard_map/ppermute | solution.py:246
  354.3 13.9 %collective-permute-start.38 = (bf16[1,96,768]{2,1,0:T(8,128)(2,1)S(1)}, bf16[1,96,768]{2,1,0:T(8,128)(2,1)S(1)}, u32[]{:S(2)}, u32[]{:S(2)}) collective-permute-start(bf16[1,96,768]{2,1,0:T(8,128)(2,1)S(1)} %get-tuple-element.244), channel_id=1, source_target_pairs={{0,8},{4,12},{8,0},{12,4},{16,24},{20,28},{24,16},{28,20},{1,9},{5... | collective-permute-start | bytes 442376 | tf_op jit(solution)/shard_map/ppermute | solution.py:241
  377.6 4.7 collective-permute-start.39
  384.2 3.7 collective-permute-done.39
  388.0 6.5 %collective-permute-done.42 = bf16[120,768]{1,0:T(8,128)(2,1)S(1)} collective-permute-done((bf16[120,768]{1,0:T(8,128)(2,1)S(1)}, bf16[120,768]{1,0:T(8,128)(2,1)S(1)}, u32[]{:S(2)}, u32[]{:S(2)}) %collective-permute-start.42) | collective-permute-done | bytes 184352 | tf_op jit(solution)/shard_map/ppermute | solution.py:241
  396.4 15.7 %collective-permute-done.43 = bf16[216,768]{1,0:T(8,128)(2,1)S(1)} collective-permute-done((bf16[216,768]{1,0:T(8,128)(2,1)S(1)}, bf16[216,768]{1,0:T(8,128)(2,1)S(1)}, u32[]{:S(2)}, u32[]{:S(2)}) %collective-permute-start.43) | collective-permute-done | bytes 331808 | tf_op jit(solution)/shard_map/ppermute | solution.py:241
  417.5 5.0 collective-permute-start.27
  422.6 7.5 %collective-permute-done.44 = bf16[432,768]{1,0:T(8,128)(2,1)S(1)} collective-permute-done((bf16[432,768]{1,0:T(8,128)(2,1)S(1)}, bf16[432,768]{1,0:T(8,128)(2,1)S(1)}, u32[]{:S(2)}, u32[]{:S(2)}) %collective-permute-start.44) | collective-permute-done | bytes 663584 | tf_op jit(solution)/shard_map/ppermute | solution.py:241
  434.0 11.8 %collective-permute-done.29 = bf16[512,768]{1,0:T(8,128)(2,1)S(1)} collective-permute-done((bf16[512,768]{1,0:T(8,128)(2,1)S(1)}, bf16[512,768]{1,0:T(8,128)(2,1)S(1)}, u32[]{:S(2)}, u32[]{:S(2)}) %collective-permute-start.29) | collective-permute-done | bytes 786464 | tf_op jit(solution)/shard_map/ppermute | solution.py:246
  447.7 7.2 %collective-permute-start.31 = (bf16[1,96,2432]{2,1,0:T(8,128)(2,1)S(1)}, bf16[1,96,2432]{2,1,0:T(8,128)(2,1)S(1)}, u32[]{:S(2)}, u32[]{:S(2)}) collective-permute-start(bf16[1,96,2432]{2,1,0:T(8,128)(2,1)S(1)} %get-tuple-element.206), channel_id=1, source_target_pairs={{0,8},{4,12},{8,0},{12,4},{16,24},{20,28},{24,16},{28,20},{1,9},{5... | collective-permute-start | bytes 1400840 | tf_op jit(solution)/shard_map/ppermute | solution.py:241
  459.0 7.6 %collective-permute-done.31 = bf16[1,96,2432]{2,1,0:T(8,128)(2,1)S(1)} collective-permute-done((bf16[1,96,2432]{2,1,0:T(8,128)(2,1)S(1)}, bf16[1,96,2432]{2,1,0:T(8,128)(2,1)S(1)}, u32[]{:S(2)}, u32[]{:S(2)}) %collective-permute-start.31) | collective-permute-done | bytes 466976 | tf_op jit(solution)/shard_map/ppermute | solution.py:241
  466.5 7.8 %collective-permute-done.33 = bf16[1,96,2432]{2,1,0:T(8,128)(2,1)S(1)} collective-permute-done((bf16[1,96,2432]{2,1,0:T(8,128)(2,1)S(1)}, bf16[1,96,2432]{2,1,0:T(8,128)(2,1)S(1)}, u32[]{:S(2)}, u32[]{:S(2)}) %collective-permute-start.33) | collective-permute-done | bytes 466976 | tf_op jit(solution)/shard_map/ppermute | solution.py:241
  493.1 6.2 %collective-permute-done.34 = bf16[160,768]{1,0:T(8,128)(2,1)S(1)} collective-permute-done((bf16[160,768]{1,0:T(8,128)(2,1)S(1)}, bf16[160,768]{1,0:T(8,128)(2,1)S(1)}, u32[]{:S(2)}, u32[]{:S(2)}) %collective-permute-start.34) | collective-permute-done | bytes 245792 | tf_op jit(solution)/shard_map/ppermute | solution.py:241
  499.8 8.5 %collective-permute-done.35 = bf16[80,768]{1,0:T(8,128)(2,1)S(1)} collective-permute-done((bf16[80,768]{1,0:T(8,128)(2,1)S(1)}, bf16[80,768]{1,0:T(8,128)(2,1)S(1)}, u32[]{:S(2)}, u32[]{:S(2)}) %collective-permute-start.35) | collective-permute-done | bytes 122912 | tf_op jit(solution)/shard_map/ppermute | solution.py:241
  509.0 6.1 %collective-permute-done.36 = bf16[80,768]{1,0:T(8,128)(2,1)S(1)} collective-permute-done((bf16[80,768]{1,0:T(8,128)(2,1)S(1)}, bf16[80,768]{1,0:T(8,128)(2,1)S(1)}, u32[]{:S(2)}, u32[]{:S(2)}) %collective-permute-start.36) | collective-permute-done | bytes 122912 | tf_op jit(solution)/shard_map/ppermute | solution.py:241
  516.0 5.3 %collective-permute-done.37 = bf16[160,768]{1,0:T(8,128)(2,1)S(1)} collective-permute-done((bf16[160,768]{1,0:T(8,128)(2,1)S(1)}, bf16[160,768]{1,0:T(8,128)(2,1)S(1)}, u32[]{:S(2)}, u32[]{:S(2)}) %collective-permute-start.37) | collective-permute-done | bytes 245792 | tf_op jit(solution)/shard_map/ppermute | solution.py:241
  (522 shorter events, 156.7 us)
Async XLA Ops:
  7.2 81.3 %all-gather.7.cloned.1.call-start = ((), (), s32[]{:S(2)}) async-start(), calls=%async_computation | async-start | bytes 4202496 | tf_op jit(solution)/shard_map/all_gather | solution.py:409
  10.9 124.1 %all-gather.9.cloned.1.call-start = ((), (), s32[]{:S(2)}) async-start(), calls=%async_computation.1 | async-start | bytes 11943936 | tf_op jit(solution)/shard_map/all_gather | solution.py:409
  10.9 22.7 %collective-permute-start.1 = (bf16[512,768]{1,0:T(8,128)(2,1)}, bf16[512,768]{1,0:T(8,128)(2,1)S(1)}, u32[]{:S(2)}, u32[]{:S(2)}) collective-permute-start(bf16[512,768]{1,0:T(8,128)(2,1)} %param.28), channel_id=1, source_target_pairs={{1,0},{2,1},{3,2},{5,4},{6,5},{7,6},{9,8},{10,9},{11,10},{13,12},{... | collective-permute-start | bytes 2359304 | tf_op jit(solution)/shard_map/ppermute | solution.py:246
  12.2 22.7 %collective-permute-start = (bf16[512,768]{1,0:T(8,128)(2,1)}, bf16[512,768]{1,0:T(8,128)(2,1)S(1)}, u32[]{:S(2)}, u32[]{:S(2)}) collective-permute-start(bf16[512,768]{1,0:T(8,128)(2,1)} %param.28), channel_id=1, source_target_pairs={{0,1},{1,2},{2,3},{4,5},{5,6},{6,7},{8,9},{9,10},{10,11},{12,13},{... | collective-permute-start | bytes 2359304 | tf_op jit(solution)/shard_map/ppermute | solution.py:246
  42.0 113.7 %all-gather.11.cloned.1.call-start = ((), (), s32[]{:S(2)}) async-start(), calls=%async_computation.2 | async-start | bytes 5308416 | tf_op jit(solution)/shard_map/all_gather | solution.py:409
  42.8 154.2 %all-gather.13.cloned.1.call-start = ((), (), s32[]{:S(2)}) async-start(), calls=%async_computation.3 | async-start | bytes 5308416 | tf_op jit(solution)/shard_map/all_gather | solution.py:409
  45.7 19.4 %collective-permute-start.6 = (bf16[3,768]{1,0:T(4,128)(2,1)S(1)}, bf16[3,768]{1,0:T(4,128)(2,1)S(1)}, u32[]{:S(2)}, u32[]{:S(2)}) collective-permute-start(bf16[3,768]{1,0:T(4,128)(2,1)S(1)} %convolution_convert_fusion.17), channel_id=1, source_target_pairs={{0,1},{1,2},{2,3},{3,0},{4,5},{5,6},{6,7},{7,4},{8,9},{9,10},{10,1... | collective-permute-start | bytes 13832 | tf_op jit(solution)/shard_map/ppermute | solution.py:321
  48.1 17.0 %collective-permute-start.5 = (bf16[3,768]{1,0:T(4,128)(2,1)S(1)}, bf16[3,768]{1,0:T(4,128)(2,1)S(1)}, u32[]{:S(2)}, u32[]{:S(2)}) collective-permute-start(bf16[3,768]{1,0:T(4,128)(2,1)S(1)} %convolution_convert_fusion.17), channel_id=1, source_target_pairs={{0,2},{1,3},{2,0},{3,1},{4,6},{5,7},{6,4},{7,5},{8,10},{9,11},{10,... | collective-permute-start | bytes 13832 | tf_op jit(solution)/shard_map/ppermute | solution.py:321
  50.9 14.3 %collective-permute-start.4 = (bf16[3,768]{1,0:T(4,128)(2,1)S(1)}, bf16[3,768]{1,0:T(4,128)(2,1)S(1)}, u32[]{:S(2)}, u32[]{:S(2)}) collective-permute-start(bf16[3,768]{1,0:T(4,128)(2,1)S(1)} %convolution_convert_fusion.17), channel_id=1, source_target_pairs={{0,3},{1,0},{2,1},{3,2},{4,7},{5,4},{6,5},{7,6},{8,11},{9,8},{10,9... | collective-permute-start | bytes 13832 | tf_op jit(solution)/shard_map/ppermute | solution.py:321
  65.1 19.3 %collective-permute-start.2 = (bf16[512,768]{1,0:T(8,128)(2,1)S(1)}, bf16[512,768]{1,0:T(8,128)(2,1)}, u32[]{:S(2)}, u32[]{:S(2)}) collective-permute-start(bf16[512,768]{1,0:T(8,128)(2,1)S(1)} %collective-permute-done.1), channel_id=1, source_target_pairs={{1,0},{2,1},{3,2},{5,4},{6,5},{7,6},{9,8},{10,9},{11,10},{13,12},{... | collective-permute-start | bytes 2359304 | tf_op jit(solution)/shard_map/ppermute | solution.py:246
  66.4 19.1 %collective-permute-start.3 = (bf16[512,768]{1,0:T(8,128)(2,1)S(1)}, bf16[512,768]{1,0:T(8,128)(2,1)}, u32[]{:S(2)}, u32[]{:S(2)}) collective-permute-start(bf16[512,768]{1,0:T(8,128)(2,1)S(1)} %collective-permute-done), channel_id=1, source_target_pairs={{0,1},{1,2},{2,3},{4,5},{5,6},{6,7},{8,9},{9,10},{10,11},{12,13},{... | collective-permute-start | bytes 2359304 | tf_op jit(solution)/shard_map/ppermute | solution.py:246
  78.2 398.4 %all-gather.15.cloned.1.call-start = ((), (), s32[]{:S(2)}) async-start(), calls=%async_computation.4 | async-start | bytes 3538944 | tf_op jit(solution)/shard_map/all_gather | solution.py:549
  167.0 16.3 %collective-permute-start.8 = (f32[48,896]{1,0:T(8,128)S(1)}, f32[48,896]{1,0:T(8,128)S(1)}, u32[]{:S(2)}, u32[]{:S(2)}) collective-permute-start(f32[48,896]{1,0:T(8,128)S(1)} %get-tuple-element.261), channel_id=1, source_target_pairs={{0,2},{1,3},{2,0},{3,1},{4,6},{5,7},{6,4},{7,5},{8,10},{9,11},{10,... | collective-permute-start | bytes 516104 | tf_op jit(solution)/shard_map/ppermute | solution.py:321
  172.5 10.8 %collective-permute-start.7 = (f32[48,896]{1,0:T(8,128)S(1)}, f32[48,896]{1,0:T(8,128)S(1)}, u32[]{:S(2)}, u32[]{:S(2)}) collective-permute-start(f32[48,896]{1,0:T(8,128)S(1)} %get-tuple-element.261), channel_id=1, source_target_pairs={{0,3},{1,0},{2,1},{3,2},{4,7},{5,4},{6,5},{7,6},{8,11},{9,8},{10,9... | collective-permute-start | bytes 516104 | tf_op jit(solution)/shard_map/ppermute | solution.py:321
  173.0 10.3 %collective-permute-start.9 = (f32[48,896]{1,0:T(8,128)S(1)}, f32[48,896]{1,0:T(8,128)S(1)}, u32[]{:S(2)}, u32[]{:S(2)}) collective-permute-start(f32[48,896]{1,0:T(8,128)S(1)} %get-tuple-element.261), channel_id=1, source_target_pairs={{0,1},{1,2},{2,3},{3,0},{4,5},{5,6},{6,7},{7,4},{8,9},{9,10},{10,1... | collective-permute-start | bytes 516104 | tf_op jit(solution)/shard_map/ppermute | solution.py:321
  205.2 9.3 %collective-permute-start.19 = (bf16[6,768]{1,0:T(8,128)(2,1)S(1)}, bf16[6,768]{1,0:T(8,128)(2,1)S(1)}, u32[]{:S(2)}, u32[]{:S(2)}) collective-permute-start(bf16[6,768]{1,0:T(8,128)(2,1)S(1)} %get-tuple-element.284), channel_id=1, source_target_pairs={{0,2},{1,3},{2,0},{3,1},{4,6},{5,7},{6,4},{7,5},{8,10},{9,11},{10,... | collective-permute-start | bytes 27656 | tf_op jit(solution)/shard_map/ppermute | solution.py:321
  207.6 6.9 %collective-permute-start.18 = (bf16[6,768]{1,0:T(8,128)(2,1)S(1)}, bf16[6,768]{1,0:T(8,128)(2,1)S(1)}, u32[]{:S(2)}, u32[]{:S(2)}) collective-permute-start(bf16[6,768]{1,0:T(8,128)(2,1)S(1)} %get-tuple-element.284), channel_id=1, source_target_pairs={{0,3},{1,0},{2,1},{3,2},{4,7},{5,4},{6,5},{7,6},{8,11},{9,8},{10,9... | collective-permute-start | bytes 27656 | tf_op jit(solution)/shard_map/ppermute | solution.py:321
  209.1 5.6 %collective-permute-start.20 = (bf16[6,768]{1,0:T(8,128)(2,1)S(1)}, bf16[6,768]{1,0:T(8,128)(2,1)S(1)}, u32[]{:S(2)}, u32[]{:S(2)}) collective-permute-start(bf16[6,768]{1,0:T(8,128)(2,1)S(1)} %get-tuple-element.284), channel_id=1, source_target_pairs={{0,1},{1,2},{2,3},{3,0},{4,5},{5,6},{6,7},{7,4},{8,9},{9,10},{10,1... | collective-permute-start | bytes 27656 | tf_op jit(solution)/shard_map/ppermute | solution.py:321
  214.5 5.7 %collective-permute-start.12 = (f32[6,768]{1,0:T(8,128)S(1)}, f32[6,768]{1,0:T(8,128)S(1)}, u32[]{:S(2)}, u32[]{:S(2)}) collective-permute-start(f32[6,768]{1,0:T(8,128)S(1)} %get-tuple-element.276), channel_id=1, source_target_pairs={{0,1},{1,2},{2,3},{3,0},{4,5},{5,6},{6,7},{7,4},{8,9},{9,10},{10,1... | collective-permute-start | bytes 55304 | tf_op jit(solution)/shard_map/ppermute | solution.py:321
  225.2 36.1 %collective-permute-start.17 = (bf16[48,768]{1,0:T(8,128)(2,1)S(1)}, bf16[48,768]{1,0:T(8,128)(2,1)S(1)}, u32[]{:S(2)}, u32[]{:S(2)}) collective-permute-start(bf16[48,768]{1,0:T(8,128)(2,1)S(1)} %convolution_convert_fusion.12), channel_id=1, source_target_pairs={{0,1},{1,2},{2,3},{3,0},{4,5},{5,6},{6,7},{7,4},{8,9},{9,10},{10,1... | collective-permute-start | bytes 221192 | tf_op jit(solution)/shard_map/ppermute | solution.py:321
  225.3 36.0 %collective-permute-start.16 = (bf16[48,768]{1,0:T(8,128)(2,1)S(1)}, bf16[48,768]{1,0:T(8,128)(2,1)S(1)}, u32[]{:S(2)}, u32[]{:S(2)}) collective-permute-start(bf16[48,768]{1,0:T(8,128)(2,1)S(1)} %convolution_convert_fusion.12), channel_id=1, source_target_pairs={{0,2},{1,3},{2,0},{3,1},{4,6},{5,7},{6,4},{7,5},{8,10},{9,11},{10,... | collective-permute-start | bytes 221192 | tf_op jit(solution)/shard_map/ppermute | solution.py:321
  225.6 35.7 %collective-permute-start.15 = (bf16[48,768]{1,0:T(8,128)(2,1)S(1)}, bf16[48,768]{1,0:T(8,128)(2,1)S(1)}, u32[]{:S(2)}, u32[]{:S(2)}) collective-permute-start(bf16[48,768]{1,0:T(8,128)(2,1)S(1)} %convolution_convert_fusion.12), channel_id=1, source_target_pairs={{0,3},{1,0},{2,1},{3,2},{4,7},{5,4},{6,5},{7,6},{8,11},{9,8},{10,9... | collective-permute-start | bytes 221192 | tf_op jit(solution)/shard_map/ppermute | solution.py:321
  255.0 9.5 %collective-permute-start.14 = (bf16[4,96,3072]{2,1,0:T(8,128)(2,1)}, bf16[4,96,3072]{2,1,0:T(8,128)(2,1)}, u32[]{:S(2)}, u32[]{:S(2)}) collective-permute-start(bf16[4,96,3072]{2,1,0:T(8,128)(2,1)} %dynamic-slice_bitcast_fusion), channel_id=1, source_target_pairs={{0,4},{4,0},{8,12},{12,8},{16,20},{20,16},{24,28},{28,24},{1,5},{5... | collective-permute-start | bytes 7077896 | tf_op jit(solution)/shard_map/ppermute | solution.py:241
  259.8 8.2 %collective-permute-start.13 = (bf16[4,96,3840]{2,1,0:T(8,128)(2,1)}, bf16[4,96,3840]{2,1,0:T(8,128)(2,1)}, u32[]{:S(2)}, u32[]{:S(2)}) collective-permute-start(bf16[4,96,3840]{2,1,0:T(8,128)(2,1)} %get-tuple-element.216), channel_id=1, source_target_pairs={{0,4},{4,0},{8,12},{12,8},{16,20},{20,16},{24,28},{28,24},{1,5},{5... | collective-permute-start | bytes 8847368 | tf_op jit(solution)/shard_map/ppermute | solution.py:241
  270.8 38.3 %collective-permute-start.21 = (bf16[4,96,1536]{2,1,0:T(8,128)(2,1)S(1)}, bf16[4,96,1536]{2,1,0:T(8,128)(2,1)S(1)}, u32[]{:S(2)}, u32[]{:S(2)}) collective-permute-start(bf16[4,96,1536]{2,1,0:T(8,128)(2,1)S(1)} %broadcast_select_fusion), channel_id=1, source_target_pairs={{0,1},{1,0},{2,3},{3,2},{4,5},{5,4},{6,7},{7,6},{8,9},{9,8},{10,11... | collective-permute-start | bytes 3538952 | tf_op jit(solution)/shard_map/ppermute | solution.py:241
  271.6 24.8 %collective-permute-start.23 = (bf16[1,96,3840]{2,1,0:T(8,128)(2,1)S(1)}, bf16[1,96,3840]{2,1,0:T(8,128)(2,1)S(1)}, u32[]{:S(2)}, u32[]{:S(2)}) collective-permute-start(bf16[1,96,3840]{2,1,0:T(8,128)(2,1)S(1)} %get-tuple-element.203), channel_id=1, source_target_pairs={{0,8},{4,12},{8,0},{12,4},{16,24},{20,28},{24,16},{28,20},{1,9},{5... | collective-permute-start | bytes 2211848 | tf_op jit(solution)/shard_map/ppermute | solution.py:241
  273.1 33.4 %collective-permute-start.25 = (bf16[1,96,3840]{2,1,0:T(8,128)(2,1)S(1)}, bf16[1,96,3840]{2,1,0:T(8,128)(2,1)S(1)}, u32[]{:S(2)}, u32[]{:S(2)}) collective-permute-start(bf16[1,96,3840]{2,1,0:T(8,128)(2,1)S(1)} %get-tuple-element.204), channel_id=1, source_target_pairs={{0,24},{4,28},{8,16},{12,20},{16,8},{20,12},{24,0},{28,4},{1,25},{... | collective-permute-start | bytes 2211848 | tf_op jit(solution)/shard_map/ppermute | solution.py:241
  274.4 33.4 %collective-permute-start.24 = (bf16[1,96,3840]{2,1,0:T(8,128)(2,1)S(1)}, bf16[1,96,3840]{2,1,0:T(8,128)(2,1)S(1)}, u32[]{:S(2)}, u32[]{:S(2)}) collective-permute-start(bf16[1,96,3840]{2,1,0:T(8,128)(2,1)S(1)} %get-tuple-element.205), channel_id=1, source_target_pairs={{0,16},{4,20},{8,24},{12,28},{16,0},{20,4},{24,8},{28,12},{1,17},{... | collective-permute-start | bytes 2211848 | tf_op jit(solution)/shard_map/ppermute | solution.py:241
  309.6 26.3 %collective-permute-start.22 = (bf16[4,96,768]{2,1,0:T(8,128)(2,1)S(1)}, bf16[4,96,768]{2,1,0:T(8,128)(2,1)S(1)}, u32[]{:S(2)}, u32[]{:S(2)}) collective-permute-start(bf16[4,96,768]{2,1,0:T(8,128)(2,1)S(1)} %broadcast_select_fusion.3), channel_id=1, source_target_pairs={{0,2},{1,3},{2,0},{3,1},{4,6},{5,7},{6,4},{7,5},{8,10},{9,11},{10,... | collective-permute-start | bytes 1769480 | tf_op jit(solution)/shard_map/ppermute | solution.py:241
  345.2 67.0 %collective-permute-start.28 = (bf16[512,768]{1,0:T(8,128)(2,1)}, bf16[512,768]{1,0:T(8,128)(2,1)}, u32[]{:S(2)}, u32[]{:S(2)}) collective-permute-start(bf16[512,768]{1,0:T(8,128)(2,1)} %add_convert_fusion.5), channel_id=1, source_target_pairs={{1,0},{2,1},{3,2},{5,4},{6,5},{7,6},{9,8},{10,9},{11,10},{13,12},{... | collective-permute-start | bytes 2359304 | tf_op jit(solution)/shard_map/ppermute | solution.py:246
  346.5 69.0 %collective-permute-start.26 = (bf16[512,768]{1,0:T(8,128)(2,1)}, bf16[512,768]{1,0:T(8,128)(2,1)}, u32[]{:S(2)}, u32[]{:S(2)}) collective-permute-start(bf16[512,768]{1,0:T(8,128)(2,1)} %add_convert_fusion.5), channel_id=1, source_target_pairs={{0,1},{1,2},{2,3},{4,5},{5,6},{6,7},{8,9},{9,10},{10,11},{12,13},{... | collective-permute-start | bytes 2359304 | tf_op jit(solution)/shard_map/ppermute | solution.py:246
  354.3 28.2 %collective-permute-start.38 = (bf16[1,96,768]{2,1,0:T(8,128)(2,1)S(1)}, bf16[1,96,768]{2,1,0:T(8,128)(2,1)S(1)}, u32[]{:S(2)}, u32[]{:S(2)}) collective-permute-start(bf16[1,96,768]{2,1,0:T(8,128)(2,1)S(1)} %get-tuple-element.244), channel_id=1, source_target_pairs={{0,8},{4,12},{8,0},{12,4},{16,24},{20,28},{24,16},{28,20},{1,9},{5... | collective-permute-start | bytes 442376 | tf_op jit(solution)/shard_map/ppermute | solution.py:241
  368.2 14.4 %collective-permute-start.40 = (bf16[1,96,768]{2,1,0:T(8,128)(2,1)S(1)}, bf16[1,96,768]{2,1,0:T(8,128)(2,1)S(1)}, u32[]{:S(2)}, u32[]{:S(2)}) collective-permute-start(bf16[1,96,768]{2,1,0:T(8,128)(2,1)S(1)} %get-tuple-element.245), channel_id=1, source_target_pairs={{0,24},{4,28},{8,16},{12,20},{16,8},{20,12},{24,0},{28,4},{1,25},{... | collective-permute-start | bytes 442376 | tf_op jit(solution)/shard_map/ppermute | solution.py:241
  369.7 8.0 %collective-permute-start.41 = (bf16[240,768]{1,0:T(8,128)(2,1)S(1)}, bf16[240,768]{1,0:T(8,128)(2,1)S(1)}, u32[]{:S(2)}, u32[]{:S(2)}) collective-permute-start(bf16[240,768]{1,0:T(8,128)(2,1)S(1)} %broadcast_select_fusion.6), channel_id=1, source_target_pairs={{0,1},{1,0},{2,3},{3,2},{4,5},{5,4},{6,7},{7,6},{8,9},{9,8},{10,11... | collective-permute-start | bytes 1105928 | tf_op jit(solution)/shard_map/ppermute | solution.py:241
  377.6 10.3 %collective-permute-start.39 = (bf16[1,96,768]{2,1,0:T(8,128)(2,1)S(1)}, bf16[1,96,768]{2,1,0:T(8,128)(2,1)S(1)}, u32[]{:S(2)}, u32[]{:S(2)}) collective-permute-start(bf16[1,96,768]{2,1,0:T(8,128)(2,1)S(1)} %get-tuple-element.246), channel_id=1, source_target_pairs={{0,16},{4,20},{8,24},{12,28},{16,0},{20,4},{24,8},{28,12},{1,17},{... | collective-permute-start | bytes 442376 | tf_op jit(solution)/shard_map/ppermute | solution.py:241
  382.5 64.5 %collective-permute-start.30 = (bf16[4,96,2432]{2,1,0:T(8,128)(2,1)S(1)}, bf16[4,96,2432]{2,1,0:T(8,128)(2,1)S(1)}, u32[]{:S(2)}, u32[]{:S(2)}) collective-permute-start(bf16[4,96,2432]{2,1,0:T(8,128)(2,1)S(1)} %pad_maximum_fusion.1), channel_id=1, source_target_pairs={{0,4},{4,0},{8,12},{12,8},{16,20},{20,16},{24,28},{28,24},{1,5},{5... | collective-permute-start | bytes 5603336 | tf_op jit(solution)/shard_map/ppermute | solution.py:241
  382.6 11.9 %collective-permute-start.42 = (bf16[120,768]{1,0:T(8,128)(2,1)S(1)}, bf16[120,768]{1,0:T(8,128)(2,1)S(1)}, u32[]{:S(2)}, u32[]{:S(2)}) collective-permute-start(bf16[120,768]{1,0:T(8,128)(2,1)S(1)} %broadcast_select_fusion.14), channel_id=1, source_target_pairs={{0,2},{1,3},{2,0},{3,1},{4,6},{5,7},{6,4},{7,5},{8,10},{9,11},{10,... | collective-permute-start | bytes 552968 | tf_op jit(solution)/shard_map/ppermute | solution.py:241
  394.6 17.4 %collective-permute-start.43 = (bf16[216,768]{1,0:T(8,128)(2,1)S(1)}, bf16[216,768]{1,0:T(8,128)(2,1)S(1)}, u32[]{:S(2)}, u32[]{:S(2)}) collective-permute-start(bf16[216,768]{1,0:T(8,128)(2,1)S(1)} %pad_maximum_fusion.12), channel_id=1, source_target_pairs={{0,2},{1,3},{2,0},{3,1},{4,6},{5,7},{6,4},{7,5},{8,10},{9,11},{10,... | collective-permute-start | bytes 995336 | tf_op jit(solution)/shard_map/ppermute | solution.py:241
  412.2 17.9 %collective-permute-start.44 = (bf16[432,768]{1,0:T(8,128)(2,1)S(1)}, bf16[432,768]{1,0:T(8,128)(2,1)S(1)}, u32[]{:S(2)}, u32[]{:S(2)}) collective-permute-start(bf16[432,768]{1,0:T(8,128)(2,1)S(1)} %pad_maximum_fusion.4), channel_id=1, source_target_pairs={{0,1},{1,0},{2,3},{3,2},{4,5},{5,4},{6,7},{7,6},{8,9},{9,8},{10,11... | collective-permute-start | bytes 1990664 | tf_op jit(solution)/shard_map/ppermute | solution.py:241
  414.2 31.5 %collective-permute-start.29 = (bf16[512,768]{1,0:T(8,128)(2,1)S(1)}, bf16[512,768]{1,0:T(8,128)(2,1)S(1)}, u32[]{:S(2)}, u32[]{:S(2)}) collective-permute-start(bf16[512,768]{1,0:T(8,128)(2,1)S(1)} %add_convert_fusion.3), channel_id=1, source_target_pairs={{1,0},{2,1},{3,2},{5,4},{6,5},{7,6},{9,8},{10,9},{11,10},{13,12},{... | collective-permute-start | bytes 2359304 | tf_op jit(solution)/shard_map/ppermute | solution.py:246
  417.5 28.2 %collective-permute-start.27 = (bf16[512,768]{1,0:T(8,128)(2,1)S(1)}, bf16[512,768]{1,0:T(8,128)(2,1)S(1)}, u32[]{:S(2)}, u32[]{:S(2)}) collective-permute-start(bf16[512,768]{1,0:T(8,128)(2,1)S(1)} %add_convert_fusion.4), channel_id=1, source_target_pairs={{0,1},{1,2},{2,3},{4,5},{5,6},{6,7},{8,9},{9,10},{10,11},{12,13},{... | collective-permute-start | bytes 2359304 | tf_op jit(solution)/shard_map/ppermute | solution.py:246
  447.7 18.8 %collective-permute-start.31 = (bf16[1,96,2432]{2,1,0:T(8,128)(2,1)S(1)}, bf16[1,96,2432]{2,1,0:T(8,128)(2,1)S(1)}, u32[]{:S(2)}, u32[]{:S(2)}) collective-permute-start(bf16[1,96,2432]{2,1,0:T(8,128)(2,1)S(1)} %get-tuple-element.206), channel_id=1, source_target_pairs={{0,8},{4,12},{8,0},{12,4},{16,24},{20,28},{24,16},{28,20},{1,9},{5... | collective-permute-start | bytes 1400840 | tf_op jit(solution)/shard_map/ppermute | solution.py:241
  454.9 19.4 %collective-permute-start.33 = (bf16[1,96,2432]{2,1,0:T(8,128)(2,1)S(1)}, bf16[1,96,2432]{2,1,0:T(8,128)(2,1)S(1)}, u32[]{:S(2)}, u32[]{:S(2)}) collective-permute-start(bf16[1,96,2432]{2,1,0:T(8,128)(2,1)S(1)} %get-tuple-element.207), channel_id=1, source_target_pairs={{0,24},{4,28},{8,16},{12,20},{16,8},{20,12},{24,0},{28,4},{1,25},{... | collective-permute-start | bytes 1400840 | tf_op jit(solution)/shard_map/ppermute | solution.py:241
  454.9 21.3 %collective-permute-start.32 = (bf16[1,96,2432]{2,1,0:T(8,128)(2,1)S(1)}, bf16[1,96,2432]{2,1,0:T(8,128)(2,1)S(1)}, u32[]{:S(2)}, u32[]{:S(2)}) collective-permute-start(bf16[1,96,2432]{2,1,0:T(8,128)(2,1)S(1)} %get-tuple-element.208), channel_id=1, source_target_pairs={{0,16},{4,20},{8,24},{12,28},{16,0},{20,4},{24,8},{28,12},{1,17},{... | collective-permute-start | bytes 1400840 | tf_op jit(solution)/shard_map/ppermute | solution.py:241
  491.8 7.5 %collective-permute-start.34 = (bf16[160,768]{1,0:T(8,128)(2,1)S(1)}, bf16[160,768]{1,0:T(8,128)(2,1)S(1)}, u32[]{:S(2)}, u32[]{:S(2)}) collective-permute-start(bf16[160,768]{1,0:T(8,128)(2,1)S(1)} %broadcast_select_fusion.11), channel_id=1, source_target_pairs={{0,1},{1,0},{2,3},{3,2},{4,5},{5,4},{6,7},{7,6},{8,9},{9,8},{10,11... | collective-permute-start | bytes 737288 | tf_op jit(solution)/shard_map/ppermute | solution.py:241
  499.5 8.8 %collective-permute-start.35 = (bf16[80,768]{1,0:T(8,128)(2,1)S(1)}, bf16[80,768]{1,0:T(8,128)(2,1)S(1)}, u32[]{:S(2)}, u32[]{:S(2)}) collective-permute-start(bf16[80,768]{1,0:T(8,128)(2,1)S(1)} %broadcast_select_fusion.19), channel_id=1, source_target_pairs={{0,2},{1,3},{2,0},{3,1},{4,6},{5,7},{6,4},{7,5},{8,10},{9,11},{10,... | collective-permute-start | bytes 368648 | tf_op jit(solution)/shard_map/ppermute | solution.py:241
  508.4 6.7 %collective-permute-start.36 = (bf16[80,768]{1,0:T(8,128)(2,1)S(1)}, bf16[80,768]{1,0:T(8,128)(2,1)S(1)}, u32[]{:S(2)}, u32[]{:S(2)}) collective-permute-start(bf16[80,768]{1,0:T(8,128)(2,1)S(1)} %add_convert_fusion.13), channel_id=1, source_target_pairs={{0,2},{1,3},{2,0},{3,1},{4,6},{5,7},{6,4},{7,5},{8,10},{9,11},{10,... | collective-permute-start | bytes 368648 | tf_op jit(solution)/shard_map/ppermute | solution.py:241
  515.1 6.3 %collective-permute-start.37 = (bf16[160,768]{1,0:T(8,128)(2,1)S(1)}, bf16[160,768]{1,0:T(8,128)(2,1)S(1)}, u32[]{:S(2)}, u32[]{:S(2)}) collective-permute-start(bf16[160,768]{1,0:T(8,128)(2,1)S(1)} %pad_maximum_fusion.18), channel_id=1, source_target_pairs={{0,1},{1,0},{2,3},{3,2},{4,5},{5,4},{6,7},{7,6},{8,9},{9,8},{10,11... | collective-permute-start | bytes 737288 | tf_op jit(solution)/shard_map/ppermute | solution.py:241
  (109 other events, 1443.3 us)
Sparse Core Ops, SparseCore 0:
  11.0 37.4 all-gather.6
  51.0 63.8 all-gather.8
  116.8 38.9 all-gather.10
  158.0 38.9 all-gather.12
  352.1 43.4 all-gather.14
where the time goes:
time: 539 us; the launch traced here: 531 us
  waiting for transfers between devices  158 us (29%)
  matrix products  106 us (20%)
  starting transfers between devices  92.6 us (17%)
  Pallas kernels  68.3 us (13%)
  other arithmetic  43.1 us (8%)
  local copies, waits for them, and re-layouts  37.3 us (7%)
  between operations  25.7 us (5%)
    ppermute x22, waiting for transfers between devices, swap(): return lax.ppermute(values, axis, [(n, n ^ bit) for n in range(count)])  91.6 us
    pallas_call x2, Pallas kernels, attn_bwd(): pl.pallas_call(kernel, grid=(count,), in_specs=[pl.BlockSpec(memory_space...  42.4 us
    ppermute x22, starting transfers between devices, swap(): return lax.ppermute(values, axis, [(n, n ^ bit) for n in range(count)])  39.2 us
    dot_general x17, matrix products, nn(): lax.dot_general(a, b, (((1,), (0,)), ((), ())), preferred_element_type=jn...  37.6 us
    ppermute x8, waiting for transfers between devices, shift(): lax.ppermute(values, axis, [(n, n + step) for n in range(count) if 0 <= n...  36 us
    dot_general x22, matrix products, nt(): lax.dot_general(a, b, (((1,), (1,)), ((), ())), preferred_element_type=jn...  33.3 us
    dot_general x15, matrix products, tn(): lax.dot_general(a, b, (((0,), (0,)), ((), ())), preferred_element_type=jn...  31.1 us
    ppermute x8, starting transfers between devices, shift(): lax.ppermute(values, axis, [(n, n + step) for n in range(count) if 0 <= n...  26.7 us
  transfers between devices with their start and end apart: 50, of which 26 were waited for; matrix products, arithmetic and copies ran while one was open for 25% of the time, Pallas kernels for 13%

commit v1 on v0

--- a/solution.py
+++ b/solution.py
@@ -51,13 +51,15 @@
                 off = ((r - c) if flip else (c - r)) + 2*(d-2)
                 tiles[hh, d, r*SUB:(r+1)*SUB, c*SUB:(c+1)*SUB] = low if off < -1 else high if off > 1 else near[off+1]
 
-def fwd_kernel(info, band_ref, q_ref, k_ref, v_ref, ctx_ref, lse_ref, tiles, s_scr):
+def fwd_kernel(info, band_ref, q_ref, k_ref, v_ref, ctx_ref, lse_ref, tiles, s_scr, kt_scr):
     p0, e0, e1 = info[0], info[1], info[2]
     T = q_ref.shape[0]; G = k_ref.shape[0]
     lane = lax.broadcasted_iota(jnp.int32, (1,128), 1)
     left = lane < HEAD
     for hh in range(2):
         build_tiles(band_ref, tiles, hh, False)
+    for c in range(G//BLK):
+        kt_scr[c] = k_ref[c*BLK:(c+1)*BLK, :].T
     for i in range(T//BLK):
         a = p0 + i*BLK; b = a + BLK - 1
         lo = jnp.where(a >= e1, e1, jnp.where(a >= e0, e0, 0))
@@ -70,15 +72,14 @@
         zero = jnp.zeros_like(qb)
         qh = [jnp.where(left, qb, zero), jnp.where(left, zero, qb)]
         def score(j, carry):
-            koff = pl.multiple_of(lax.rem(j*BLK + G - p0, G), BLK)
-            kb = k_ref[pl.ds(koff, BLK), :]
+            kt = kt_scr[lax.rem(j*BLK + G - p0, G) // BLK]
             kpos = j*BLK + lax.broadcasted_iota(jnp.int32, (1,BLK), 1)
             kseg = seg_of(kpos, e0, e1)
             same = jnp.concatenate([row_seg == kseg[:, :128], row_seg == kseg[:,128:]],axis=1)
             d = jnp.clip(j - ib, -2, 2) + 2
             out = []
             for hh in range(2):
-                s = nt(qh[hh], kb) + tiles[hh, d]
+                s = nn(qh[hh], kt) + tiles[hh, d]
                 s = jnp.where(same, s, NEG)
                 s_scr[hh, j] = s
                 out.append(jnp.maximum(carry[hh], jnp.maximum(s[:, :128], s[:, 128:])))
@@ -117,12 +118,13 @@
                   pl.BlockSpec((G,128), lambda p:(0,p))],
         out_specs=[pl.BlockSpec((T,128), lambda p:(0,p)), pl.BlockSpec((T,128), lambda p:(0,p))],
         out_shape=[jax.ShapeDtypeStruct((T,W), jnp.bfloat16), jax.ShapeDtypeStruct((T,W), jnp.float32)],
-        scratch_shapes=[pltpu.VMEM((2,5,BLK,BLK), jnp.float32), pltpu.VMEM((2,G//BLK,BLK,BLK), jnp.float32)],
+        scratch_shapes=[pltpu.VMEM((2,5,BLK,BLK), jnp.float32), pltpu.VMEM((2,G//BLK,BLK,BLK), jnp.float32),
+                        pltpu.VMEM((G//BLK,128,BLK), jnp.bfloat16)],
         compiler_params=pltpu.CompilerParams(vmem_limit_bytes=24<<20),
         cost_estimate=pl.CostEstimate(flops=4*HEADS*T*1280*128, bytes_accessed=4*G*W+8*T*W, transcendentals=HEADS*T*1280),
     )(info, band, q, k, v)
 
-def bwd_kernel(info, band_ref, q_ref, k_ref, v_ref, g_ref, ctx_ref, lse_ref, gq_ref, gk_ref, gv_ref, gb_ref, gf_ref, tiles, gt, gk_acc, gv_acc):
+def bwd_kernel(info, band_ref, q_ref, k_ref, v_ref, g_ref, ctx_ref, lse_ref, gq_ref, gk_ref, gv_ref, gb_ref, gf_ref, tiles, gt, gk_acc, gv_acc, kt_scr):
     p0, e0, e1 = info[0], info[1], info[2]
     T = q_ref.shape[0]; G = k_ref.shape[0]
     lane = lax.broadcasted_iota(jnp.int32, (1,128), 1)
@@ -130,6 +132,8 @@
     sub_left = lax.broadcasted_iota(jnp.int32, (128,1), 0) < HEAD
     for hh in range(2):
         build_tiles(band_ref, tiles, hh, True)
+    for c in range(G//BLK//2):
+        kt_scr[c] = k_ref[c*2*BLK:(c+1)*2*BLK, :].T
     gt[...] = jnp.zeros_like(gt)
     gk_acc[...] = jnp.zeros_like(gk_acc)
     gv_acc[...] = jnp.zeros_like(gv_acc)
@@ -144,39 +148,46 @@
         zero = jnp.zeros_like(qb)
         qh = [jnp.where(left, qb, zero), jnp.where(left, zero, qb)]
         gh = [jnp.where(left, gb, zero), jnp.where(left, zero, gb)]
+        qt = [x.T for x in qh]; gth = [x.T for x in gh]
         prod = (gb.astype(jnp.float32) * ctx_ref[rows,:].astype(jnp.float32)).T
         lse_t = lse_ref[rows,:].T
         dot = [jnp.sum(prod[hh*HEAD:(hh+1)*HEAD], axis=0, keepdims=True) for hh in range(2)]
         lse = [lse_t[hh*HEAD:hh*HEAD+1] for hh in range(2)]
         q_pos = a + lax.broadcasted_iota(jnp.int32, (1,BLK), 1)
         q_seg = seg_of(q_pos, e0, e1)
-        def step(j, carry):
-            koff = pl.multiple_of(lax.rem(j*BLK + G - p0, G), BLK)
-            kb = k_ref[pl.ds(koff, BLK), :]
-            vb = v_ref[pl.ds(koff, BLK), :]
-            kpos = j*BLK + lax.broadcasted_iota(jnp.int32, (BLK,1), 0)
-            same = jnp.broadcast_to(seg_of(kpos, e0, e1), (BLK,BLK)) == jnp.broadcast_to(q_seg, (BLK,BLK))
-            d = jnp.clip(j - ib, -2, 2) + 2
+        def step(jj, carry):
+            koff = pl.multiple_of(lax.rem(jj*2*BLK + G - p0, G), 2*BLK)
+            kb = k_ref[pl.ds(koff, 2*BLK), :]
+            vb = v_ref[pl.ds(koff, 2*BLK), :]
+            kt = kt_scr[koff // (2*BLK)]
+            same = []
+            for half in range(2):
+                kpos = (jj*2+half)*BLK + lax.broadcasted_iota(jnp.int32, (BLK,1), 0)
+                same.append(jnp.broadcast_to(seg_of(kpos, e0, e1), (BLK,BLK)) == jnp.broadcast_to(q_seg, (BLK,BLK)))
             gqs=[]
             gk = None; gv=None
             for hh in range(2):
-                s = nt(kb, qh[hh]) + tiles[hh, d]
-                s = jnp.where(same, s, NEG)
-                p = jnp.exp(s - lse[hh])
-                gp = nt(vb, gh[hh])
-                gs = p * (gp - dot[hh])
-                gt[hh, d] += gs
-                pb = p.astype(jnp.bfloat16); gsb = gs.astype(jnp.bfloat16)
+                s_all = nn(kb, qt[hh]); gp_all = nn(vb, gth[hh])
+                ps = []; gss = []
+                for half in range(2):
+                    d = jnp.clip(jj*2 + half - ib, -2, 2) + 2
+                    s = s_all[half*BLK:(half+1)*BLK] + tiles[hh, d]
+                    s = jnp.where(same[half], s, NEG)
+                    p = jnp.exp(s - lse[hh])
+                    gs = p * (gp_all[half*BLK:(half+1)*BLK] - dot[hh])
+                    gt[hh, d] += gs
+                    ps.append(p.astype(jnp.bfloat16)); gss.append(gs.astype(jnp.bfloat16))
+                pb = jnp.concatenate(ps, axis=0); gsb = jnp.concatenate(gss, axis=0)
                 tk = nn(gsb, qh[hh]); tv = nn(pb, gh[hh])
                 gk = tk if gk is None else gk + tk
                 gv = tv if gv is None else gv + tv
-                gqs.append(carry[hh] + tn(gsb, kb))
-            gk_acc[pl.ds(koff,BLK), :] += gk
-            gv_acc[pl.ds(koff,BLK), :] += gv
+                gqs.append(carry[hh] + nn(kt[hh*HEAD:(hh+1)*HEAD], gsb))
+            gk_acc[pl.ds(koff,2*BLK), :] += gk
+            gv_acc[pl.ds(koff,2*BLK), :] += gv
             return tuple(gqs)
-        zf = jnp.zeros((BLK,128), jnp.float32)
-        gq = lax.fori_loop(j0, j1, step, (zf, zf))
-        gq_ref[rows,:] = jnp.where(left, gq[0], gq[1]).astype(jnp.bfloat16)
+        zf = jnp.zeros((HEAD,BLK), jnp.float32)
+        gq = lax.fori_loop(j0 // 2, (j1 + 1) // 2, step, (zf, zf))
+        gq_ref[rows,:] = jnp.concatenate(gq, axis=0).T.astype(jnp.bfloat16)
     gk_ref[...] = gk_acc[...].astype(jnp.bfloat16)
     gv_ref[...] = gv_acc[...].astype(jnp.bfloat16)
     for hh in range(2):
@@ -215,7 +226,8 @@
         out_shape=[jax.ShapeDtypeStruct((T,W), jnp.bfloat16), jax.ShapeDtypeStruct((G,W), jnp.bfloat16), jax.ShapeDtypeStruct((G,W), jnp.bfloat16),
                    jax.ShapeDtypeStruct((pairs,2,BAND), jnp.float32), jax.ShapeDtypeStruct((pairs,2,2*SUB), jnp.float32)],
         scratch_shapes=[pltpu.VMEM((2,5,BLK,BLK), jnp.float32), pltpu.VMEM((2,5,BLK,BLK), jnp.float32),
-                        pltpu.VMEM((G,128), jnp.float32), pltpu.VMEM((G,128), jnp.float32)],
+                        pltpu.VMEM((G,128), jnp.float32), pltpu.VMEM((G,128), jnp.float32),
+                        pltpu.VMEM((G//BLK//2,128,2*BLK), jnp.bfloat16)],
         input_output_aliases={8+n: n for n in range(len(extra))},
         compiler_params=pltpu.CompilerParams(vmem_limit_bytes=24<<20),
         cost_estimate=pl.CostEstimate(flops=count*10*2*T*1280*128*4, bytes_accessed=(8*G*W+12*T*W)*count//pairs, transcendentals=2*count*T*1280),
@@ -292,27 +304,19 @@
     return add_low(jnp.where(mine == 0, low, high), swap(jnp.where(mine == 0, high, low), "seq", bit))
 
 
-def whole_seq(pieces, dims, width):
-    index = lax.axis_index("seq")
-    for bit in bits_of("seq")[::-1]:
-        mine = index // bit % 2
-        shapes = [piece.shape for piece in pieces]
-        flat = [jnp.concatenate(jnp.split(piece, piece.shape[1] // width, axis=1), axis=0) for piece in pieces]
-        come = swap(jnp.concatenate(flat, axis=0), "seq", bit)
-        at = 0
-        for n, (shape, dim) in enumerate(zip(shapes, dims)):
-            rows = flat[n].shape[0]
-            other = come[at : at + rows]
-            at += rows
-            other = jnp.concatenate(jnp.split(other, shape[1] // width, axis=0), axis=1)
-            pieces[n] = jnp.concatenate([jnp.where(mine == 0, pieces[n], other), jnp.where(mine == 0, other, pieces[n])], axis=dim)
-    return pieces
-
-
-def sum_seq(piece, dim):
-    for bit in bits_of("seq"):
-        piece = halve_seq(piece, bit, dim)
-    return whole_seq([piece], [dim], piece.shape[1])[0]
+def join_seq(pieces, dims, bit, width):
+    mine = lax.axis_index("seq") // bit % 2
+    flat = [jnp.concatenate(jnp.split(piece, piece.shape[1] // width, axis=1), axis=0) for piece in pieces]
+    come = swap(jnp.concatenate(flat, axis=0), "seq", bit)
+    at = 0
+    joined = []
+    for piece, rows_of, dim in zip(pieces, flat, dims):
+        other = come[at : at + rows_of.shape[0]]
+        at += rows_of.shape[0]
+        other = jnp.concatenate(jnp.split(other, piece.shape[1] // width, axis=0), axis=1)
+        low, high = jnp.where(mine == 0, piece, other), jnp.where(mine == 0, other, piece)
+        joined.append(jnp.concatenate([low, high], axis=dim))
+    return joined
 
 
 def gather_seq(values):
@@ -343,17 +347,6 @@
         found += [left[count - place]] if count - place <= reach else []
         slots.append(sum(found[1:], found[0]) if found else jnp.zeros_like(values))
     return jnp.concatenate(slots, axis=0), beside
-
-
-def scatter_window(block, reach):
-    total = None
-    carried = {}
-    for far in range(reach, 0, -1):
-        for sign in (1, -1):
-            term = block(sign * far)
-            moving = term.astype(jnp.bfloat16) if far == reach else add_low(term, carried[sign])
-            carried[sign] = shift(moving, "seq", sign)
-    return carried[1].astype(jnp.float32) + carried[-1].astype(jnp.float32)
 
 
 eps = 1e-06
@@ -551,14 +544,6 @@
         [shard[:, n * width : (n + 1) * width] for n in range(shard.shape[1] // width)], axis=0)
     unstack = lambda rows_of: jnp.concatenate(
         [rows_of[n * part : (n + 1) * part] for n in range(rows_of.shape[0] // part)], axis=1)
-    across = scatter_chips(across)
-    early = stack(early)
-    for bit in seq_bits:
-        early = halve_seq(early, bit, 0)
-    across, early = whole_seq([across, early], [1, 0], width)
-    shard_ff_out = early[: wide * part].astype(f32)
-    shard_ff_in = across.astype(f32)
-    shard_out = early[wide * part :].astype(f32)
     grad_query, grad_key, grad_value, grad_band, grad_far = grads
     reach = window_blocks(rows)
 
@@ -567,12 +552,22 @@
         block = lambda values: values[place : place + rows]
         return nt(block(grad_key), kv_full[:, :width]) + nt(block(grad_value), kv_full[:, width:])
 
-    grad_normed = scatter_window(term, reach) + (term(0) + nt(grad_query, query_full))
+    signs = (1, -1)
+    moving = [shift(term(sign * reach).astype(bf16), "seq", sign) for sign in signs]
+    early = halve_seq(stack(early), seq_bits[0], 0)
+    across = scatter_chips(across)
     late = [tn(normed, grad_query), tn(normed_all, grad_key), tn(normed_all, grad_value)]
     late = [piece.astype(bf16).reshape(fsdp, part, width) for piece in late]
     grad_table = table_grad(grad_band, grad_far).reshape(fsdp, 1, buckets_part).astype(bf16)
     late += [jnp.pad(grad_table, ((0, 0), (0, part - 1), (0, 128 - buckets_part)))]
     late = scatter_core(late)
+    near = [[term(sign * far) for sign in signs] for far in range(reach - 1, 0, -1)]
+    moving, early, across, late, near = lax.optimization_barrier((moving, early, across, late, near))
+    for terms in near:
+        moving = [shift(add_low(one, come), "seq", sign) for one, come, sign in zip(terms, moving, signs)]
+    for bit in seq_bits[1:]:
+        early = halve_seq(early, bit, 0)
+    late = scatter_chips(late)
     rowset = lambda n: packs[:, n * tile : (n + 1) * tile].reshape(fsdp * tile, width)
     mine = lambda values: lax.dynamic_slice_in_dim(values, own * part, part, 1)
     at = 12
@@ -591,14 +586,25 @@
         tn(mine(rowset(10)), pre_all),
         tn(lax.dynamic_slice_in_dim(hid_all, own * part_ff, part_ff, 1), rowset(11)),
     ]
-    late = scatter_chips(late)
-    late, dec_shards = lax.optimization_barrier((late, dec_shards))
+    moving, early, late, dec_shards = lax.optimization_barrier((moving, early, late, dec_shards))
     shard_self_value, shard_self_out, shard_cross_query, shard_cross_key = dec_shards[:4]
     shard_cross_value, shard_cross_out, shard_dff_in, shard_dff_out = dec_shards[4:]
     table_rows = jnp.pad(late[:1, 3 * width :], ((0, 31), (0, width - 128)))
-    late = sum_seq(jnp.concatenate([stack(late[:, : 3 * width]), table_rows], axis=0), 0).astype(f32)
+    late = jnp.concatenate([stack(late[:, : 3 * width]), table_rows], axis=0)
+    for back, bit in zip(seq_bits[::-1], seq_bits):
+        across, early = join_seq([across, early], [1, 0], back, width)
+        late = halve_seq(late, bit, 0)
+        across, early, late = lax.optimization_barrier((across, early, late))
+    for back in seq_bits[::-1]:
+        (late,) = join_seq([late], [0], back, width)
+    shard_ff_out = early[: wide * part].astype(f32)
+    shard_ff_in = across.astype(f32)
+    shard_out = early[wide * part :].astype(f32)
+    late = late.astype(f32)
     shard_query, shard_key, shard_value = (late[n * part : (n + 1) * part] for n in range(3))
     shard_table = late[3 * part, :buckets_part]
+    grad_normed = term(0) + nt(grad_query, query_full)
+    grad_normed = grad_normed + (moving[0].astype(f32) + moving[1].astype(f32))
     back_values = norm_backward(tokens_f, inverse_attn, gain_attn_f, grad_normed)
     first_back = lax.dot_general(local_pick.astype(f32), grad_first, (((0,), (0,)), ((), ())),
                                  precision=lax.Precision.HIGHEST, preferred_element_type=f32)

time: 539 us -> 499 us (0.926)
  waiting for transfers between devices: 158 us -> 139 us
  starting transfers between devices: 92.6 us -> 75.4 us
    ppermute x22, waiting for transfers between devices: 91.6 us -> 64.3 us  [swap(): return lax.ppermute(values, axis, [(n, n ^ bit) for n in range(count)])]
    ppermute x22, starting transfers between devices: 39.2 us -> 28.3 us  [swap(): return lax.ppermute(values, axis, [(n, n ^ bit) for n in range(count)])]
    all_gather x4, waiting for transfers between devices: 16.1 us -> 25.3 us  [body(): lax.all_gather(jnp.concatenate(pieces, axis=1), 'fsdp', axis=0, tiled=True)]
    unnamed x246 -> x220, local copies, waits for them, and re-layouts: 17.6 us -> 17.1 us
  transfers between devices with their start and end apart: 50 -> 50, of which waited for: 26 -> 27; matrix products, arithmetic and copies ran while one was open for 25% -> 32% of each run, Pallas kernels for 13% -> 13%
where the time goes in v1:
time: 499 us; the launch traced here: 494 us
  waiting for transfers between devices  139 us (28%)
  matrix products  108 us (22%)
  starting transfers between devices  75.4 us (15%)
  Pallas kernels  63.8 us (13%)
  other arithmetic  42.8 us (9%)
  local copies, waits for them, and re-layouts  39.8 us (8%)
  between operations  25.4 us (5%)
    ppermute x22, waiting for transfers between devices, swap(): return lax.ppermute(values, axis, [(n, n ^ bit) for n in range(count)])  64.3 us
    dot_general x17, matrix products, nn(): lax.dot_general(a, b, (((1,), (0,)), ((), ())), preferred_element_type=jn...  38.3 us
    pallas_call x2, Pallas kernels, attn_bwd(): pl.pallas_call(kernel, grid=(count,), in_specs=[pl.BlockSpec(memory_space...  37.4 us
    ppermute x8, waiting for transfers between devices, shift(): lax.ppermute(values, axis, [(n, n + step) for n in range(count) if 0 <= n...  35.7 us
    dot_general x22, matrix products, nt(): lax.dot_general(a, b, (((1,), (1,)), ((), ())), preferred_element_type=jn...  34.6 us
    dot_general x15, matrix products, tn(): lax.dot_general(a, b, (((0,), (0,)), ((), ())), preferred_element_type=jn...  31.2 us
    ppermute x22, starting transfers between devices, swap(): return lax.ppermute(values, axis, [(n, n ^ bit) for n in range(count)])  28.3 us
    pallas_call x1, Pallas kernels, attn_fwd(): pl.pallas_call(fwd_kernel, grid=(pairs,), in_specs=[pl.BlockSpec(memory_s...  26.4 us
  transfers between devices with their start and end apart: 50, of which 27 were waited for; matrix products, arithmetic and copies ran while one was open for 32% of the time, Pallas kernels for 13%

profile of v1, /device:TPU:0, one launch (start us, length us, event | category | flops | bytes accessed | tf_op | source)
XLA Modules:
  0.0 493.9 jit_solution(4883034206677633147)
XLA Ops:
  12.2 5.6 %collective-permute-start = (bf16[512,768]{1,0:T(8,128)(2,1)}, bf16[512,768]{1,0:T(8,128)(2,1)S(1)}, u32[]{:S(2)}, u32[]{:S(2)}) collective-permute-start(bf16[512,768]{1,0:T(8,128)(2,1)} %param.28), channel_id=1, source_target_pairs={{0,1},{1,2},{2,3},{4,5},{5,6},{6,7},{8,9},{9,10},{10,11},{12,13},{... | collective-permute-start | bytes 2359304 | tf_op jit(solution)/shard_map/ppermute | solution.py:258
  17.9 15.8 %collective-permute-done.1 = bf16[512,768]{1,0:T(8,128)(2,1)S(1)} collective-permute-done((bf16[512,768]{1,0:T(8,128)(2,1)}, bf16[512,768]{1,0:T(8,128)(2,1)S(1)}, u32[]{:S(2)}, u32[]{:S(2)}) %collective-permute-start.1) | collective-permute-done | bytes 786464 | tf_op jit(solution)/shard_map/ppermute | solution.py:258
  45.0 2.4 collective-permute-start.6
  47.3 2.8 collective-permute-start.5
  63.5 5.5 %collective-permute-start.3 = (bf16[512,768]{1,0:T(8,128)(2,1)S(1)}, bf16[512,768]{1,0:T(8,128)(2,1)}, u32[]{:S(2)}, u32[]{:S(2)}) collective-permute-start(bf16[512,768]{1,0:T(8,128)(2,1)S(1)} %collective-permute-done), channel_id=1, source_target_pairs={{0,1},{1,2},{2,3},{4,5},{5,6},{6,7},{8,9},{9,10},{10,11},{12,13},{... | collective-permute-start | bytes 2359304 | tf_op jit(solution)/shard_map/ppermute | solution.py:258
  69.7 2.9 reshape.589
  72.6 2.4 dynamic-slice_reduce_fusion
  77.4 4.0 collective-permute-done.2
  90.6 3.7 fusion.2
  96.0 2.8 convolution_convert_fusion.2.v_ref.refs_4_
  98.9 2.8 convolution_convert_fusion.3.k_ref.refs_3_
  101.7 26.4 %shard_map.407 = (bf16[512,768]{1,0:T(8,128)(2,1)S(1)}, f32[512,768]{1,0:T(8,128)S(1)}) custom-call(s32[3]{0:T(128)S(1)} %add_add_fusion.info.refs_0_, f32[6,2,512]{2,1,0:T(2,128)S(1)} %copy.71.band_ref, bf16[512,768]{1,0:T(8,128)(2,1)S(1)} %convolution_convert_fusion.9.q_ref.refs_2_, bf16[2048,768]{1,0:T(8,128)(2,1)S(1)} %convolution_convert_fusion.3.k_ref.refs_3_, ...), custom_call_target="tpu_custom_call" | custom-call | flops 4026531840 | bytes 9437184 | tf_op jit(solution)/shard_map/pallas_call | solution.py:111
  129.8 2.4 convolution_convert_fusion.16
  134.4 2.4 multiply_reduce_fusion.1
  141.0 7.5 %fusion.13 = f32[512,3072]{1,0:T(8,128)} fusion(bf16[768,6912]{1,0:T(8,128)(2,1)} %all-gather.9.cloned.1.call-done, f32[512,768]{1,0:T(8,128)S(1)} %get-tuple-element.334, f32[768]{0:T(1024)S(1)} %get-tuple-element.194, f32[512]{0:T(512)S(1)} %get-tuple-element.320), kind=kOutput, calls=%fused_computation.23 | convolution fusion | flops 2417098752 | bytes 12588032 | tf_op jit(solution)/shard_map/dot_general | solution.py:27
  148.5 7.3 %all-gather.11.cloned.1.call-done = bf16[3072,768]{1,0:T(8,128)(2,1)} async-done(((bf16[384,768]{1,0:T(8,128)(2,1)}), bf16[3072,768]{1,0:T(8,128)(2,1)}) %all-gather.11.cloned.1.call-update) | async-done | bytes 4718608 | tf_op jit(solution)/shard_map/all_gather | solution.py:402
  155.7 9.5 %fusion.194 = (bf16[512,768]{1,0:T(8,128)(2,1)S(1)}, f32[512,768]{1,0:T(8,128)}) fusion(f32[512,768]{1,0:T(8,128)} %copy-done.34, bf16[3072,768]{1,0:T(8,128)(2,1)} %all-gather.11.cloned.1.call-done, f32[512,3072]{1,0:T(8,128)} %fusion.13), kind=kOutput, calls=%fused_computation.495 | convolution fusion | flops 2430861312 | bytes 14942208 | tf_op jit(solution)/shard_map/dot_general | solution.py:27
  166.3 2.5 collective-permute-start.8
  170.9 6.7 %collective-permute-done.8 = f32[48,896]{1,0:T(8,128)S(1)} collective-permute-done((f32[48,896]{1,0:T(8,128)S(1)}, f32[48,896]{1,0:T(8,128)S(1)}, u32[]{:S(2)}, u32[]{:S(2)}) %collective-permute-start.8) | collective-permute-done | bytes 172064 | tf_op jit(solution)/shard_map/ppermute | solution.py:325
  179.0 18.0 %all-gather.13.cloned.1.call-done = bf16[768,3072]{1,0:T(8,128)(2,1)} async-done(((bf16[96,3072]{1,0:T(8,128)(2,1)}), bf16[768,3072]{1,0:T(8,128)(2,1)}) %all-gather.13.cloned.1.call-update) | async-done | bytes 4718608 | tf_op jit(solution)/shard_map/all_gather | solution.py:402
  203.9 2.5 collective-permute-start.19
  210.1 2.9 collective-permute-start.10
  214.8 4.0 collective-permute-done.12
  224.3 3.4 collective-permute-start.15
  228.2 6.4 %convolution_convert_fusion.1 = bf16[3072,768]{1,0:T(8,128)(2,1)S(1)} fusion(f32[512,768]{1,0:T(8,128)S(1)} %convert_add_fusion.2, f32[512,3072]{1,0:T(8,128)} %fusion.13), kind=kOutput, calls=%fused_computation.18 | convolution fusion | flops 2432827392 | bytes 12582912 | tf_op jit(solution)/shard_map/dot_general | solution.py:25
  235.0 9.0 %fusion.9 = bf16[512,3072]{1,0:T(8,128)(2,1)} fusion(f32[512,3072]{1,0:T(8,128)} %fusion.13, bf16[3072,768]{1,0:T(8,128)(2,1)S(1)} %bitcast.324, f32[512,768]{1,0:T(8,128)S(1)} %convert_add_fusion.2), kind=kOutput, calls=%fused_computation.13 | convolution fusion | flops 2446196736 | bytes 15728640 | tf_op jit(solution)/shard_map/dot_general | solution.py:23
  243.9 5.1 %convolution_convert_fusion = bf16[768,3072]{1,0:T(8,128)(2,1)S(1)} fusion(bf16[512,3072]{1,0:T(8,128)(2,1)} %fusion.9, f32[512,768]{1,0:T(8,128)S(1)} %copy-done.35, f32[768]{0:T(1024)S(1)} %copy-done.75, f32[512]{0:T(512)S(1)} %copy-done.66), kind=kOutput, calls=%fused_computation.17 | convolution fusion | flops 2419458048 | bytes 9442304 | tf_op jit(solution)/shard_map/dot_general | solution.py:25
  249.1 2.7 multiply_reduce_fusion
  264.3 3.4 fusion.10
  267.8 2.7 add_convert_fusion
  275.1 18.8 %shard_map.408 = (bf16[512,768]{1,0:T(8,128)(2,1)S(1)}, bf16[2048,768]{1,0:T(8,128)(2,1)S(1)}, bf16[2048,768]{1,0:T(8,128)(2,1)S(1)}, f32[6,2,512]{2,1,0:T(2,128)S(1)}, f32[6,2,256]{2,1,0:T(2,128)S(1)}) custom-call(s32[3]{0:T(128)S(1)} %add_add_fusion.info.refs_0_, f32[6,2,512]{2,1,0:T(2,128)S(1)} %copy.93.band_ref, bf16[512,768]{1,0:T(8,128)(2,1)S(1)} %copy-done.10, ...), custom_call_target="tpu_custom_call" | custom-call | flops 20132659200 | bytes 8650752 | tf_op jit(solution)/shard_map/pallas_call | solution.py:220
  293.9 12.5 %collective-permute-done.25 = bf16[1,96,3840]{2,1,0:T(8,128)(2,1)S(1)} collective-permute-done((bf16[1,96,3840]{2,1,0:T(8,128)(2,1)S(1)}, bf16[1,96,3840]{2,1,0:T(8,128)(2,1)S(1)}, u32[]{:S(2)}, u32[]{:S(2)}) %collective-permute-start.25) | collective-permute-done | bytes 737312 | tf_op jit(solution)/shard_map/ppermute | solution.py:253
  310.6 18.6 %shard_map.409 = (bf16[512,768]{1,0:T(8,128)(2,1)S(1)}, bf16[2048,768]{1,0:T(8,128)(2,1)S(1)}, bf16[2048,768]{1,0:T(8,128)(2,1)S(1)}, f32[6,2,512]{2,1,0:T(2,128)S(1)}, f32[6,2,256]{2,1,0:T(2,128)S(1)}) custom-call(s32[3]{0:T(128)S(1)} %add_add_fusion.info.refs_0_, ...), custom_call_target="tpu_custom_call", output_to_operand_aliasing={{0}: (8, {}), {1}: (9, {}), {2}: (10, {}), {3}: (11, {}), {... | custom-call | flops 20132659200 | bytes 8650752 | tf_op jit(solution)/shard_map/pallas_call | solution.py:220
  331.7 3.5 collective-permute-done.22
  343.3 5.0 %collective-permute-start.29 = (bf16[1,96,768]{2,1,0:T(8,128)(2,1)S(1)}, bf16[1,96,768]{2,1,0:T(8,128)(2,1)S(1)}, u32[]{:S(2)}, u32[]{:S(2)}) collective-permute-start(bf16[1,96,768]{2,1,0:T(8,128)(2,1)S(1)} %get-tuple-element.276), channel_id=1, source_target_pairs={{0,8},{4,12},{8,0},{12,4},{16,24},{20,28},{24,16},{28,20},{1,9},{5... | collective-permute-start | bytes 442376 | tf_op jit(solution)/shard_map/ppermute | solution.py:253
  351.9 2.8 convolution_convert_fusion.5
  354.6 2.7 convolution_convert_fusion.4
  372.3 4.6 collective-permute-start.26
  378.6 12.2 %collective-permute-done.27 = bf16[512,768]{1,0:T(8,128)(2,1)S(1)} collective-permute-done((bf16[512,768]{1,0:T(8,128)(2,1)S(1)}, bf16[512,768]{1,0:T(8,128)(2,1)S(1)}, u32[]{:S(2)}, u32[]{:S(2)}) %collective-permute-start.27) | collective-permute-done | bytes 786464 | tf_op jit(solution)/shard_map/ppermute | solution.py:258
  405.4 4.4 collective-permute-done.36
  409.8 6.5 %collective-permute-done.38 = bf16[1,96,2432]{2,1,0:T(8,128)(2,1)S(1)} collective-permute-done((bf16[1,96,2432]{2,1,0:T(8,128)(2,1)S(1)}, bf16[1,96,2432]{2,1,0:T(8,128)(2,1)S(1)}, u32[]{:S(2)}, u32[]{:S(2)}) %collective-permute-start.38) | collective-permute-done | bytes 466976 | tf_op jit(solution)/shard_map/ppermute | solution.py:253
  435.4 3.0 collective-permute-start.40
  438.5 2.5 fusion.18
  444.0 9.7 %collective-permute-done.39 = bf16[216,768]{1,0:T(8,128)(2,1)S(1)} collective-permute-done((bf16[216,768]{1,0:T(8,128)(2,1)S(1)}, bf16[216,768]{1,0:T(8,128)(2,1)S(1)}, u32[]{:S(2)}, u32[]{:S(2)}) %collective-permute-start.39) | collective-permute-done | bytes 331808 | tf_op jit(solution)/shard_map/ppermute | solution.py:253
  454.0 3.1 collective-permute-start.42
  457.6 11.1 %collective-permute-done.42 = bf16[80,768]{1,0:T(8,128)(2,1)S(1)} collective-permute-done((bf16[80,768]{1,0:T(8,128)(2,1)S(1)}, bf16[80,768]{1,0:T(8,128)(2,1)S(1)}, u32[]{:S(2)}, u32[]{:S(2)}) %collective-permute-start.42) | collective-permute-done | bytes 122912 | tf_op jit(solution)/shard_map/ppermute | solution.py:253
  474.9 3.5 collective-permute-done.43
  480.2 4.7 collective-permute-done.44
  (505 shorter events, 164.0 us)
Async XLA Ops:
  7.3 79.9 %all-gather.7.cloned.1.call-start = ((), (), s32[]{:S(2)}) async-start(), calls=%async_computation | async-start | bytes 4202496 | tf_op jit(solution)/shard_map/all_gather | solution.py:402
  10.9 118.9 %all-gather.9.cloned.1.call-start = ((), (), s32[]{:S(2)}) async-start(), calls=%async_computation.1 | async-start | bytes 11943936 | tf_op jit(solution)/shard_map/all_gather | solution.py:402
  10.9 22.7 %collective-permute-start.1 = (bf16[512,768]{1,0:T(8,128)(2,1)}, bf16[512,768]{1,0:T(8,128)(2,1)S(1)}, u32[]{:S(2)}, u32[]{:S(2)}) collective-permute-start(bf16[512,768]{1,0:T(8,128)(2,1)} %param.28), channel_id=1, source_target_pairs={{1,0},{2,1},{3,2},{5,4},{6,5},{7,6},{9,8},{10,9},{11,10},{13,12},{... | collective-permute-start | bytes 2359304 | tf_op jit(solution)/shard_map/ppermute | solution.py:258
  12.2 22.7 %collective-permute-start = (bf16[512,768]{1,0:T(8,128)(2,1)}, bf16[512,768]{1,0:T(8,128)(2,1)S(1)}, u32[]{:S(2)}, u32[]{:S(2)}) collective-permute-start(bf16[512,768]{1,0:T(8,128)(2,1)} %param.28), channel_id=1, source_target_pairs={{0,1},{1,2},{2,3},{4,5},{5,6},{6,7},{8,9},{9,10},{10,11},{12,13},{... | collective-permute-start | bytes 2359304 | tf_op jit(solution)/shard_map/ppermute | solution.py:258
  41.3 114.4 %all-gather.11.cloned.1.call-start = ((), (), s32[]{:S(2)}) async-start(), calls=%async_computation.2 | async-start | bytes 5308416 | tf_op jit(solution)/shard_map/all_gather | solution.py:402
  42.0 154.9 %all-gather.13.cloned.1.call-start = ((), (), s32[]{:S(2)}) async-start(), calls=%async_computation.3 | async-start | bytes 5308416 | tf_op jit(solution)/shard_map/all_gather | solution.py:402
  45.0 17.2 %collective-permute-start.6 = (bf16[3,768]{1,0:T(4,128)(2,1)S(1)}, bf16[3,768]{1,0:T(4,128)(2,1)S(1)}, u32[]{:S(2)}, u32[]{:S(2)}) collective-permute-start(bf16[3,768]{1,0:T(4,128)(2,1)S(1)} %convolution_convert_fusion.17), channel_id=1, source_target_pairs={{0,1},{1,2},{2,3},{3,0},{4,5},{5,6},{6,7},{7,4},{8,9},{9,10},{10,1... | collective-permute-start | bytes 13832 | tf_op jit(solution)/shard_map/ppermute | solution.py:325
  47.3 14.8 %collective-permute-start.5 = (bf16[3,768]{1,0:T(4,128)(2,1)S(1)}, bf16[3,768]{1,0:T(4,128)(2,1)S(1)}, u32[]{:S(2)}, u32[]{:S(2)}) collective-permute-start(bf16[3,768]{1,0:T(4,128)(2,1)S(1)} %convolution_convert_fusion.17), channel_id=1, source_target_pairs={{0,2},{1,3},{2,0},{3,1},{4,6},{5,7},{6,4},{7,5},{8,10},{9,11},{10,... | collective-permute-start | bytes 13832 | tf_op jit(solution)/shard_map/ppermute | solution.py:325
  50.1 12.0 %collective-permute-start.4 = (bf16[3,768]{1,0:T(4,128)(2,1)S(1)}, bf16[3,768]{1,0:T(4,128)(2,1)S(1)}, u32[]{:S(2)}, u32[]{:S(2)}) collective-permute-start(bf16[3,768]{1,0:T(4,128)(2,1)S(1)} %convolution_convert_fusion.17), channel_id=1, source_target_pairs={{0,3},{1,0},{2,1},{3,2},{4,7},{5,4},{6,5},{7,6},{8,11},{9,8},{10,9... | collective-permute-start | bytes 13832 | tf_op jit(solution)/shard_map/ppermute | solution.py:325
  62.2 19.3 %collective-permute-start.2 = (bf16[512,768]{1,0:T(8,128)(2,1)S(1)}, bf16[512,768]{1,0:T(8,128)(2,1)}, u32[]{:S(2)}, u32[]{:S(2)}) collective-permute-start(bf16[512,768]{1,0:T(8,128)(2,1)S(1)} %collective-permute-done.1), channel_id=1, source_target_pairs={{1,0},{2,1},{3,2},{5,4},{6,5},{7,6},{9,8},{10,9},{11,10},{13,12},{... | collective-permute-start | bytes 2359304 | tf_op jit(solution)/shard_map/ppermute | solution.py:258
  63.5 19.1 %collective-permute-start.3 = (bf16[512,768]{1,0:T(8,128)(2,1)S(1)}, bf16[512,768]{1,0:T(8,128)(2,1)}, u32[]{:S(2)}, u32[]{:S(2)}) collective-permute-start(bf16[512,768]{1,0:T(8,128)(2,1)S(1)} %collective-permute-done), channel_id=1, source_target_pairs={{0,1},{1,2},{2,3},{4,5},{5,6},{6,7},{8,9},{9,10},{10,11},{12,13},{... | collective-permute-start | bytes 2359304 | tf_op jit(solution)/shard_map/ppermute | solution.py:258
  77.1 340.8 %all-gather.15.cloned.1.call-start = ((), (), s32[]{:S(2)}) async-start(), calls=%async_computation.4 | async-start | bytes 3538944 | tf_op jit(solution)/shard_map/all_gather | solution.py:542
  166.3 11.3 %collective-permute-start.8 = (f32[48,896]{1,0:T(8,128)S(1)}, f32[48,896]{1,0:T(8,128)S(1)}, u32[]{:S(2)}, u32[]{:S(2)}) collective-permute-start(f32[48,896]{1,0:T(8,128)S(1)} %get-tuple-element.295), channel_id=1, source_target_pairs={{0,2},{1,3},{2,0},{3,1},{4,6},{5,7},{6,4},{7,5},{8,10},{9,11},{10,... | collective-permute-start | bytes 516104 | tf_op jit(solution)/shard_map/ppermute | solution.py:325
  168.7 9.5 %collective-permute-start.7 = (f32[48,896]{1,0:T(8,128)S(1)}, f32[48,896]{1,0:T(8,128)S(1)}, u32[]{:S(2)}, u32[]{:S(2)}) collective-permute-start(f32[48,896]{1,0:T(8,128)S(1)} %get-tuple-element.295), channel_id=1, source_target_pairs={{0,3},{1,0},{2,1},{3,2},{4,7},{5,4},{6,5},{7,6},{8,11},{9,8},{10,9... | collective-permute-start | bytes 516104 | tf_op jit(solution)/shard_map/ppermute | solution.py:325
  170.2 8.1 %collective-permute-start.9 = (f32[48,896]{1,0:T(8,128)S(1)}, f32[48,896]{1,0:T(8,128)S(1)}, u32[]{:S(2)}, u32[]{:S(2)}) collective-permute-start(f32[48,896]{1,0:T(8,128)S(1)} %get-tuple-element.295), channel_id=1, source_target_pairs={{0,1},{1,2},{2,3},{3,0},{4,5},{5,6},{6,7},{7,4},{8,9},{9,10},{10,1... | collective-permute-start | bytes 516104 | tf_op jit(solution)/shard_map/ppermute | solution.py:325
  203.9 9.3 %collective-permute-start.19 = (bf16[6,768]{1,0:T(8,128)(2,1)S(1)}, bf16[6,768]{1,0:T(8,128)(2,1)S(1)}, u32[]{:S(2)}, u32[]{:S(2)}) collective-permute-start(bf16[6,768]{1,0:T(8,128)(2,1)S(1)} %get-tuple-element.318), channel_id=1, source_target_pairs={{0,2},{1,3},{2,0},{3,1},{4,6},{5,7},{6,4},{7,5},{8,10},{9,11},{10,... | collective-permute-start | bytes 27656 | tf_op jit(solution)/shard_map/ppermute | solution.py:325
  206.4 6.9 %collective-permute-start.18 = (bf16[6,768]{1,0:T(8,128)(2,1)S(1)}, bf16[6,768]{1,0:T(8,128)(2,1)S(1)}, u32[]{:S(2)}, u32[]{:S(2)}) collective-permute-start(bf16[6,768]{1,0:T(8,128)(2,1)S(1)} %get-tuple-element.318), channel_id=1, source_target_pairs={{0,3},{1,0},{2,1},{3,2},{4,7},{5,4},{6,5},{7,6},{8,11},{9,8},{10,9... | collective-permute-start | bytes 27656 | tf_op jit(solution)/shard_map/ppermute | solution.py:325
  207.8 5.6 %collective-permute-start.20 = (bf16[6,768]{1,0:T(8,128)(2,1)S(1)}, bf16[6,768]{1,0:T(8,128)(2,1)S(1)}, u32[]{:S(2)}, u32[]{:S(2)}) collective-permute-start(bf16[6,768]{1,0:T(8,128)(2,1)S(1)} %get-tuple-element.318), channel_id=1, source_target_pairs={{0,1},{1,2},{2,3},{3,0},{4,5},{5,6},{6,7},{7,4},{8,9},{9,10},{10,1... | collective-permute-start | bytes 27656 | tf_op jit(solution)/shard_map/ppermute | solution.py:325
  213.2 5.7 %collective-permute-start.12 = (f32[6,768]{1,0:T(8,128)S(1)}, f32[6,768]{1,0:T(8,128)S(1)}, u32[]{:S(2)}, u32[]{:S(2)}) collective-permute-start(f32[6,768]{1,0:T(8,128)S(1)} %get-tuple-element.310), channel_id=1, source_target_pairs={{0,1},{1,2},{2,3},{3,0},{4,5},{5,6},{6,7},{7,4},{8,9},{9,10},{10,1... | collective-permute-start | bytes 55304 | tf_op jit(solution)/shard_map/ppermute | solution.py:325
  223.9 37.8 %collective-permute-start.17 = (bf16[48,768]{1,0:T(8,128)(2,1)S(1)}, bf16[48,768]{1,0:T(8,128)(2,1)S(1)}, u32[]{:S(2)}, u32[]{:S(2)}) collective-permute-start(bf16[48,768]{1,0:T(8,128)(2,1)S(1)} %convolution_convert_fusion.12), channel_id=1, source_target_pairs={{0,1},{1,2},{2,3},{3,0},{4,5},{5,6},{6,7},{7,4},{8,9},{9,10},{10,1... | collective-permute-start | bytes 221192 | tf_op jit(solution)/shard_map/ppermute | solution.py:325
  223.9 37.7 %collective-permute-start.16 = (bf16[48,768]{1,0:T(8,128)(2,1)S(1)}, bf16[48,768]{1,0:T(8,128)(2,1)S(1)}, u32[]{:S(2)}, u32[]{:S(2)}) collective-permute-start(bf16[48,768]{1,0:T(8,128)(2,1)S(1)} %convolution_convert_fusion.12), channel_id=1, source_target_pairs={{0,2},{1,3},{2,0},{3,1},{4,6},{5,7},{6,4},{7,5},{8,10},{9,11},{10,... | collective-permute-start | bytes 221192 | tf_op jit(solution)/shard_map/ppermute | solution.py:325
  224.3 37.4 %collective-permute-start.15 = (bf16[48,768]{1,0:T(8,128)(2,1)S(1)}, bf16[48,768]{1,0:T(8,128)(2,1)S(1)}, u32[]{:S(2)}, u32[]{:S(2)}) collective-permute-start(bf16[48,768]{1,0:T(8,128)(2,1)S(1)} %convolution_convert_fusion.12), channel_id=1, source_target_pairs={{0,3},{1,0},{2,1},{3,2},{4,7},{5,4},{6,5},{7,6},{8,11},{9,8},{10,9... | collective-permute-start | bytes 221192 | tf_op jit(solution)/shard_map/ppermute | solution.py:325
  254.7 9.7 %collective-permute-start.14 = (bf16[4,96,3072]{2,1,0:T(8,128)(2,1)}, bf16[4,96,3072]{2,1,0:T(8,128)(2,1)}, u32[]{:S(2)}, u32[]{:S(2)}) collective-permute-start(bf16[4,96,3072]{2,1,0:T(8,128)(2,1)} %dynamic-slice_bitcast_fusion), channel_id=1, source_target_pairs={{0,4},{4,0},{8,12},{12,8},{16,20},{20,16},{24,28},{28,24},{1,5},{5... | collective-permute-start | bytes 7077896 | tf_op jit(solution)/shard_map/ppermute | solution.py:253
  259.4 8.3 %collective-permute-start.13 = (bf16[4,96,3840]{2,1,0:T(8,128)(2,1)}, bf16[4,96,3840]{2,1,0:T(8,128)(2,1)}, u32[]{:S(2)}, u32[]{:S(2)}) collective-permute-start(bf16[4,96,3840]{2,1,0:T(8,128)(2,1)} %get-tuple-element.248), channel_id=1, source_target_pairs={{0,4},{4,0},{8,12},{12,8},{16,20},{20,16},{24,28},{28,24},{1,5},{5... | collective-permute-start | bytes 8847368 | tf_op jit(solution)/shard_map/ppermute | solution.py:253
  270.7 37.5 %collective-permute-start.21 = (bf16[4,96,1536]{2,1,0:T(8,128)(2,1)S(1)}, bf16[4,96,1536]{2,1,0:T(8,128)(2,1)S(1)}, u32[]{:S(2)}, u32[]{:S(2)}) collective-permute-start(bf16[4,96,1536]{2,1,0:T(8,128)(2,1)S(1)} %broadcast_select_fusion), channel_id=1, source_target_pairs={{0,1},{1,0},{2,3},{3,2},{4,5},{5,4},{6,7},{7,6},{8,9},{9,8},{10,11... | collective-permute-start | bytes 3538952 | tf_op jit(solution)/shard_map/ppermute | solution.py:253
  271.5 22.4 %collective-permute-start.23 = (bf16[1,96,3840]{2,1,0:T(8,128)(2,1)S(1)}, bf16[1,96,3840]{2,1,0:T(8,128)(2,1)S(1)}, u32[]{:S(2)}, u32[]{:S(2)}) collective-permute-start(bf16[1,96,3840]{2,1,0:T(8,128)(2,1)S(1)} %get-tuple-element.235), channel_id=1, source_target_pairs={{0,8},{4,12},{8,0},{12,4},{16,24},{20,28},{24,16},{28,20},{1,9},{5... | collective-permute-start | bytes 2211848 | tf_op jit(solution)/shard_map/ppermute | solution.py:253
  273.1 33.4 %collective-permute-start.25 = (bf16[1,96,3840]{2,1,0:T(8,128)(2,1)S(1)}, bf16[1,96,3840]{2,1,0:T(8,128)(2,1)S(1)}, u32[]{:S(2)}, u32[]{:S(2)}) collective-permute-start(bf16[1,96,3840]{2,1,0:T(8,128)(2,1)S(1)} %get-tuple-element.236), channel_id=1, source_target_pairs={{0,24},{4,28},{8,16},{12,20},{16,8},{20,12},{24,0},{28,4},{1,25},{... | collective-permute-start | bytes 2211848 | tf_op jit(solution)/shard_map/ppermute | solution.py:253
  274.4 33.5 %collective-permute-start.24 = (bf16[1,96,3840]{2,1,0:T(8,128)(2,1)S(1)}, bf16[1,96,3840]{2,1,0:T(8,128)(2,1)S(1)}, u32[]{:S(2)}, u32[]{:S(2)}) collective-permute-start(bf16[1,96,3840]{2,1,0:T(8,128)(2,1)S(1)} %get-tuple-element.237), channel_id=1, source_target_pairs={{0,16},{4,20},{8,24},{12,28},{16,0},{20,4},{24,8},{28,12},{1,17},{... | collective-permute-start | bytes 2211848 | tf_op jit(solution)/shard_map/ppermute | solution.py:253
  308.7 26.4 %collective-permute-start.22 = (bf16[4,96,768]{2,1,0:T(8,128)(2,1)S(1)}, bf16[4,96,768]{2,1,0:T(8,128)(2,1)S(1)}, u32[]{:S(2)}, u32[]{:S(2)}) collective-permute-start(bf16[4,96,768]{2,1,0:T(8,128)(2,1)S(1)} %broadcast_select_fusion.3), channel_id=1, source_target_pairs={{0,2},{1,3},{2,0},{3,1},{4,6},{5,7},{6,4},{7,5},{8,10},{9,11},{10,... | collective-permute-start | bytes 1769480 | tf_op jit(solution)/shard_map/ppermute | solution.py:253
  341.9 36.0 %collective-permute-start.28 = (bf16[240,768]{1,0:T(8,128)(2,1)S(1)}, bf16[240,768]{1,0:T(8,128)(2,1)S(1)}, u32[]{:S(2)}, u32[]{:S(2)}) collective-permute-start(bf16[240,768]{1,0:T(8,128)(2,1)S(1)} %broadcast_select_fusion.6), channel_id=1, source_target_pairs={{0,1},{1,0},{2,3},{3,2},{4,5},{5,4},{6,7},{7,6},{8,9},{9,8},{10,11... | collective-permute-start | bytes 1105928 | tf_op jit(solution)/shard_map/ppermute | solution.py:253
  343.3 27.5 %collective-permute-start.29 = (bf16[1,96,768]{2,1,0:T(8,128)(2,1)S(1)}, bf16[1,96,768]{2,1,0:T(8,128)(2,1)S(1)}, u32[]{:S(2)}, u32[]{:S(2)}) collective-permute-start(bf16[1,96,768]{2,1,0:T(8,128)(2,1)S(1)} %get-tuple-element.276), channel_id=1, source_target_pairs={{0,8},{4,12},{8,0},{12,4},{16,24},{20,28},{24,16},{28,20},{1,9},{5... | collective-permute-start | bytes 442376 | tf_op jit(solution)/shard_map/ppermute | solution.py:253
  348.3 24.0 %collective-permute-start.31 = (bf16[1,96,768]{2,1,0:T(8,128)(2,1)S(1)}, bf16[1,96,768]{2,1,0:T(8,128)(2,1)S(1)}, u32[]{:S(2)}, u32[]{:S(2)}) collective-permute-start(bf16[1,96,768]{2,1,0:T(8,128)(2,1)S(1)} %get-tuple-element.277), channel_id=1, source_target_pairs={{0,24},{4,28},{8,16},{12,20},{16,8},{20,12},{24,0},{28,4},{1,25},{... | collective-permute-start | bytes 442376 | tf_op jit(solution)/shard_map/ppermute | solution.py:253
  348.3 28.6 %collective-permute-start.30 = (bf16[1,96,768]{2,1,0:T(8,128)(2,1)S(1)}, bf16[1,96,768]{2,1,0:T(8,128)(2,1)S(1)}, u32[]{:S(2)}, u32[]{:S(2)}) collective-permute-start(bf16[1,96,768]{2,1,0:T(8,128)(2,1)S(1)} %get-tuple-element.278), channel_id=1, source_target_pairs={{0,16},{4,20},{8,24},{12,28},{16,0},{20,4},{24,8},{28,12},{1,17},{... | collective-permute-start | bytes 442376 | tf_op jit(solution)/shard_map/ppermute | solution.py:253
  357.7 20.4 %collective-permute-start.32 = (bf16[4,96,2432]{2,1,0:T(8,128)(2,1)S(1)}, bf16[4,96,2432]{2,1,0:T(8,128)(2,1)S(1)}, u32[]{:S(2)}, u32[]{:S(2)}) collective-permute-start(bf16[4,96,2432]{2,1,0:T(8,128)(2,1)S(1)} %pad_maximum_fusion.1), channel_id=1, source_target_pairs={{0,4},{4,0},{8,12},{12,8},{16,20},{20,16},{24,28},{28,24},{1,5},{5... | collective-permute-start | bytes 5603336 | tf_op jit(solution)/shard_map/ppermute | solution.py:253
  370.8 20.0 %collective-permute-start.27 = (bf16[512,768]{1,0:T(8,128)(2,1)S(1)}, bf16[512,768]{1,0:T(8,128)(2,1)S(1)}, u32[]{:S(2)}, u32[]{:S(2)}) collective-permute-start(bf16[512,768]{1,0:T(8,128)(2,1)S(1)} %add_convert_fusion.5), channel_id=1, source_target_pairs={{1,0},{2,1},{3,2},{5,4},{6,5},{7,6},{9,8},{10,9},{11,10},{13,12},{... | collective-permute-start | bytes 2359304 | tf_op jit(solution)/shard_map/ppermute | solution.py:258
  372.3 19.9 %collective-permute-start.26 = (bf16[512,768]{1,0:T(8,128)(2,1)S(1)}, bf16[512,768]{1,0:T(8,128)(2,1)S(1)}, u32[]{:S(2)}, u32[]{:S(2)}) collective-permute-start(bf16[512,768]{1,0:T(8,128)(2,1)S(1)} %add_convert_fusion.5), channel_id=1, source_target_pairs={{0,1},{1,2},{2,3},{4,5},{5,6},{6,7},{8,9},{9,10},{10,11},{12,13},{... | collective-permute-start | bytes 2359304 | tf_op jit(solution)/shard_map/ppermute | solution.py:258
  392.2 10.8 %collective-permute-start.35 = (bf16[120,768]{1,0:T(8,128)(2,1)S(1)}, bf16[120,768]{1,0:T(8,128)(2,1)S(1)}, u32[]{:S(2)}, u32[]{:S(2)}) collective-permute-start(bf16[120,768]{1,0:T(8,128)(2,1)S(1)} %broadcast_select_fusion.14), channel_id=1, source_target_pairs={{0,2},{1,3},{2,0},{3,1},{4,6},{5,7},{6,4},{7,5},{8,10},{9,11},{10,... | collective-permute-start | bytes 552968 | tf_op jit(solution)/shard_map/ppermute | solution.py:253
  394.7 38.4 %collective-permute-start.34 = (bf16[512,768]{1,0:T(8,128)(2,1)S(1)}, bf16[512,768]{1,0:T(8,128)(2,1)S(1)}, u32[]{:S(2)}, u32[]{:S(2)}) collective-permute-start(bf16[512,768]{1,0:T(8,128)(2,1)S(1)} %add_convert_fusion.3), channel_id=1, source_target_pairs={{1,0},{2,1},{3,2},{5,4},{6,5},{7,6},{9,8},{10,9},{11,10},{13,12},{... | collective-permute-start | bytes 2359304 | tf_op jit(solution)/shard_map/ppermute | solution.py:258
  396.1 13.7 %collective-permute-start.36 = (bf16[1,96,2432]{2,1,0:T(8,128)(2,1)S(1)}, bf16[1,96,2432]{2,1,0:T(8,128)(2,1)S(1)}, u32[]{:S(2)}, u32[]{:S(2)}) collective-permute-start(bf16[1,96,2432]{2,1,0:T(8,128)(2,1)S(1)} %get-tuple-element.238), channel_id=1, source_target_pairs={{0,8},{4,12},{8,0},{12,4},{16,24},{20,28},{24,16},{28,20},{1,9},{5... | collective-permute-start | bytes 1400840 | tf_op jit(solution)/shard_map/ppermute | solution.py:253
  398.2 18.1 %collective-permute-start.38 = (bf16[1,96,2432]{2,1,0:T(8,128)(2,1)S(1)}, bf16[1,96,2432]{2,1,0:T(8,128)(2,1)S(1)}, u32[]{:S(2)}, u32[]{:S(2)}) collective-permute-start(bf16[1,96,2432]{2,1,0:T(8,128)(2,1)S(1)} %get-tuple-element.239), channel_id=1, source_target_pairs={{0,24},{4,28},{8,16},{12,20},{16,8},{20,12},{24,0},{28,4},{1,25},{... | collective-permute-start | bytes 1400840 | tf_op jit(solution)/shard_map/ppermute | solution.py:253
  398.4 19.2 %collective-permute-start.37 = (bf16[1,96,2432]{2,1,0:T(8,128)(2,1)S(1)}, bf16[1,96,2432]{2,1,0:T(8,128)(2,1)S(1)}, u32[]{:S(2)}, u32[]{:S(2)}) collective-permute-start(bf16[1,96,2432]{2,1,0:T(8,128)(2,1)S(1)} %get-tuple-element.240), channel_id=1, source_target_pairs={{0,16},{4,20},{8,24},{12,28},{16,0},{20,4},{24,8},{28,12},{1,17},{... | collective-permute-start | bytes 1400840 | tf_op jit(solution)/shard_map/ppermute | solution.py:253
  403.0 30.1 %collective-permute-start.33 = (bf16[512,768]{1,0:T(8,128)(2,1)}, bf16[512,768]{1,0:T(8,128)(2,1)S(1)}, u32[]{:S(2)}, u32[]{:S(2)}) collective-permute-start(bf16[512,768]{1,0:T(8,128)(2,1)} %add_convert_fusion.4), channel_id=1, source_target_pairs={{0,1},{1,2},{2,3},{4,5},{5,6},{6,7},{8,9},{9,10},{10,11},{12,13},{... | collective-permute-start | bytes 2359304 | tf_op jit(solution)/shard_map/ppermute | solution.py:258
  435.4 8.4 %collective-permute-start.40 = (bf16[160,768]{1,0:T(8,128)(2,1)S(1)}, bf16[160,768]{1,0:T(8,128)(2,1)S(1)}, u32[]{:S(2)}, u32[]{:S(2)}) collective-permute-start(bf16[160,768]{1,0:T(8,128)(2,1)S(1)} %broadcast_select_fusion.11), channel_id=1, source_target_pairs={{0,1},{1,0},{2,3},{3,2},{4,5},{5,4},{6,7},{7,6},{8,9},{9,8},{10,11... | collective-permute-start | bytes 737288 | tf_op jit(solution)/shard_map/ppermute | solution.py:253
  441.0 12.7 %collective-permute-start.39 = (bf16[216,768]{1,0:T(8,128)(2,1)S(1)}, bf16[216,768]{1,0:T(8,128)(2,1)S(1)}, u32[]{:S(2)}, u32[]{:S(2)}) collective-permute-start(bf16[216,768]{1,0:T(8,128)(2,1)S(1)} %pad_maximum_fusion.13), channel_id=1, source_target_pairs={{0,2},{1,3},{2,0},{3,1},{4,6},{5,7},{6,4},{7,5},{8,10},{9,11},{10,... | collective-permute-start | bytes 995336 | tf_op jit(solution)/shard_map/ppermute | solution.py:253
  453.9 17.0 %collective-permute-start.41 = (bf16[432,768]{1,0:T(8,128)(2,1)S(1)}, bf16[432,768]{1,0:T(8,128)(2,1)S(1)}, u32[]{:S(2)}, u32[]{:S(2)}) collective-permute-start(bf16[432,768]{1,0:T(8,128)(2,1)S(1)} %pad_maximum_fusion.5), channel_id=1, source_target_pairs={{0,1},{1,0},{2,3},{3,2},{4,5},{5,4},{6,7},{7,6},{8,9},{9,8},{10,11... | collective-permute-start | bytes 1990664 | tf_op jit(solution)/shard_map/ppermute | solution.py:253
  454.0 14.7 %collective-permute-start.42 = (bf16[80,768]{1,0:T(8,128)(2,1)S(1)}, bf16[80,768]{1,0:T(8,128)(2,1)S(1)}, u32[]{:S(2)}, u32[]{:S(2)}) collective-permute-start(bf16[80,768]{1,0:T(8,128)(2,1)S(1)} %broadcast_select_fusion.19), channel_id=1, source_target_pairs={{0,2},{1,3},{2,0},{3,1},{4,6},{5,7},{6,4},{7,5},{8,10},{9,11},{10,... | collective-permute-start | bytes 368648 | tf_op jit(solution)/shard_map/ppermute | solution.py:253
  471.2 7.3 %collective-permute-start.43 = (bf16[80,768]{1,0:T(8,128)(2,1)S(1)}, bf16[80,768]{1,0:T(8,128)(2,1)S(1)}, u32[]{:S(2)}, u32[]{:S(2)}) collective-permute-start(bf16[80,768]{1,0:T(8,128)(2,1)S(1)} %add_convert_fusion.13), channel_id=1, source_target_pairs={{0,2},{1,3},{2,0},{3,1},{4,6},{5,7},{6,4},{7,5},{8,10},{9,11},{10,... | collective-permute-start | bytes 368648 | tf_op jit(solution)/shard_map/ppermute | solution.py:253
  478.6 6.3 %collective-permute-start.44 = (bf16[160,768]{1,0:T(8,128)(2,1)S(1)}, bf16[160,768]{1,0:T(8,128)(2,1)S(1)}, u32[]{:S(2)}, u32[]{:S(2)}) collective-permute-start(bf16[160,768]{1,0:T(8,128)(2,1)S(1)} %pad_maximum_fusion.19), channel_id=1, source_target_pairs={{0,1},{1,0},{2,3},{3,2},{4,5},{5,4},{6,7},{7,6},{8,9},{9,8},{10,11... | collective-permute-start | bytes 737288 | tf_op jit(solution)/shard_map/ppermute | solution.py:253
  (96 other events, 1216.3 us)
Sparse Core Ops, SparseCore 0:
  11.0 37.4 all-gather.6
  51.0 63.8 all-gather.8
  116.7 38.9 all-gather.10
  158.0 38.8 all-gather.12
  337.1 38.7 all-gather.14

commit v2 on v1

--- a/solution.py
+++ b/solution.py
@@ -498,7 +498,9 @@
     grad_scores = (probs * (nt(pull, memory) - row_dot)).astype(bf16)
     grad_memory = tn(jnp.concatenate([grad_scores, probs.astype(bf16)], axis=0),
                      jnp.concatenate([probe, pull], axis=0))
-    grad_mixed = jnp.sum(gather_seq(nn(grad_scores, memory).astype(bf16)).astype(f32), axis=0).astype(bf16)
+    joint = gather_seq(jnp.concatenate([nn(grad_scores, memory).astype(bf16), dec_hid, grad_dec_pre], axis=0))
+    heads_rows = head_rows * docs
+    grad_mixed = jnp.sum(joint[:, :heads_rows].astype(f32), axis=0).astype(bf16)
     grad_cross_q = from_heads(nn(grad_mixed, cross_key_full)).astype(bf16)
     back_values = norm_backward(state_one, cross_inv, gain_cross_f, nt(grad_cross_q, cross_query_full))
     grad_one = grad_two + back_values
@@ -507,7 +509,7 @@
     back_values = norm_backward(first, self_inv, gain_self_f, nt(grad_self_vals, self_value_full))
     grad_first = grad_one + back_values
 
-    both = gather_seq(jnp.concatenate([dec_hid, grad_dec_pre])).reshape(seq_count, 2, docs, fsdp, units)
+    both = joint[:, heads_rows:].reshape(seq_count, 2, docs, fsdp, units)
     both = both.transpose(1, 2, 3, 0, 4).reshape(2, docs, fsdp * seq_count * units)
     pack = [self_low, grad_self_vals, self_vals, grad_one_low, cross_low, grad_cross_q, cross_q, grad_cross_ctx,
             cross_ctx, grad_two_low, ffn_low, dec_cot]

time: 499 us -> 494 us (0.990)
  starting transfers between devices: 75.4 us -> 68.3 us
  Pallas kernels: 63.8 us -> 69.6 us
    all_gather x4, waiting for transfers between devices: 25.3 us -> 15.7 us  [body(): lax.all_gather(jnp.concatenate(pieces, axis=1), 'fsdp', axis=0, tiled=True)]
    pallas_call x1, Pallas kernels: 26.4 us -> 32.2 us  [attn_fwd(): pl.pallas_call(fwd_kernel, grid=(pairs,), in_specs=[pl.BlockSpec(memory_s...]
    ppermute x15 -> x12, starting transfers between devices: 23.3 us -> 17.6 us  [gather_seq(): lax.ppermute(values, 'seq', [(n, (n + step) % count) for n in range(count)])]
    ppermute x15 -> x12, waiting for transfers between devices: 12.6 us -> 16.3 us  [gather_seq(): lax.ppermute(values, 'seq', [(n, (n + step) % count) for n in range(count)])]
    unnamed x220 -> x215, local copies, waits for them, and re-layouts: 17.1 us -> 17.1 us
  transfers between devices with their start and end apart: 50 -> 47, of which waited for: 27 -> 26; matrix products, arithmetic and copies ran while one was open for 32% -> 32% of each run, Pallas kernels for 13% -> 14%
where the time goes in v2:
time: 494 us; the launch traced here: 488 us
  waiting for transfers between devices  136 us (28%)
  matrix products  106 us (21%)
  Pallas kernels  69.6 us (14%)
  starting transfers between devices  68.3 us (14%)
  other arithmetic  42.9 us (9%)
  local copies, waits for them, and re-layouts  39.9 us (8%)
  between operations  25.4 us (5%)
    ppermute x22, waiting for transfers between devices, swap(): return lax.ppermute(values, axis, [(n, n ^ bit) for n in range(count)])  66.8 us
    dot_general x17, matrix products, nn(): lax.dot_general(a, b, (((1,), (0,)), ((), ())), preferred_element_type=jn...  38.4 us
    pallas_call x2, Pallas kernels, attn_bwd(): pl.pallas_call(kernel, grid=(count,), in_specs=[pl.BlockSpec(memory_space...  37.4 us
    ppermute x8, waiting for transfers between devices, shift(): lax.ppermute(values, axis, [(n, n + step) for n in range(count) if 0 <= n...  36.6 us
    dot_general x22, matrix products, nt(): lax.dot_general(a, b, (((1,), (1,)), ((), ())), preferred_element_type=jn...  33 us
    pallas_call x1, Pallas kernels, attn_fwd(): pl.pallas_call(fwd_kernel, grid=(pairs,), in_specs=[pl.BlockSpec(memory_s...  32.2 us
    dot_general x15, matrix products, tn(): lax.dot_general(a, b, (((0,), (0,)), ((), ())), preferred_element_type=jn...  31.2 us
    ppermute x22, starting transfers between devices, swap(): return lax.ppermute(values, axis, [(n, n ^ bit) for n in range(count)])  26.4 us
  transfers between devices with their start and end apart: 47, of which 26 were waited for; matrix products, arithmetic and copies ran while one was open for 32% of the time, Pallas kernels for 14%

profile of v2, /device:TPU:0, one launch (start us, length us, event | category | flops | bytes accessed | tf_op | source)
XLA Modules:
  0.0 488.4 jit_solution(15254686418623924681)
XLA Ops:
  12.2 5.6 %collective-permute-start = (bf16[512,768]{1,0:T(8,128)(2,1)}, bf16[512,768]{1,0:T(8,128)(2,1)S(1)}, u32[]{:S(2)}, u32[]{:S(2)}) collective-permute-start(bf16[512,768]{1,0:T(8,128)(2,1)} %param.28), channel_id=1, source_target_pairs={{0,1},{1,2},{2,3},{4,5},{5,6},{6,7},{8,9},{9,10},{10,11},{12,13},{... | collective-permute-start | bytes 2359304 | tf_op jit(solution)/shard_map/ppermute | solution.py:258
  17.9 15.8 %collective-permute-done.1 = bf16[512,768]{1,0:T(8,128)(2,1)S(1)} collective-permute-done((bf16[512,768]{1,0:T(8,128)(2,1)}, bf16[512,768]{1,0:T(8,128)(2,1)S(1)}, u32[]{:S(2)}, u32[]{:S(2)}) %collective-permute-start.1) | collective-permute-done | bytes 786464 | tf_op jit(solution)/shard_map/ppermute | solution.py:258
  45.0 2.4 collective-permute-start.6
  47.3 2.8 collective-permute-start.5
  63.5 5.5 %collective-permute-start.3 = (bf16[512,768]{1,0:T(8,128)(2,1)S(1)}, bf16[512,768]{1,0:T(8,128)(2,1)}, u32[]{:S(2)}, u32[]{:S(2)}) collective-permute-start(bf16[512,768]{1,0:T(8,128)(2,1)S(1)} %collective-permute-done), channel_id=1, source_target_pairs={{0,1},{1,2},{2,3},{4,5},{5,6},{6,7},{8,9},{9,10},{10,11},{12,13},{... | collective-permute-start | bytes 2359304 | tf_op jit(solution)/shard_map/ppermute | solution.py:258
  69.7 2.9 reshape.575
  72.6 2.4 dynamic-slice_reduce_fusion
  77.4 4.0 collective-permute-done.2
  90.6 3.7 fusion.2
  95.9 2.8 convolution_convert_fusion.2.v_ref.refs_4_
  98.8 2.8 convolution_convert_fusion.3.k_ref.refs_3_
  101.7 32.2 %shard_map.407 = (bf16[512,768]{1,0:T(8,128)(2,1)S(1)}, f32[512,768]{1,0:T(8,128)S(1)}) custom-call(s32[3]{0:T(128)S(1)} %add_add_fusion.info.refs_0_, f32[6,2,512]{2,1,0:T(2,128)S(1)} %copy.71.band_ref, bf16[512,768]{1,0:T(8,128)(2,1)S(1)} %convolution_convert_fusion.9.q_ref.refs_2_, bf16[2048,768]{1,0:T(8,128)(2,1)S(1)} %convolution_convert_fusion.3.k_ref.refs_3_, ...), custom_call_target="tpu_custom_call" | custom-call | flops 4026531840 | bytes 9437184 | tf_op jit(solution)/shard_map/pallas_call | solution.py:111
  135.6 2.4 convolution_convert_fusion.16
  140.2 2.4 multiply_reduce_fusion.1
  146.6 7.5 %fusion.13 = f32[512,3072]{1,0:T(8,128)} fusion(bf16[768,6912]{1,0:T(8,128)(2,1)} %all-gather.9.cloned.1.call-done, f32[512,768]{1,0:T(8,128)S(1)} %get-tuple-element.334, f32[768]{0:T(1024)S(1)} %get-tuple-element.194, f32[512]{0:T(512)S(1)} %get-tuple-element.320), kind=kOutput, calls=%fused_computation.23 | convolution fusion | flops 2417098752 | bytes 12588032 | tf_op jit(solution)/shard_map/dot_general | solution.py:27
  155.8 9.5 %fusion.204 = (bf16[512,768]{1,0:T(8,128)(2,1)S(1)}, f32[512,768]{1,0:T(8,128)}) fusion(f32[512,768]{1,0:T(8,128)} %copy-done.34, bf16[3072,768]{1,0:T(8,128)(2,1)} %all-gather.11.cloned.1.call-done, f32[512,3072]{1,0:T(8,128)} %fusion.13), kind=kOutput, calls=%fused_computation.500 | convolution fusion | flops 2430861312 | bytes 14942208 | tf_op jit(solution)/shard_map/dot_general | solution.py:27
  166.3 2.4 collective-permute-start.8
  170.9 7.7 %collective-permute-done.8 = f32[48,896]{1,0:T(8,128)S(1)} collective-permute-done((f32[48,896]{1,0:T(8,128)S(1)}, f32[48,896]{1,0:T(8,128)S(1)}, u32[]{:S(2)}, u32[]{:S(2)}) %collective-permute-start.8) | collective-permute-done | bytes 172064 | tf_op jit(solution)/shard_map/ppermute | solution.py:325
  178.7 3.6 collective-permute-done.9
  182.9 14.1 %all-gather.13.cloned.1.call-done = bf16[768,3072]{1,0:T(8,128)(2,1)} async-done(((bf16[96,3072]{1,0:T(8,128)(2,1)}), bf16[768,3072]{1,0:T(8,128)(2,1)}) %all-gather.13.cloned.1.call-update) | async-done | bytes 4718608 | tf_op jit(solution)/shard_map/all_gather | solution.py:402
  204.7 2.5 collective-permute-start.11
  211.0 3.2 collective-permute-done.12
  219.3 6.4 %convolution_convert_fusion.1 = bf16[3072,768]{1,0:T(8,128)(2,1)S(1)} fusion(f32[512,768]{1,0:T(8,128)S(1)} %convert_add_fusion.2, f32[512,3072]{1,0:T(8,128)} %fusion.13), kind=kOutput, calls=%fused_computation.18 | convolution fusion | flops 2432827392 | bytes 12582912 | tf_op jit(solution)/shard_map/dot_general | solution.py:25
  226.1 9.0 %fusion.9 = bf16[512,3072]{1,0:T(8,128)(2,1)} fusion(f32[512,3072]{1,0:T(8,128)} %fusion.13, bf16[3072,768]{1,0:T(8,128)(2,1)S(1)} %bitcast.314, f32[512,768]{1,0:T(8,128)S(1)} %convert_add_fusion.2), kind=kOutput, calls=%fused_computation.13 | convolution fusion | flops 2446196736 | bytes 15728640 | tf_op jit(solution)/shard_map/dot_general | solution.py:23
  235.1 5.1 %convolution_convert_fusion = bf16[768,3072]{1,0:T(8,128)(2,1)S(1)} fusion(bf16[512,3072]{1,0:T(8,128)(2,1)} %fusion.9, f32[512,768]{1,0:T(8,128)S(1)} %copy-done.35, f32[768]{0:T(1024)S(1)} %copy-done.72, f32[512]{0:T(512)S(1)} %get-tuple-element.320), kind=kOutput, calls=%fused_computation.17 | convolution fusion | flops 2419458048 | bytes 9442304 | tf_op jit(solution)/shard_map/dot_general | solution.py:25
  240.3 2.7 multiply_reduce_fusion
  257.0 3.4 fusion.10
  260.5 2.7 add_convert_fusion
  268.6 18.8 %shard_map.408 = (bf16[512,768]{1,0:T(8,128)(2,1)S(1)}, bf16[2048,768]{1,0:T(8,128)(2,1)S(1)}, bf16[2048,768]{1,0:T(8,128)(2,1)S(1)}, f32[6,2,512]{2,1,0:T(2,128)S(1)}, f32[6,2,256]{2,1,0:T(2,128)S(1)}) custom-call(s32[3]{0:T(128)S(1)} %add_add_fusion.info.refs_0_, f32[6,2,512]{2,1,0:T(2,128)S(1)} %copy.93.band_ref, bf16[512,768]{1,0:T(8,128)(2,1)S(1)} %copy-done.10, ...), custom_call_target="tpu_custom_call" | custom-call | flops 20132659200 | bytes 8650752 | tf_op jit(solution)/shard_map/pallas_call | solution.py:220
  287.5 12.5 %collective-permute-done.22 = bf16[1,96,3840]{2,1,0:T(8,128)(2,1)S(1)} collective-permute-done((bf16[1,96,3840]{2,1,0:T(8,128)(2,1)S(1)}, bf16[1,96,3840]{2,1,0:T(8,128)(2,1)S(1)}, u32[]{:S(2)}, u32[]{:S(2)}) %collective-permute-start.22) | collective-permute-done | bytes 737312 | tf_op jit(solution)/shard_map/ppermute | solution.py:253
  304.4 18.6 %shard_map.409 = (bf16[512,768]{1,0:T(8,128)(2,1)S(1)}, bf16[2048,768]{1,0:T(8,128)(2,1)S(1)}, bf16[2048,768]{1,0:T(8,128)(2,1)S(1)}, f32[6,2,512]{2,1,0:T(2,128)S(1)}, f32[6,2,256]{2,1,0:T(2,128)S(1)}) custom-call(s32[3]{0:T(128)S(1)} %add_add_fusion.info.refs_0_, ...), custom_call_target="tpu_custom_call", output_to_operand_aliasing={{0}: (8, {}), {1}: (9, {}), {2}: (10, {}), {3}: (11, {}), {... | custom-call | flops 20132659200 | bytes 8650752 | tf_op jit(solution)/shard_map/pallas_call | solution.py:220
  325.6 3.1 collective-permute-done.19
  342.5 2.8 convolution_convert_fusion.5
  345.2 2.7 convolution_convert_fusion.4
  362.8 4.6 collective-permute-start.23
  369.1 13.0 %collective-permute-done.24 = bf16[512,768]{1,0:T(8,128)(2,1)S(1)} collective-permute-done((bf16[512,768]{1,0:T(8,128)(2,1)S(1)}, bf16[512,768]{1,0:T(8,128)(2,1)S(1)}, u32[]{:S(2)}, u32[]{:S(2)}) %collective-permute-start.24) | collective-permute-done | bytes 786464 | tf_op jit(solution)/shard_map/ppermute | solution.py:258
  383.5 3.7 collective-permute-start.32
  395.3 2.8 collective-permute-start.30
  398.2 4.4 collective-permute-done.33
  402.6 8.3 %collective-permute-done.35 = bf16[1,96,2432]{2,1,0:T(8,128)(2,1)S(1)} collective-permute-done((bf16[1,96,2432]{2,1,0:T(8,128)(2,1)S(1)}, bf16[1,96,2432]{2,1,0:T(8,128)(2,1)S(1)}, u32[]{:S(2)}, u32[]{:S(2)}) %collective-permute-start.35) | collective-permute-done | bytes 466976 | tf_op jit(solution)/shard_map/ppermute | solution.py:253
  425.4 2.3 fusion.110
  430.0 2.4 collective-permute-start.37
  432.5 2.5 fusion.18
  437.9 10.1 %collective-permute-done.36 = bf16[216,768]{1,0:T(8,128)(2,1)S(1)} collective-permute-done((bf16[216,768]{1,0:T(8,128)(2,1)S(1)}, bf16[216,768]{1,0:T(8,128)(2,1)S(1)}, u32[]{:S(2)}, u32[]{:S(2)}) %collective-permute-start.36) | collective-permute-done | bytes 331808 | tf_op jit(solution)/shard_map/ppermute | solution.py:253
  448.3 2.7 collective-permute-start.39
  451.5 11.8 %collective-permute-done.39 = bf16[80,768]{1,0:T(8,128)(2,1)S(1)} collective-permute-done((bf16[80,768]{1,0:T(8,128)(2,1)S(1)}, bf16[80,768]{1,0:T(8,128)(2,1)S(1)}, u32[]{:S(2)}, u32[]{:S(2)}) %collective-permute-start.39) | collective-permute-done | bytes 122912 | tf_op jit(solution)/shard_map/ppermute | solution.py:253
  469.5 3.5 collective-permute-done.40
  474.5 4.9 %collective-permute-done.41 = bf16[160,768]{1,0:T(8,128)(2,1)S(1)} collective-permute-done((bf16[160,768]{1,0:T(8,128)(2,1)S(1)}, bf16[160,768]{1,0:T(8,128)(2,1)S(1)}, u32[]{:S(2)}, u32[]{:S(2)}) %collective-permute-start.41) | collective-permute-done | bytes 245792 | tf_op jit(solution)/shard_map/ppermute | solution.py:253
  (493 shorter events, 159.9 us)
Async XLA Ops:
  7.3 79.9 %all-gather.7.cloned.1.call-start = ((), (), s32[]{:S(2)}) async-start(), calls=%async_computation | async-start | bytes 4202496 | tf_op jit(solution)/shard_map/all_gather | solution.py:402
  10.9 124.7 %all-gather.9.cloned.1.call-start = ((), (), s32[]{:S(2)}) async-start(), calls=%async_computation.1 | async-start | bytes 11943936 | tf_op jit(solution)/shard_map/all_gather | solution.py:402
  10.9 22.7 %collective-permute-start.1 = (bf16[512,768]{1,0:T(8,128)(2,1)}, bf16[512,768]{1,0:T(8,128)(2,1)S(1)}, u32[]{:S(2)}, u32[]{:S(2)}) collective-permute-start(bf16[512,768]{1,0:T(8,128)(2,1)} %param.28), channel_id=1, source_target_pairs={{1,0},{2,1},{3,2},{5,4},{6,5},{7,6},{9,8},{10,9},{11,10},{13,12},{... | collective-permute-start | bytes 2359304 | tf_op jit(solution)/shard_map/ppermute | solution.py:258
  12.2 22.7 %collective-permute-start = (bf16[512,768]{1,0:T(8,128)(2,1)}, bf16[512,768]{1,0:T(8,128)(2,1)S(1)}, u32[]{:S(2)}, u32[]{:S(2)}) collective-permute-start(bf16[512,768]{1,0:T(8,128)(2,1)} %param.28), channel_id=1, source_target_pairs={{0,1},{1,2},{2,3},{4,5},{5,6},{6,7},{8,9},{9,10},{10,11},{12,13},{... | collective-permute-start | bytes 2359304 | tf_op jit(solution)/shard_map/ppermute | solution.py:258
  41.3 114.5 %all-gather.11.cloned.1.call-start = ((), (), s32[]{:S(2)}) async-start(), calls=%async_computation.2 | async-start | bytes 5308416 | tf_op jit(solution)/shard_map/all_gather | solution.py:402
  42.0 155.0 %all-gather.13.cloned.1.call-start = ((), (), s32[]{:S(2)}) async-start(), calls=%async_computation.3 | async-start | bytes 5308416 | tf_op jit(solution)/shard_map/all_gather | solution.py:402
  45.0 17.2 %collective-permute-start.6 = (bf16[3,768]{1,0:T(4,128)(2,1)S(1)}, bf16[3,768]{1,0:T(4,128)(2,1)S(1)}, u32[]{:S(2)}, u32[]{:S(2)}) collective-permute-start(bf16[3,768]{1,0:T(4,128)(2,1)S(1)} %convolution_convert_fusion.17), channel_id=1, source_target_pairs={{0,1},{1,2},{2,3},{3,0},{4,5},{5,6},{6,7},{7,4},{8,9},{9,10},{10,1... | collective-permute-start | bytes 13832 | tf_op jit(solution)/shard_map/ppermute | solution.py:325
  47.3 14.8 %collective-permute-start.5 = (bf16[3,768]{1,0:T(4,128)(2,1)S(1)}, bf16[3,768]{1,0:T(4,128)(2,1)S(1)}, u32[]{:S(2)}, u32[]{:S(2)}) collective-permute-start(bf16[3,768]{1,0:T(4,128)(2,1)S(1)} %convolution_convert_fusion.17), channel_id=1, source_target_pairs={{0,2},{1,3},{2,0},{3,1},{4,6},{5,7},{6,4},{7,5},{8,10},{9,11},{10,... | collective-permute-start | bytes 13832 | tf_op jit(solution)/shard_map/ppermute | solution.py:325
  50.1 12.0 %collective-permute-start.4 = (bf16[3,768]{1,0:T(4,128)(2,1)S(1)}, bf16[3,768]{1,0:T(4,128)(2,1)S(1)}, u32[]{:S(2)}, u32[]{:S(2)}) collective-permute-start(bf16[3,768]{1,0:T(4,128)(2,1)S(1)} %convolution_convert_fusion.17), channel_id=1, source_target_pairs={{0,3},{1,0},{2,1},{3,2},{4,7},{5,4},{6,5},{7,6},{8,11},{9,8},{10,9... | collective-permute-start | bytes 13832 | tf_op jit(solution)/shard_map/ppermute | solution.py:325
  52.8 117.9 %copy-start.64 = (s32[512]{0:T(512)}, s32[512]{0:T(512)S(1)}, u32[]{:S(2)}) copy-start(s32[512]{0:T(512)S(1)} %select_add_fusion) | copy-start | bytes 6148
  62.2 19.3 %collective-permute-start.2 = (bf16[512,768]{1,0:T(8,128)(2,1)S(1)}, bf16[512,768]{1,0:T(8,128)(2,1)}, u32[]{:S(2)}, u32[]{:S(2)}) collective-permute-start(bf16[512,768]{1,0:T(8,128)(2,1)S(1)} %collective-permute-done.1), channel_id=1, source_target_pairs={{1,0},{2,1},{3,2},{5,4},{6,5},{7,6},{9,8},{10,9},{11,10},{13,12},{... | collective-permute-start | bytes 2359304 | tf_op jit(solution)/shard_map/ppermute | solution.py:258
  63.5 19.1 %collective-permute-start.3 = (bf16[512,768]{1,0:T(8,128)(2,1)S(1)}, bf16[512,768]{1,0:T(8,128)(2,1)}, u32[]{:S(2)}, u32[]{:S(2)}) collective-permute-start(bf16[512,768]{1,0:T(8,128)(2,1)S(1)} %collective-permute-done), channel_id=1, source_target_pairs={{0,1},{1,2},{2,3},{4,5},{5,6},{6,7},{8,9},{9,10},{10,11},{12,13},{... | collective-permute-start | bytes 2359304 | tf_op jit(solution)/shard_map/ppermute | solution.py:258
  77.1 335.4 %all-gather.15.cloned.1.call-start = ((), (), s32[]{:S(2)}) async-start(), calls=%async_computation.4 | async-start | bytes 3538944 | tf_op jit(solution)/shard_map/all_gather | solution.py:544
  166.3 12.3 %collective-permute-start.8 = (f32[48,896]{1,0:T(8,128)S(1)}, f32[48,896]{1,0:T(8,128)S(1)}, u32[]{:S(2)}, u32[]{:S(2)}) collective-permute-start(f32[48,896]{1,0:T(8,128)S(1)} %get-tuple-element.299), channel_id=1, source_target_pairs={{0,2},{1,3},{2,0},{3,1},{4,6},{5,7},{6,4},{7,5},{8,10},{9,11},{10,... | collective-permute-start | bytes 516104 | tf_op jit(solution)/shard_map/ppermute | solution.py:325
  168.7 9.9 %collective-permute-start.7 = (f32[48,896]{1,0:T(8,128)S(1)}, f32[48,896]{1,0:T(8,128)S(1)}, u32[]{:S(2)}, u32[]{:S(2)}) collective-permute-start(f32[48,896]{1,0:T(8,128)S(1)} %get-tuple-element.299), channel_id=1, source_target_pairs={{0,3},{1,0},{2,1},{3,2},{4,7},{5,4},{6,5},{7,6},{8,11},{9,8},{10,9... | collective-permute-start | bytes 516104 | tf_op jit(solution)/shard_map/ppermute | solution.py:325
  170.2 12.0 %collective-permute-start.9 = (f32[48,896]{1,0:T(8,128)S(1)}, f32[48,896]{1,0:T(8,128)S(1)}, u32[]{:S(2)}, u32[]{:S(2)}) collective-permute-start(f32[48,896]{1,0:T(8,128)S(1)} %get-tuple-element.299), channel_id=1, source_target_pairs={{0,1},{1,2},{2,3},{3,0},{4,5},{5,6},{6,7},{7,4},{8,9},{9,10},{10,1... | collective-permute-start | bytes 516104 | tf_op jit(solution)/shard_map/ppermute | solution.py:325
  204.7 4.8 collective-permute-start.11
  207.1 3.8 collective-permute-start.10
  208.6 5.6 %collective-permute-start.12 = (f32[6,768]{1,0:T(8,128)S(1)}, f32[6,768]{1,0:T(8,128)S(1)}, u32[]{:S(2)}, u32[]{:S(2)}) collective-permute-start(f32[6,768]{1,0:T(8,128)S(1)} %get-tuple-element.312), channel_id=1, source_target_pairs={{0,1},{1,2},{2,3},{3,0},{4,5},{5,6},{6,7},{7,4},{8,9},{9,10},{10,1... | collective-permute-start | bytes 55304 | tf_op jit(solution)/shard_map/ppermute | solution.py:325
  216.7 35.9 %collective-permute-start.16 = (bf16[54,768]{1,0:T(8,128)(2,1)S(1)}, bf16[54,768]{1,0:T(8,128)(2,1)S(1)}, u32[]{:S(2)}, u32[]{:S(2)}) collective-permute-start(bf16[54,768]{1,0:T(8,128)(2,1)S(1)} %get-tuple-element.301), channel_id=1, source_target_pairs={{0,2},{1,3},{2,0},{3,1},{4,6},{5,7},{6,4},{7,5},{8,10},{9,11},{10,... | collective-permute-start | bytes 248840 | tf_op jit(solution)/shard_map/ppermute | solution.py:325
  216.8 35.9 %collective-permute-start.15 = (bf16[54,768]{1,0:T(8,128)(2,1)S(1)}, bf16[54,768]{1,0:T(8,128)(2,1)S(1)}, u32[]{:S(2)}, u32[]{:S(2)}) collective-permute-start(bf16[54,768]{1,0:T(8,128)(2,1)S(1)} %get-tuple-element.301), channel_id=1, source_target_pairs={{0,3},{1,0},{2,1},{3,2},{4,7},{5,4},{6,5},{7,6},{8,11},{9,8},{10,9... | collective-permute-start | bytes 248840 | tf_op jit(solution)/shard_map/ppermute | solution.py:325
  217.9 34.7 %collective-permute-start.17 = (bf16[54,768]{1,0:T(8,128)(2,1)S(1)}, bf16[54,768]{1,0:T(8,128)(2,1)S(1)}, u32[]{:S(2)}, u32[]{:S(2)}) collective-permute-start(bf16[54,768]{1,0:T(8,128)(2,1)S(1)} %get-tuple-element.301), channel_id=1, source_target_pairs={{0,1},{1,2},{2,3},{3,0},{4,5},{5,6},{6,7},{7,4},{8,9},{9,10},{10,1... | collective-permute-start | bytes 248840 | tf_op jit(solution)/shard_map/ppermute | solution.py:325
  245.8 11.2 %collective-permute-start.14 = (bf16[4,96,3072]{2,1,0:T(8,128)(2,1)}, bf16[4,96,3072]{2,1,0:T(8,128)(2,1)}, u32[]{:S(2)}, u32[]{:S(2)}) collective-permute-start(bf16[4,96,3072]{2,1,0:T(8,128)(2,1)} %dynamic-slice_bitcast_fusion), channel_id=1, source_target_pairs={{0,4},{4,0},{8,12},{12,8},{16,20},{20,16},{24,28},{28,24},{1,5},{5... | collective-permute-start | bytes 7077896 | tf_op jit(solution)/shard_map/ppermute | solution.py:253
  250.4 10.0 %collective-permute-start.13 = (bf16[4,96,3840]{2,1,0:T(8,128)(2,1)}, bf16[4,96,3840]{2,1,0:T(8,128)(2,1)}, u32[]{:S(2)}, u32[]{:S(2)}) collective-permute-start(bf16[4,96,3840]{2,1,0:T(8,128)(2,1)} %get-tuple-element.248), channel_id=1, source_target_pairs={{0,4},{4,0},{8,12},{12,8},{16,20},{20,16},{24,28},{28,24},{1,5},{5... | collective-permute-start | bytes 8847368 | tf_op jit(solution)/shard_map/ppermute | solution.py:253
  263.4 38.3 %collective-permute-start.18 = (bf16[4,96,1536]{2,1,0:T(8,128)(2,1)S(1)}, bf16[4,96,1536]{2,1,0:T(8,128)(2,1)S(1)}, u32[]{:S(2)}, u32[]{:S(2)}) collective-permute-start(bf16[4,96,1536]{2,1,0:T(8,128)(2,1)S(1)} %broadcast_select_fusion), channel_id=1, source_target_pairs={{0,1},{1,0},{2,3},{3,2},{4,5},{5,4},{6,7},{7,6},{8,9},{9,8},{10,11... | collective-permute-start | bytes 3538952 | tf_op jit(solution)/shard_map/ppermute | solution.py:253
  265.0 22.4 %collective-permute-start.20 = (bf16[1,96,3840]{2,1,0:T(8,128)(2,1)S(1)}, bf16[1,96,3840]{2,1,0:T(8,128)(2,1)S(1)}, u32[]{:S(2)}, u32[]{:S(2)}) collective-permute-start(bf16[1,96,3840]{2,1,0:T(8,128)(2,1)S(1)} %get-tuple-element.235), channel_id=1, source_target_pairs={{0,8},{4,12},{8,0},{12,4},{16,24},{20,28},{24,16},{28,20},{1,9},{5... | collective-permute-start | bytes 2211848 | tf_op jit(solution)/shard_map/ppermute | solution.py:253
  266.6 33.4 %collective-permute-start.22 = (bf16[1,96,3840]{2,1,0:T(8,128)(2,1)S(1)}, bf16[1,96,3840]{2,1,0:T(8,128)(2,1)S(1)}, u32[]{:S(2)}, u32[]{:S(2)}) collective-permute-start(bf16[1,96,3840]{2,1,0:T(8,128)(2,1)S(1)} %get-tuple-element.236), channel_id=1, source_target_pairs={{0,24},{4,28},{8,16},{12,20},{16,8},{20,12},{24,0},{28,4},{1,25},{... | collective-permute-start | bytes 2211848 | tf_op jit(solution)/shard_map/ppermute | solution.py:253
  267.9 33.5 %collective-permute-start.21 = (bf16[1,96,3840]{2,1,0:T(8,128)(2,1)S(1)}, bf16[1,96,3840]{2,1,0:T(8,128)(2,1)S(1)}, u32[]{:S(2)}, u32[]{:S(2)}) collective-permute-start(bf16[1,96,3840]{2,1,0:T(8,128)(2,1)S(1)} %get-tuple-element.237), channel_id=1, source_target_pairs={{0,16},{4,20},{8,24},{12,28},{16,0},{20,4},{24,8},{28,12},{1,17},{... | collective-permute-start | bytes 2211848 | tf_op jit(solution)/shard_map/ppermute | solution.py:253
  302.3 26.4 %collective-permute-start.19 = (bf16[4,96,768]{2,1,0:T(8,128)(2,1)S(1)}, bf16[4,96,768]{2,1,0:T(8,128)(2,1)S(1)}, u32[]{:S(2)}, u32[]{:S(2)}) collective-permute-start(bf16[4,96,768]{2,1,0:T(8,128)(2,1)S(1)} %broadcast_select_fusion.3), channel_id=1, source_target_pairs={{0,2},{1,3},{2,0},{3,1},{4,6},{5,7},{6,4},{7,5},{8,10},{9,11},{10,... | collective-permute-start | bytes 1769480 | tf_op jit(solution)/shard_map/ppermute | solution.py:253
  335.4 33.0 %collective-permute-start.25 = (bf16[240,768]{1,0:T(8,128)(2,1)S(1)}, bf16[240,768]{1,0:T(8,128)(2,1)S(1)}, u32[]{:S(2)}, u32[]{:S(2)}) collective-permute-start(bf16[240,768]{1,0:T(8,128)(2,1)S(1)} %broadcast_select_fusion.6), channel_id=1, source_target_pairs={{0,1},{1,0},{2,3},{3,2},{4,5},{5,4},{6,7},{7,6},{8,9},{9,8},{10,11... | collective-permute-start | bytes 1105928 | tf_op jit(solution)/shard_map/ppermute | solution.py:253
  336.9 24.4 %collective-permute-start.26 = (bf16[1,96,768]{2,1,0:T(8,128)(2,1)S(1)}, bf16[1,96,768]{2,1,0:T(8,128)(2,1)S(1)}, u32[]{:S(2)}, u32[]{:S(2)}) collective-permute-start(bf16[1,96,768]{2,1,0:T(8,128)(2,1)S(1)} %get-tuple-element.276), channel_id=1, source_target_pairs={{0,8},{4,12},{8,0},{12,4},{16,24},{20,28},{24,16},{28,20},{1,9},{5... | collective-permute-start | bytes 442376 | tf_op jit(solution)/shard_map/ppermute | solution.py:253
  337.6 25.2 %collective-permute-start.28 = (bf16[1,96,768]{2,1,0:T(8,128)(2,1)S(1)}, bf16[1,96,768]{2,1,0:T(8,128)(2,1)S(1)}, u32[]{:S(2)}, u32[]{:S(2)}) collective-permute-start(bf16[1,96,768]{2,1,0:T(8,128)(2,1)S(1)} %get-tuple-element.277), channel_id=1, source_target_pairs={{0,24},{4,28},{8,16},{12,20},{16,8},{20,12},{24,0},{28,4},{1,25},{... | collective-permute-start | bytes 442376 | tf_op jit(solution)/shard_map/ppermute | solution.py:253
  339.1 28.3 %collective-permute-start.27 = (bf16[1,96,768]{2,1,0:T(8,128)(2,1)S(1)}, bf16[1,96,768]{2,1,0:T(8,128)(2,1)S(1)}, u32[]{:S(2)}, u32[]{:S(2)}) collective-permute-start(bf16[1,96,768]{2,1,0:T(8,128)(2,1)S(1)} %get-tuple-element.278), channel_id=1, source_target_pairs={{0,16},{4,20},{8,24},{12,28},{16,0},{20,4},{24,8},{28,12},{1,17},{... | collective-permute-start | bytes 442376 | tf_op jit(solution)/shard_map/ppermute | solution.py:253
  348.3 20.3 %collective-permute-start.29 = (bf16[4,96,2432]{2,1,0:T(8,128)(2,1)S(1)}, bf16[4,96,2432]{2,1,0:T(8,128)(2,1)S(1)}, u32[]{:S(2)}, u32[]{:S(2)}) collective-permute-start(bf16[4,96,2432]{2,1,0:T(8,128)(2,1)S(1)} %pad_maximum_fusion.1), channel_id=1, source_target_pairs={{0,4},{4,0},{8,12},{12,8},{16,20},{20,16},{24,28},{28,24},{1,5},{5... | collective-permute-start | bytes 5603336 | tf_op jit(solution)/shard_map/ppermute | solution.py:253
  361.3 20.8 %collective-permute-start.24 = (bf16[512,768]{1,0:T(8,128)(2,1)S(1)}, bf16[512,768]{1,0:T(8,128)(2,1)S(1)}, u32[]{:S(2)}, u32[]{:S(2)}) collective-permute-start(bf16[512,768]{1,0:T(8,128)(2,1)S(1)} %add_convert_fusion.5), channel_id=1, source_target_pairs={{1,0},{2,1},{3,2},{5,4},{6,5},{7,6},{9,8},{10,9},{11,10},{13,12},{... | collective-permute-start | bytes 2359304 | tf_op jit(solution)/shard_map/ppermute | solution.py:258
  362.8 20.7 %collective-permute-start.23 = (bf16[512,768]{1,0:T(8,128)(2,1)S(1)}, bf16[512,768]{1,0:T(8,128)(2,1)S(1)}, u32[]{:S(2)}, u32[]{:S(2)}) collective-permute-start(bf16[512,768]{1,0:T(8,128)(2,1)S(1)} %add_convert_fusion.5), channel_id=1, source_target_pairs={{0,1},{1,2},{2,3},{4,5},{5,6},{6,7},{8,9},{9,10},{10,11},{12,13},{... | collective-permute-start | bytes 2359304 | tf_op jit(solution)/shard_map/ppermute | solution.py:258
  383.5 11.8 %collective-permute-start.32 = (bf16[120,768]{1,0:T(8,128)(2,1)S(1)}, bf16[120,768]{1,0:T(8,128)(2,1)S(1)}, u32[]{:S(2)}, u32[]{:S(2)}) collective-permute-start(bf16[120,768]{1,0:T(8,128)(2,1)S(1)} %broadcast_select_fusion.14), channel_id=1, source_target_pairs={{0,2},{1,3},{2,0},{3,1},{4,6},{5,7},{6,4},{7,5},{8,10},{9,11},{10,... | collective-permute-start | bytes 552968 | tf_op jit(solution)/shard_map/ppermute | solution.py:253
  387.4 40.2 %collective-permute-start.31 = (bf16[512,768]{1,0:T(8,128)(2,1)S(1)}, bf16[512,768]{1,0:T(8,128)(2,1)S(1)}, u32[]{:S(2)}, u32[]{:S(2)}) collective-permute-start(bf16[512,768]{1,0:T(8,128)(2,1)S(1)} %add_convert_fusion.3), channel_id=1, source_target_pairs={{1,0},{2,1},{3,2},{5,4},{6,5},{7,6},{9,8},{10,9},{11,10},{13,12},{... | collective-permute-start | bytes 2359304 | tf_op jit(solution)/shard_map/ppermute | solution.py:258
  388.9 13.7 %collective-permute-start.33 = (bf16[1,96,2432]{2,1,0:T(8,128)(2,1)S(1)}, bf16[1,96,2432]{2,1,0:T(8,128)(2,1)S(1)}, u32[]{:S(2)}, u32[]{:S(2)}) collective-permute-start(bf16[1,96,2432]{2,1,0:T(8,128)(2,1)S(1)} %get-tuple-element.238), channel_id=1, source_target_pairs={{0,8},{4,12},{8,0},{12,4},{16,24},{20,28},{24,16},{28,20},{1,9},{5... | collective-permute-start | bytes 1400840 | tf_op jit(solution)/shard_map/ppermute | solution.py:253
  389.6 21.2 %collective-permute-start.35 = (bf16[1,96,2432]{2,1,0:T(8,128)(2,1)S(1)}, bf16[1,96,2432]{2,1,0:T(8,128)(2,1)S(1)}, u32[]{:S(2)}, u32[]{:S(2)}) collective-permute-start(bf16[1,96,2432]{2,1,0:T(8,128)(2,1)S(1)} %get-tuple-element.239), channel_id=1, source_target_pairs={{0,24},{4,28},{8,16},{12,20},{16,8},{20,12},{24,0},{28,4},{1,25},{... | collective-permute-start | bytes 1400840 | tf_op jit(solution)/shard_map/ppermute | solution.py:253
  391.9 20.4 %collective-permute-start.34 = (bf16[1,96,2432]{2,1,0:T(8,128)(2,1)S(1)}, bf16[1,96,2432]{2,1,0:T(8,128)(2,1)S(1)}, u32[]{:S(2)}, u32[]{:S(2)}) collective-permute-start(bf16[1,96,2432]{2,1,0:T(8,128)(2,1)S(1)} %get-tuple-element.240), channel_id=1, source_target_pairs={{0,16},{4,20},{8,24},{12,28},{16,0},{20,4},{24,8},{28,12},{1,17},{... | collective-permute-start | bytes 1400840 | tf_op jit(solution)/shard_map/ppermute | solution.py:253
  395.3 32.4 %collective-permute-start.30 = (bf16[512,768]{1,0:T(8,128)(2,1)}, bf16[512,768]{1,0:T(8,128)(2,1)S(1)}, u32[]{:S(2)}, u32[]{:S(2)}) collective-permute-start(bf16[512,768]{1,0:T(8,128)(2,1)} %add_convert_fusion.4), channel_id=1, source_target_pairs={{0,1},{1,2},{2,3},{4,5},{5,6},{6,7},{8,9},{9,10},{10,11},{12,13},{... | collective-permute-start | bytes 2359304 | tf_op jit(solution)/shard_map/ppermute | solution.py:258
  430.0 7.8 %collective-permute-start.37 = (bf16[160,768]{1,0:T(8,128)(2,1)S(1)}, bf16[160,768]{1,0:T(8,128)(2,1)S(1)}, u32[]{:S(2)}, u32[]{:S(2)}) collective-permute-start(bf16[160,768]{1,0:T(8,128)(2,1)S(1)} %broadcast_select_fusion.11), channel_id=1, source_target_pairs={{0,1},{1,0},{2,3},{3,2},{4,5},{5,4},{6,7},{7,6},{8,9},{9,8},{10,11... | collective-permute-start | bytes 737288 | tf_op jit(solution)/shard_map/ppermute | solution.py:253
  435.0 13.0 %collective-permute-start.36 = (bf16[216,768]{1,0:T(8,128)(2,1)S(1)}, bf16[216,768]{1,0:T(8,128)(2,1)S(1)}, u32[]{:S(2)}, u32[]{:S(2)}) collective-permute-start(bf16[216,768]{1,0:T(8,128)(2,1)S(1)} %pad_maximum_fusion.15), channel_id=1, source_target_pairs={{0,2},{1,3},{2,0},{3,1},{4,6},{5,7},{6,4},{7,5},{8,10},{9,11},{10,... | collective-permute-start | bytes 995336 | tf_op jit(solution)/shard_map/ppermute | solution.py:253
  448.2 17.3 %collective-permute-start.38 = (bf16[432,768]{1,0:T(8,128)(2,1)S(1)}, bf16[432,768]{1,0:T(8,128)(2,1)S(1)}, u32[]{:S(2)}, u32[]{:S(2)}) collective-permute-start(bf16[432,768]{1,0:T(8,128)(2,1)S(1)} %pad_maximum_fusion.5), channel_id=1, source_target_pairs={{0,1},{1,0},{2,3},{3,2},{4,5},{5,4},{6,7},{7,6},{8,9},{9,8},{10,11... | collective-permute-start | bytes 1990664 | tf_op jit(solution)/shard_map/ppermute | solution.py:253
  448.3 15.0 %collective-permute-start.39 = (bf16[80,768]{1,0:T(8,128)(2,1)S(1)}, bf16[80,768]{1,0:T(8,128)(2,1)S(1)}, u32[]{:S(2)}, u32[]{:S(2)}) collective-permute-start(bf16[80,768]{1,0:T(8,128)(2,1)S(1)} %broadcast_select_fusion.19), channel_id=1, source_target_pairs={{0,2},{1,3},{2,0},{3,1},{4,6},{5,7},{6,4},{7,5},{8,10},{9,11},{10,... | collective-permute-start | bytes 368648 | tf_op jit(solution)/shard_map/ppermute | solution.py:253
  465.8 7.3 %collective-permute-start.40 = (bf16[80,768]{1,0:T(8,128)(2,1)S(1)}, bf16[80,768]{1,0:T(8,128)(2,1)S(1)}, u32[]{:S(2)}, u32[]{:S(2)}) collective-permute-start(bf16[80,768]{1,0:T(8,128)(2,1)S(1)} %add_convert_fusion.13), channel_id=1, source_target_pairs={{0,2},{1,3},{2,0},{3,1},{4,6},{5,7},{6,4},{7,5},{8,10},{9,11},{10,... | collective-permute-start | bytes 368648 | tf_op jit(solution)/shard_map/ppermute | solution.py:253
  473.1 6.3 %collective-permute-start.41 = (bf16[160,768]{1,0:T(8,128)(2,1)S(1)}, bf16[160,768]{1,0:T(8,128)(2,1)S(1)}, u32[]{:S(2)}, u32[]{:S(2)}) collective-permute-start(bf16[160,768]{1,0:T(8,128)(2,1)S(1)} %pad_maximum_fusion.20), channel_id=1, source_target_pairs={{0,1},{1,0},{2,3},{3,2},{4,5},{5,4},{6,7},{7,6},{8,9},{9,8},{10,11... | collective-permute-start | bytes 737288 | tf_op jit(solution)/shard_map/ppermute | solution.py:253
  (90 other events, 1014.0 us)
Sparse Core Ops, SparseCore 0:
  11.0 37.4 all-gather.6
  51.0 63.8 all-gather.8
  116.7 38.9 all-gather.10
  158.1 38.8 all-gather.12
  330.6 38.3 all-gather.14

commit v3 on v2

--- a/solution.py
+++ b/solution.py
@@ -533,14 +533,10 @@
     band, early, across, pack = lax.optimization_barrier((make_band(table, -1), early, across, pack))
     early = scatter_chips(early)
     seq_bits = bits_of("seq")
-    grads = None
     pairs = HEADS // 2
-    for call, bit in enumerate(seq_bits):
-        across_next = halve_seq(across, bit, 2)
-        first, count = call * pairs // len(seq_bits), (call + 1) * pairs // len(seq_bits) - call * pairs // len(seq_bits)
-        grads = attn_bwd(info, band, query, key, value, grad_context, context, lse, first, count, grads)
-        band, across, grads = lax.optimization_barrier((band, across_next, grads))
-    grads, early, pack = lax.optimization_barrier((grads, early, pack))
+    across = halve_seq(across, seq_bits[0], 2)
+    grads = attn_bwd(info, band, query, key, value, grad_context, context, lse, 0, pairs, None)
+    grads, early, across, pack = lax.optimization_barrier((grads, early, across, pack))
     packs = lax.all_gather(pack, "fsdp", axis=0)
     stack = lambda shard: jnp.concatenate(
         [shard[:, n * width : (n + 1) * width] for n in range(shard.shape[1] // width)], axis=0)
@@ -557,7 +553,8 @@
     signs = (1, -1)
     moving = [shift(term(sign * reach).astype(bf16), "seq", sign) for sign in signs]
     early = halve_seq(stack(early), seq_bits[0], 0)
-    across = scatter_chips(across)
+    for bit in seq_bits[1:]:
+        across = halve_seq(across, bit, 2)
     late = [tn(normed, grad_query), tn(normed_all, grad_key), tn(normed_all, grad_value)]
     late = [piece.astype(bf16).reshape(fsdp, part, width) for piece in late]
     grad_table = table_grad(grad_band, grad_far).reshape(fsdp, 1, buckets_part).astype(bf16)
@@ -569,7 +566,7 @@
         moving = [shift(add_low(one, come), "seq", sign) for one, come, sign in zip(terms, moving, signs)]
     for bit in seq_bits[1:]:
         early = halve_seq(early, bit, 0)
-    late = scatter_chips(late)
+    late, across = scatter_chips(late), scatter_chips(across)
     rowset = lambda n: packs[:, n * tile : (n + 1) * tile].reshape(fsdp * tile, width)
     mine = lambda values: lax.dynamic_slice_in_dim(values, own * part, part, 1)
     at = 12
@@ -588,7 +585,7 @@
         tn(mine(rowset(10)), pre_all),
         tn(lax.dynamic_slice_in_dim(hid_all, own * part_ff, part_ff, 1), rowset(11)),
     ]
-    moving, early, late, dec_shards = lax.optimization_barrier((moving, early, late, dec_shards))
+    moving, early, across, late, dec_shards = lax.optimization_barrier((moving, early, across, late, dec_shards))
     shard_self_value, shard_self_out, shard_cross_query, shard_cross_key = dec_shards[:4]
     shard_cross_value, shard_cross_out, shard_dff_in, shard_dff_out = dec_shards[4:]
     table_rows = jnp.pad(late[:1, 3 * width :], ((0, 31), (0, width - 128)))

time: 494 us -> 497 us (level)
  starting transfers between devices: 68.3 us -> 92.3 us
  waiting for transfers between devices: 136 us -> 114 us
    ppermute x8, waiting for transfers between devices: 36.6 us -> 22.2 us  [shift(): lax.ppermute(values, axis, [(n, n + step) for n in range(count) if 0 <= n...]
    ppermute x22, starting transfers between devices: 26.4 us -> 40.5 us  [swap(): return lax.ppermute(values, axis, [(n, n ^ bit) for n in range(count)])]
    ppermute x8, starting transfers between devices: 23.8 us -> 33.7 us  [shift(): lax.ppermute(values, axis, [(n, n + step) for n in range(count) if 0 <= n...]
    ppermute x22, waiting for transfers between devices: 66.8 us -> 59.1 us  [swap(): return lax.ppermute(values, axis, [(n, n ^ bit) for n in range(count)])]
    unnamed x215 -> x255, local copies, waits for them, and re-layouts: 17.1 us -> 16.4 us
    pallas_call x2 -> x1, Pallas kernels: 37.4 us -> 37.1 us  [attn_bwd(): pl.pallas_call(kernel, grid=(count,), in_specs=[pl.BlockSpec(memory_space...]
  transfers between devices with their start and end apart: 47 -> 47, of which waited for: 26 -> 21; matrix products, arithmetic and copies ran while one was open for 32% -> 31% of each run, Pallas kernels for 14% -> 14%
where the time goes in v3:
time: 497 us; the launch traced here: 494 us
  waiting for transfers between devices  114 us (23%)
  matrix products  109 us (22%)
  starting transfers between devices  92.3 us (19%)
  Pallas kernels  69.3 us (14%)
  other arithmetic  45.7 us (9%)
  local copies, waits for them, and re-layouts  38 us (8%)
  between operations  25.6 us (5%)
    ppermute x22, waiting for transfers between devices, swap(): return lax.ppermute(values, axis, [(n, n ^ bit) for n in range(count)])  59.1 us
    ppermute x22, starting transfers between devices, swap(): return lax.ppermute(values, axis, [(n, n ^ bit) for n in range(count)])  40.5 us
    dot_general x17, matrix products, nn(): lax.dot_general(a, b, (((1,), (0,)), ((), ())), preferred_element_type=jn...  37.9 us
    pallas_call x1, Pallas kernels, attn_bwd(): pl.pallas_call(kernel, grid=(count,), in_specs=[pl.BlockSpec(memory_space...  37.1 us
    dot_general x22, matrix products, nt(): lax.dot_general(a, b, (((1,), (1,)), ((), ())), preferred_element_type=jn...  34 us
    ppermute x8, starting transfers between devices, shift(): lax.ppermute(values, axis, [(n, n + step) for n in range(count) if 0 <= n...  33.7 us
    dot_general x15, matrix products, tn(): lax.dot_general(a, b, (((0,), (0,)), ((), ())), preferred_element_type=jn...  33.2 us
    pallas_call x1, Pallas kernels, attn_fwd(): pl.pallas_call(fwd_kernel, grid=(pairs,), in_specs=[pl.BlockSpec(memory_s...  32.2 us
  transfers between devices with their start and end apart: 47, of which 21 were waited for; matrix products, arithmetic and copies ran while one was open for 31% of the time, Pallas kernels for 14%

profile of v3, /device:TPU:0, one launch (start us, length us, event | category | flops | bytes accessed | tf_op | source)
XLA Modules:
  0.0 493.5 jit_solution(10984708248344899777)
XLA Ops:
  12.2 5.6 %collective-permute-start = (bf16[512,768]{1,0:T(8,128)(2,1)}, bf16[512,768]{1,0:T(8,128)(2,1)S(1)}, u32[]{:S(2)}, u32[]{:S(2)}) collective-permute-start(bf16[512,768]{1,0:T(8,128)(2,1)} %param.28), channel_id=1, source_target_pairs={{0,1},{1,2},{2,3},{4,5},{5,6},{6,7},{8,9},{9,10},{10,11},{12,13},{... | collective-permute-start | bytes 2359304 | tf_op jit(solution)/shard_map/ppermute | solution.py:258
  17.9 15.8 %collective-permute-done.1 = bf16[512,768]{1,0:T(8,128)(2,1)S(1)} collective-permute-done((bf16[512,768]{1,0:T(8,128)(2,1)}, bf16[512,768]{1,0:T(8,128)(2,1)S(1)}, u32[]{:S(2)}, u32[]{:S(2)}) %collective-permute-start.1) | collective-permute-done | bytes 786464 | tf_op jit(solution)/shard_map/ppermute | solution.py:258
  45.0 2.4 collective-permute-start.6
  47.3 2.8 collective-permute-start.5
  63.6 5.5 %collective-permute-start.3 = (bf16[512,768]{1,0:T(8,128)(2,1)S(1)}, bf16[512,768]{1,0:T(8,128)(2,1)}, u32[]{:S(2)}, u32[]{:S(2)}) collective-permute-start(bf16[512,768]{1,0:T(8,128)(2,1)S(1)} %collective-permute-done), channel_id=1, source_target_pairs={{0,1},{1,2},{2,3},{4,5},{5,6},{6,7},{8,9},{9,10},{10,11},{12,13},{... | collective-permute-start | bytes 2359304 | tf_op jit(solution)/shard_map/ppermute | solution.py:258
  69.7 2.9 reshape.575
  72.7 2.4 dynamic-slice_reduce_fusion
  77.5 4.0 collective-permute-done.2
  90.7 3.7 fusion.2
  96.0 2.8 convolution_convert_fusion.2.v_ref
  98.9 2.8 convolution_convert_fusion.3.k_ref
  101.7 32.2 %shard_map.407 = (bf16[512,768]{1,0:T(8,128)(2,1)S(1)}, f32[512,768]{1,0:T(8,128)S(1)}) custom-call(s32[3]{0:T(128)S(1)} %add_add_fusion.info, f32[6,2,512]{2,1,0:T(2,128)S(1)} %copy.65.band_ref, bf16[512,768]{1,0:T(8,128)(2,1)S(1)} %convolution_convert_fusion.9.q_ref, bf16[2048,768]{1,0:T(8,128)(2,1)S(1)} %convolution_convert_fusion.3.k_ref, ...), custom_call_target="tpu_custom_call" | custom-call | flops 4026531840 | bytes 9437184 | tf_op jit(solution)/shard_map/pallas_call | solution.py:111
  135.7 2.4 convolution_convert_fusion.16
  140.3 2.4 multiply_reduce_fusion.1
  146.8 7.5 %fusion.13 = f32[512,3072]{1,0:T(8,128)} fusion(bf16[768,6912]{1,0:T(8,128)(2,1)} %all-gather.9.cloned.1.call-done, f32[512,768]{1,0:T(8,128)S(1)} %get-tuple-element.302, f32[768]{0:T(1024)S(1)} %get-tuple-element.162, f32[512]{0:T(512)S(1)} %get-tuple-element.288), kind=kOutput, calls=%fused_computation.23 | convolution fusion | flops 2417098752 | bytes 12588032 | tf_op jit(solution)/shard_map/dot_general | solution.py:27
  155.7 9.5 %fusion.204 = (bf16[512,768]{1,0:T(8,128)(2,1)S(1)}, f32[512,768]{1,0:T(8,128)}) fusion(f32[512,768]{1,0:T(8,128)} %copy-done.36, bf16[3072,768]{1,0:T(8,128)(2,1)} %all-gather.11.cloned.1.call-done, f32[512,3072]{1,0:T(8,128)} %fusion.13), kind=kOutput, calls=%fused_computation.500 | convolution fusion | flops 2430861312 | bytes 14942208 | tf_op jit(solution)/shard_map/dot_general | solution.py:27
  166.3 2.5 collective-permute-start.8
  170.9 7.7 %collective-permute-done.8 = f32[48,896]{1,0:T(8,128)S(1)} collective-permute-done((f32[48,896]{1,0:T(8,128)S(1)}, f32[48,896]{1,0:T(8,128)S(1)}, u32[]{:S(2)}, u32[]{:S(2)}) %collective-permute-start.8) | collective-permute-done | bytes 172064 | tf_op jit(solution)/shard_map/ppermute | solution.py:325
  178.6 3.6 collective-permute-done.9
  182.9 14.1 %all-gather.13.cloned.1.call-done = bf16[768,3072]{1,0:T(8,128)(2,1)} async-done(((bf16[96,3072]{1,0:T(8,128)(2,1)}), bf16[768,3072]{1,0:T(8,128)(2,1)}) %all-gather.13.cloned.1.call-update) | async-done | bytes 4718608 | tf_op jit(solution)/shard_map/all_gather | solution.py:402
  204.8 2.5 collective-permute-start.11
  211.1 3.2 collective-permute-done.12
  219.4 6.3 %convolution_convert_fusion.1 = bf16[3072,768]{1,0:T(8,128)(2,1)S(1)} fusion(f32[512,768]{1,0:T(8,128)S(1)} %convert_add_fusion.2, f32[512,3072]{1,0:T(8,128)} %fusion.13), kind=kOutput, calls=%fused_computation.18 | convolution fusion | flops 2432827392 | bytes 12582912 | tf_op jit(solution)/shard_map/dot_general | solution.py:25
  226.2 9.0 %fusion.9 = bf16[512,3072]{1,0:T(8,128)(2,1)} fusion(f32[512,3072]{1,0:T(8,128)} %fusion.13, bf16[3072,768]{1,0:T(8,128)(2,1)S(1)} %bitcast.314, f32[512,768]{1,0:T(8,128)S(1)} %convert_add_fusion.2), kind=kOutput, calls=%fused_computation.13 | convolution fusion | flops 2446196736 | bytes 15728640 | tf_op jit(solution)/shard_map/dot_general | solution.py:23
  235.2 5.1 %convolution_convert_fusion = bf16[768,3072]{1,0:T(8,128)(2,1)S(1)} fusion(bf16[512,3072]{1,0:T(8,128)(2,1)} %fusion.9, f32[512,768]{1,0:T(8,128)S(1)} %copy-done.37, f32[768]{0:T(1024)S(1)} %copy-done.92, f32[512]{0:T(512)S(1)} %copy-done.82), kind=kOutput, calls=%fused_computation.17 | convolution fusion | flops 2419458048 | bytes 9442304 | tf_op jit(solution)/shard_map/dot_general | solution.py:25
  240.4 2.7 multiply_reduce_fusion
  257.9 3.4 fusion.10
  261.4 2.7 add_convert_fusion
  269.5 37.1 %shard_map.408 = (bf16[512,768]{1,0:T(8,128)(2,1)S(1)}, bf16[2048,768]{1,0:T(8,128)(2,1)S(1)}, bf16[2048,768]{1,0:T(8,128)(2,1)S(1)}, f32[6,2,512]{2,1,0:T(2,128)S(1)}, f32[6,2,256]{2,1,0:T(2,128)S(1)}) custom-call(s32[3]{0:T(128)S(1)} %add_add_fusion.info, f32[6,2,512]{2,1,0:T(2,128)S(1)} %copy.87.band_ref, bf16[512,768]{1,0:T(8,128)(2,1)S(1)} %copy-done.10, ...), custom_call_target="tpu_custom_call" | custom-call | flops 40265318400 | bytes 17301504 | tf_op jit(solution)/shard_map/pallas_call | solution.py:220
  310.3 3.7 convolution_convert_fusion.5
  314.1 3.7 convolution_convert_fusion.4
  321.6 5.5 %collective-permute-start.22 = (bf16[512,768]{1,0:T(8,128)(2,1)}, bf16[512,768]{1,0:T(8,128)(2,1)}, u32[]{:S(2)}, u32[]{:S(2)}) collective-permute-start(bf16[512,768]{1,0:T(8,128)(2,1)} %add_convert_fusion.5), channel_id=1, source_target_pairs={{0,1},{1,2},{2,3},{4,5},{5,6},{6,7},{8,9},{9,10},{10,11},{12,13},{... | collective-permute-start | bytes 2359304 | tf_op jit(solution)/shard_map/ppermute | solution.py:258
  347.7 10.2 %collective-permute-done.24 = bf16[240,768]{1,0:T(8,128)(2,1)S(1)} collective-permute-done((bf16[240,768]{1,0:T(8,128)(2,1)S(1)}, bf16[240,768]{1,0:T(8,128)(2,1)S(1)}, u32[]{:S(2)}, u32[]{:S(2)}) %collective-permute-start.24) | collective-permute-done | bytes 368672 | tf_op jit(solution)/shard_map/ppermute | solution.py:253
  358.1 8.4 %collective-permute-done.25 = bf16[4,96,768]{2,1,0:T(8,128)(2,1)S(1)} collective-permute-done((bf16[4,96,768]{2,1,0:T(8,128)(2,1)S(1)}, bf16[4,96,768]{2,1,0:T(8,128)(2,1)S(1)}, u32[]{:S(2)}, u32[]{:S(2)}) %collective-permute-start.25) | collective-permute-done | bytes 589856 | tf_op jit(solution)/shard_map/ppermute | solution.py:253
  367.5 20.6 %collective-permute-start.32 = (bf16[1,96,768]{2,1,0:T(8,128)(2,1)S(1)}, bf16[1,96,768]{2,1,0:T(8,128)(2,1)S(1)}, u32[]{:S(2)}, u32[]{:S(2)}) collective-permute-start(bf16[1,96,768]{2,1,0:T(8,128)(2,1)S(1)} %get-tuple-element.245), channel_id=1, source_target_pairs={{0,24},{4,28},{8,16},{12,20},{16,8},{20,12},{24,0},{28,4},{1,25},{... | collective-permute-start | bytes 442376 | tf_op jit(solution)/shard_map/ppermute | solution.py:253
  390.9 2.2 add_convert_fusion.4
  393.7 2.9 collective-permute-start.35
  396.7 12.0 %collective-permute-start.27 = (bf16[512,768]{1,0:T(8,128)(2,1)}, bf16[512,768]{1,0:T(8,128)(2,1)S(1)}, u32[]{:S(2)}, u32[]{:S(2)}) collective-permute-start(bf16[512,768]{1,0:T(8,128)(2,1)} %add_convert_fusion.4), channel_id=1, source_target_pairs={{0,1},{1,2},{2,3},{4,5},{5,6},{6,7},{8,9},{9,10},{10,11},{12,13},{... | collective-permute-start | bytes 2359304 | tf_op jit(solution)/shard_map/ppermute | solution.py:258
  408.8 6.0 %collective-permute-done.35 = bf16[1,96,2432]{2,1,0:T(8,128)(2,1)S(1)} collective-permute-done((bf16[1,96,2432]{2,1,0:T(8,128)(2,1)S(1)}, bf16[1,96,2432]{2,1,0:T(8,128)(2,1)S(1)}, u32[]{:S(2)}, u32[]{:S(2)}) %collective-permute-start.35) | collective-permute-done | bytes 466976 | tf_op jit(solution)/shard_map/ppermute | solution.py:253
  429.4 2.3 fusion.110
  434.0 8.0 %collective-permute-start.37 = (bf16[160,768]{1,0:T(8,128)(2,1)S(1)}, bf16[160,768]{1,0:T(8,128)(2,1)S(1)}, u32[]{:S(2)}, u32[]{:S(2)}) collective-permute-start(bf16[160,768]{1,0:T(8,128)(2,1)S(1)} %broadcast_select_fusion.11), channel_id=1, source_target_pairs={{0,1},{1,0},{2,3},{3,2},{4,5},{5,4},{6,7},{7,6},{8,9},{9,8},{10,11... | collective-permute-start | bytes 737288 | tf_op jit(solution)/shard_map/ppermute | solution.py:253
  442.0 2.5 fusion.18
  444.9 4.3 collective-permute-done.37
  449.3 8.0 %collective-permute-done.36 = bf16[216,768]{1,0:T(8,128)(2,1)S(1)} collective-permute-done((bf16[216,768]{1,0:T(8,128)(2,1)S(1)}, bf16[216,768]{1,0:T(8,128)(2,1)S(1)}, u32[]{:S(2)}, u32[]{:S(2)}) %collective-permute-start.36) | collective-permute-done | bytes 331808 | tf_op jit(solution)/shard_map/ppermute | solution.py:253
  459.0 9.9 %collective-permute-done.39 = bf16[80,768]{1,0:T(8,128)(2,1)S(1)} collective-permute-done((bf16[80,768]{1,0:T(8,128)(2,1)S(1)}, bf16[80,768]{1,0:T(8,128)(2,1)S(1)}, u32[]{:S(2)}, u32[]{:S(2)}) %collective-permute-start.39) | collective-permute-done | bytes 122912 | tf_op jit(solution)/shard_map/ppermute | solution.py:253
  468.9 2.8 collective-permute-done.38
  475.1 3.1 collective-permute-done.40
  479.6 4.9 collective-permute-done.41
  (531 shorter events, 142.1 us)
Async XLA Ops:
  7.3 79.9 %all-gather.7.cloned.1.call-start = ((), (), s32[]{:S(2)}) async-start(), calls=%async_computation | async-start | bytes 4202496 | tf_op jit(solution)/shard_map/all_gather | solution.py:402
  10.9 124.8 %all-gather.9.cloned.1.call-start = ((), (), s32[]{:S(2)}) async-start(), calls=%async_computation.1 | async-start | bytes 11943936 | tf_op jit(solution)/shard_map/all_gather | solution.py:402
  10.9 22.7 %collective-permute-start.1 = (bf16[512,768]{1,0:T(8,128)(2,1)}, bf16[512,768]{1,0:T(8,128)(2,1)S(1)}, u32[]{:S(2)}, u32[]{:S(2)}) collective-permute-start(bf16[512,768]{1,0:T(8,128)(2,1)} %param.28), channel_id=1, source_target_pairs={{1,0},{2,1},{3,2},{5,4},{6,5},{7,6},{9,8},{10,9},{11,10},{13,12},{... | collective-permute-start | bytes 2359304 | tf_op jit(solution)/shard_map/ppermute | solution.py:258
  12.2 22.7 %collective-permute-start = (bf16[512,768]{1,0:T(8,128)(2,1)}, bf16[512,768]{1,0:T(8,128)(2,1)S(1)}, u32[]{:S(2)}, u32[]{:S(2)}) collective-permute-start(bf16[512,768]{1,0:T(8,128)(2,1)} %param.28), channel_id=1, source_target_pairs={{0,1},{1,2},{2,3},{4,5},{5,6},{6,7},{8,9},{9,10},{10,11},{12,13},{... | collective-permute-start | bytes 2359304 | tf_op jit(solution)/shard_map/ppermute | solution.py:258
  41.3 114.5 %all-gather.11.cloned.1.call-start = ((), (), s32[]{:S(2)}) async-start(), calls=%async_computation.2 | async-start | bytes 5308416 | tf_op jit(solution)/shard_map/all_gather | solution.py:402
  42.0 155.0 %all-gather.13.cloned.1.call-start = ((), (), s32[]{:S(2)}) async-start(), calls=%async_computation.3 | async-start | bytes 5308416 | tf_op jit(solution)/shard_map/all_gather | solution.py:402
  45.0 17.2 %collective-permute-start.6 = (bf16[3,768]{1,0:T(4,128)(2,1)S(1)}, bf16[3,768]{1,0:T(4,128)(2,1)S(1)}, u32[]{:S(2)}, u32[]{:S(2)}) collective-permute-start(bf16[3,768]{1,0:T(4,128)(2,1)S(1)} %convolution_convert_fusion.17), channel_id=1, source_target_pairs={{0,1},{1,2},{2,3},{3,0},{4,5},{5,6},{6,7},{7,4},{8,9},{9,10},{10,1... | collective-permute-start | bytes 13832 | tf_op jit(solution)/shard_map/ppermute | solution.py:325
  47.3 14.9 %collective-permute-start.5 = (bf16[3,768]{1,0:T(4,128)(2,1)S(1)}, bf16[3,768]{1,0:T(4,128)(2,1)S(1)}, u32[]{:S(2)}, u32[]{:S(2)}) collective-permute-start(bf16[3,768]{1,0:T(4,128)(2,1)S(1)} %convolution_convert_fusion.17), channel_id=1, source_target_pairs={{0,2},{1,3},{2,0},{3,1},{4,6},{5,7},{6,4},{7,5},{8,10},{9,11},{10,... | collective-permute-start | bytes 13832 | tf_op jit(solution)/shard_map/ppermute | solution.py:325
  50.1 12.1 %collective-permute-start.4 = (bf16[3,768]{1,0:T(4,128)(2,1)S(1)}, bf16[3,768]{1,0:T(4,128)(2,1)S(1)}, u32[]{:S(2)}, u32[]{:S(2)}) collective-permute-start(bf16[3,768]{1,0:T(4,128)(2,1)S(1)} %convolution_convert_fusion.17), channel_id=1, source_target_pairs={{0,3},{1,0},{2,1},{3,2},{4,7},{5,4},{6,5},{7,6},{8,11},{9,8},{10,9... | collective-permute-start | bytes 13832 | tf_op jit(solution)/shard_map/ppermute | solution.py:325
  52.8 118.0 %copy-start.84 = (s32[512]{0:T(512)}, s32[512]{0:T(512)S(1)}, u32[]{:S(2)}) copy-start(s32[512]{0:T(512)S(1)} %select_add_fusion) | copy-start | bytes 6148
  62.3 19.3 %collective-permute-start.2 = (bf16[512,768]{1,0:T(8,128)(2,1)S(1)}, bf16[512,768]{1,0:T(8,128)(2,1)}, u32[]{:S(2)}, u32[]{:S(2)}) collective-permute-start(bf16[512,768]{1,0:T(8,128)(2,1)S(1)} %collective-permute-done.1), channel_id=1, source_target_pairs={{1,0},{2,1},{3,2},{5,4},{6,5},{7,6},{9,8},{10,9},{11,10},{13,12},{... | collective-permute-start | bytes 2359304 | tf_op jit(solution)/shard_map/ppermute | solution.py:258
  63.6 19.0 %collective-permute-start.3 = (bf16[512,768]{1,0:T(8,128)(2,1)S(1)}, bf16[512,768]{1,0:T(8,128)(2,1)}, u32[]{:S(2)}, u32[]{:S(2)}) collective-permute-start(bf16[512,768]{1,0:T(8,128)(2,1)S(1)} %collective-permute-done), channel_id=1, source_target_pairs={{0,1},{1,2},{2,3},{4,5},{5,6},{6,7},{8,9},{9,10},{10,11},{12,13},{... | collective-permute-start | bytes 2359304 | tf_op jit(solution)/shard_map/ppermute | solution.py:258
  77.2 339.4 %all-gather.15.cloned.1.call-start = ((), (), s32[]{:S(2)}) async-start(), calls=%async_computation.4 | async-start | bytes 3538944 | tf_op jit(solution)/shard_map/all_gather | solution.py:540
  166.3 12.3 %collective-permute-start.8 = (f32[48,896]{1,0:T(8,128)S(1)}, f32[48,896]{1,0:T(8,128)S(1)}, u32[]{:S(2)}, u32[]{:S(2)}) collective-permute-start(f32[48,896]{1,0:T(8,128)S(1)} %get-tuple-element.267), channel_id=1, source_target_pairs={{0,2},{1,3},{2,0},{3,1},{4,6},{5,7},{6,4},{7,5},{8,10},{9,11},{10,... | collective-permute-start | bytes 516104 | tf_op jit(solution)/shard_map/ppermute | solution.py:325
  168.8 9.8 %collective-permute-start.7 = (f32[48,896]{1,0:T(8,128)S(1)}, f32[48,896]{1,0:T(8,128)S(1)}, u32[]{:S(2)}, u32[]{:S(2)}) collective-permute-start(f32[48,896]{1,0:T(8,128)S(1)} %get-tuple-element.267), channel_id=1, source_target_pairs={{0,3},{1,0},{2,1},{3,2},{4,7},{5,4},{6,5},{7,6},{8,11},{9,8},{10,9... | collective-permute-start | bytes 516104 | tf_op jit(solution)/shard_map/ppermute | solution.py:325
  170.2 12.0 %collective-permute-start.9 = (f32[48,896]{1,0:T(8,128)S(1)}, f32[48,896]{1,0:T(8,128)S(1)}, u32[]{:S(2)}, u32[]{:S(2)}) collective-permute-start(f32[48,896]{1,0:T(8,128)S(1)} %get-tuple-element.267), channel_id=1, source_target_pairs={{0,1},{1,2},{2,3},{3,0},{4,5},{5,6},{6,7},{7,4},{8,9},{9,10},{10,1... | collective-permute-start | bytes 516104 | tf_op jit(solution)/shard_map/ppermute | solution.py:325
  204.8 4.8 collective-permute-start.11
  207.2 3.8 collective-permute-start.10
  208.7 5.6 %collective-permute-start.12 = (f32[6,768]{1,0:T(8,128)S(1)}, f32[6,768]{1,0:T(8,128)S(1)}, u32[]{:S(2)}, u32[]{:S(2)}) collective-permute-start(f32[6,768]{1,0:T(8,128)S(1)} %get-tuple-element.280), channel_id=1, source_target_pairs={{0,1},{1,2},{2,3},{3,0},{4,5},{5,6},{6,7},{7,4},{8,9},{9,10},{10,1... | collective-permute-start | bytes 55304 | tf_op jit(solution)/shard_map/ppermute | solution.py:325
  216.8 36.0 %collective-permute-start.16 = (bf16[54,768]{1,0:T(8,128)(2,1)S(1)}, bf16[54,768]{1,0:T(8,128)(2,1)S(1)}, u32[]{:S(2)}, u32[]{:S(2)}) collective-permute-start(bf16[54,768]{1,0:T(8,128)(2,1)S(1)} %get-tuple-element.269), channel_id=1, source_target_pairs={{0,2},{1,3},{2,0},{3,1},{4,6},{5,7},{6,4},{7,5},{8,10},{9,11},{10,... | collective-permute-start | bytes 248840 | tf_op jit(solution)/shard_map/ppermute | solution.py:325
  216.9 36.0 %collective-permute-start.15 = (bf16[54,768]{1,0:T(8,128)(2,1)S(1)}, bf16[54,768]{1,0:T(8,128)(2,1)S(1)}, u32[]{:S(2)}, u32[]{:S(2)}) collective-permute-start(bf16[54,768]{1,0:T(8,128)(2,1)S(1)} %get-tuple-element.269), channel_id=1, source_target_pairs={{0,3},{1,0},{2,1},{3,2},{4,7},{5,4},{6,5},{7,6},{8,11},{9,8},{10,9... | collective-permute-start | bytes 248840 | tf_op jit(solution)/shard_map/ppermute | solution.py:325
  218.0 34.8 %collective-permute-start.17 = (bf16[54,768]{1,0:T(8,128)(2,1)S(1)}, bf16[54,768]{1,0:T(8,128)(2,1)S(1)}, u32[]{:S(2)}, u32[]{:S(2)}) collective-permute-start(bf16[54,768]{1,0:T(8,128)(2,1)S(1)} %get-tuple-element.269), channel_id=1, source_target_pairs={{0,1},{1,2},{2,3},{3,0},{4,5},{5,6},{6,7},{7,4},{8,9},{9,10},{10,1... | collective-permute-start | bytes 248840 | tf_op jit(solution)/shard_map/ppermute | solution.py:325
  246.0 11.9 %collective-permute-start.14 = (bf16[4,96,3072]{2,1,0:T(8,128)(2,1)}, bf16[4,96,3072]{2,1,0:T(8,128)(2,1)}, u32[]{:S(2)}, u32[]{:S(2)}) collective-permute-start(bf16[4,96,3072]{2,1,0:T(8,128)(2,1)} %dynamic-slice_bitcast_fusion), channel_id=1, source_target_pairs={{0,4},{4,0},{8,12},{12,8},{16,20},{20,16},{24,28},{28,24},{1,5},{5... | collective-permute-start | bytes 7077896 | tf_op jit(solution)/shard_map/ppermute | solution.py:253
  250.6 10.7 %collective-permute-start.13 = (bf16[4,96,3840]{2,1,0:T(8,128)(2,1)}, bf16[4,96,3840]{2,1,0:T(8,128)(2,1)}, u32[]{:S(2)}, u32[]{:S(2)}) collective-permute-start(bf16[4,96,3840]{2,1,0:T(8,128)(2,1)} %get-tuple-element.216), channel_id=1, source_target_pairs={{0,4},{4,0},{8,12},{12,8},{16,20},{20,16},{24,28},{28,24},{1,5},{5... | collective-permute-start | bytes 8847368 | tf_op jit(solution)/shard_map/ppermute | solution.py:253
  264.3 42.8 %collective-permute-start.21 = (bf16[4,96,1536]{2,1,0:T(8,128)(2,1)S(1)}, bf16[4,96,1536]{2,1,0:T(8,128)(2,1)S(1)}, u32[]{:S(2)}, u32[]{:S(2)}) collective-permute-start(bf16[4,96,1536]{2,1,0:T(8,128)(2,1)S(1)} %broadcast_select_fusion), channel_id=1, source_target_pairs={{0,1},{1,0},{2,3},{3,2},{4,5},{5,4},{6,7},{7,6},{8,9},{9,8},{10,11... | collective-permute-start | bytes 3538952 | tf_op jit(solution)/shard_map/ppermute | solution.py:253
  265.9 40.7 %collective-permute-start.18 = (bf16[1,96,3840]{2,1,0:T(8,128)(2,1)S(1)}, bf16[1,96,3840]{2,1,0:T(8,128)(2,1)S(1)}, u32[]{:S(2)}, u32[]{:S(2)}) collective-permute-start(bf16[1,96,3840]{2,1,0:T(8,128)(2,1)S(1)} %get-tuple-element.203), channel_id=1, source_target_pairs={{0,8},{4,12},{8,0},{12,4},{16,24},{20,28},{24,16},{28,20},{1,9},{5... | collective-permute-start | bytes 2211848 | tf_op jit(solution)/shard_map/ppermute | solution.py:253
  267.4 39.2 %collective-permute-start.20 = (bf16[1,96,3840]{2,1,0:T(8,128)(2,1)S(1)}, bf16[1,96,3840]{2,1,0:T(8,128)(2,1)S(1)}, u32[]{:S(2)}, u32[]{:S(2)}) collective-permute-start(bf16[1,96,3840]{2,1,0:T(8,128)(2,1)S(1)} %get-tuple-element.204), channel_id=1, source_target_pairs={{0,24},{4,28},{8,16},{12,20},{16,8},{20,12},{24,0},{28,4},{1,25},{... | collective-permute-start | bytes 2211848 | tf_op jit(solution)/shard_map/ppermute | solution.py:253
  268.7 37.9 %collective-permute-start.19 = (bf16[1,96,3840]{2,1,0:T(8,128)(2,1)S(1)}, bf16[1,96,3840]{2,1,0:T(8,128)(2,1)S(1)}, u32[]{:S(2)}, u32[]{:S(2)}) collective-permute-start(bf16[1,96,3840]{2,1,0:T(8,128)(2,1)S(1)} %get-tuple-element.205), channel_id=1, source_target_pairs={{0,16},{4,20},{8,24},{12,28},{16,0},{20,4},{24,8},{28,12},{1,17},{... | collective-permute-start | bytes 2211848 | tf_op jit(solution)/shard_map/ppermute | solution.py:253
  320.4 46.9 %collective-permute-start.23 = (bf16[512,768]{1,0:T(8,128)(2,1)}, bf16[512,768]{1,0:T(8,128)(2,1)}, u32[]{:S(2)}, u32[]{:S(2)}) collective-permute-start(bf16[512,768]{1,0:T(8,128)(2,1)} %add_convert_fusion.5), channel_id=1, source_target_pairs={{1,0},{2,1},{3,2},{5,4},{6,5},{7,6},{9,8},{10,9},{11,10},{13,12},{... | collective-permute-start | bytes 2359304 | tf_op jit(solution)/shard_map/ppermute | solution.py:258
  321.6 45.6 %collective-permute-start.22 = (bf16[512,768]{1,0:T(8,128)(2,1)}, bf16[512,768]{1,0:T(8,128)(2,1)}, u32[]{:S(2)}, u32[]{:S(2)}) collective-permute-start(bf16[512,768]{1,0:T(8,128)(2,1)} %add_convert_fusion.5), channel_id=1, source_target_pairs={{0,1},{1,2},{2,3},{4,5},{5,6},{6,7},{8,9},{9,10},{10,11},{12,13},{... | collective-permute-start | bytes 2359304 | tf_op jit(solution)/shard_map/ppermute | solution.py:258
  332.9 25.1 %collective-permute-start.24 = (bf16[240,768]{1,0:T(8,128)(2,1)S(1)}, bf16[240,768]{1,0:T(8,128)(2,1)S(1)}, u32[]{:S(2)}, u32[]{:S(2)}) collective-permute-start(bf16[240,768]{1,0:T(8,128)(2,1)S(1)} %broadcast_select_fusion.6), channel_id=1, source_target_pairs={{0,1},{1,0},{2,3},{3,2},{4,5},{5,4},{6,7},{7,6},{8,9},{9,8},{10,11... | collective-permute-start | bytes 1105928 | tf_op jit(solution)/shard_map/ppermute | solution.py:253
  333.1 33.5 %collective-permute-start.25 = (bf16[4,96,768]{2,1,0:T(8,128)(2,1)S(1)}, bf16[4,96,768]{2,1,0:T(8,128)(2,1)S(1)}, u32[]{:S(2)}, u32[]{:S(2)}) collective-permute-start(bf16[4,96,768]{2,1,0:T(8,128)(2,1)S(1)} %broadcast_select_fusion.3), channel_id=1, source_target_pairs={{0,2},{1,3},{2,0},{3,1},{4,6},{5,7},{6,4},{7,5},{8,10},{9,11},{10,... | collective-permute-start | bytes 1769480 | tf_op jit(solution)/shard_map/ppermute | solution.py:253
  336.4 30.4 %collective-permute-start.26 = (bf16[4,96,2432]{2,1,0:T(8,128)(2,1)S(1)}, bf16[4,96,2432]{2,1,0:T(8,128)(2,1)S(1)}, u32[]{:S(2)}, u32[]{:S(2)}) collective-permute-start(bf16[4,96,2432]{2,1,0:T(8,128)(2,1)S(1)} %pad_maximum_fusion.1), channel_id=1, source_target_pairs={{0,4},{4,0},{8,12},{12,8},{16,20},{20,16},{24,28},{28,24},{1,5},{5... | collective-permute-start | bytes 5603336 | tf_op jit(solution)/shard_map/ppermute | solution.py:253
  367.3 29.4 %collective-permute-start.29 = (bf16[120,768]{1,0:T(8,128)(2,1)S(1)}, bf16[120,768]{1,0:T(8,128)(2,1)S(1)}, u32[]{:S(2)}, u32[]{:S(2)}) collective-permute-start(bf16[120,768]{1,0:T(8,128)(2,1)S(1)} %broadcast_select_fusion.14), channel_id=1, source_target_pairs={{0,2},{1,3},{2,0},{3,1},{4,6},{5,7},{6,4},{7,5},{8,10},{9,11},{10,... | collective-permute-start | bytes 552968 | tf_op jit(solution)/shard_map/ppermute | solution.py:253
  367.5 25.7 %collective-permute-start.30 = (bf16[1,96,768]{2,1,0:T(8,128)(2,1)S(1)}, bf16[1,96,768]{2,1,0:T(8,128)(2,1)S(1)}, u32[]{:S(2)}, u32[]{:S(2)}) collective-permute-start(bf16[1,96,768]{2,1,0:T(8,128)(2,1)S(1)} %get-tuple-element.244), channel_id=1, source_target_pairs={{0,8},{4,12},{8,0},{12,4},{16,24},{20,28},{24,16},{28,20},{1,9},{5... | collective-permute-start | bytes 442376 | tf_op jit(solution)/shard_map/ppermute | solution.py:253
  367.5 26.2 %collective-permute-start.32 = (bf16[1,96,768]{2,1,0:T(8,128)(2,1)S(1)}, bf16[1,96,768]{2,1,0:T(8,128)(2,1)S(1)}, u32[]{:S(2)}, u32[]{:S(2)}) collective-permute-start(bf16[1,96,768]{2,1,0:T(8,128)(2,1)S(1)} %get-tuple-element.245), channel_id=1, source_target_pairs={{0,24},{4,28},{8,16},{12,20},{16,8},{20,12},{24,0},{28,4},{1,25},{... | collective-permute-start | bytes 442376 | tf_op jit(solution)/shard_map/ppermute | solution.py:253
  388.2 8.5 %collective-permute-start.31 = (bf16[1,96,768]{2,1,0:T(8,128)(2,1)S(1)}, bf16[1,96,768]{2,1,0:T(8,128)(2,1)S(1)}, u32[]{:S(2)}, u32[]{:S(2)}) collective-permute-start(bf16[1,96,768]{2,1,0:T(8,128)(2,1)S(1)} %get-tuple-element.246), channel_id=1, source_target_pairs={{0,16},{4,20},{8,24},{12,28},{16,0},{20,4},{24,8},{28,12},{1,17},{... | collective-permute-start | bytes 442376 | tf_op jit(solution)/shard_map/ppermute | solution.py:253
  389.5 42.2 %collective-permute-start.28 = (bf16[512,768]{1,0:T(8,128)(2,1)S(1)}, bf16[512,768]{1,0:T(8,128)(2,1)S(1)}, u32[]{:S(2)}, u32[]{:S(2)}) collective-permute-start(bf16[512,768]{1,0:T(8,128)(2,1)S(1)} %add_convert_fusion.3), channel_id=1, source_target_pairs={{1,0},{2,1},{3,2},{5,4},{6,5},{7,6},{9,8},{10,9},{11,10},{13,12},{... | collective-permute-start | bytes 2359304 | tf_op jit(solution)/shard_map/ppermute | solution.py:258
  393.1 15.7 %collective-permute-start.33 = (bf16[1,96,2432]{2,1,0:T(8,128)(2,1)S(1)}, bf16[1,96,2432]{2,1,0:T(8,128)(2,1)S(1)}, u32[]{:S(2)}, u32[]{:S(2)}) collective-permute-start(bf16[1,96,2432]{2,1,0:T(8,128)(2,1)S(1)} %get-tuple-element.206), channel_id=1, source_target_pairs={{0,8},{4,12},{8,0},{12,4},{16,24},{20,28},{24,16},{28,20},{1,9},{5... | collective-permute-start | bytes 1400840 | tf_op jit(solution)/shard_map/ppermute | solution.py:253
  393.7 21.1 %collective-permute-start.35 = (bf16[1,96,2432]{2,1,0:T(8,128)(2,1)S(1)}, bf16[1,96,2432]{2,1,0:T(8,128)(2,1)S(1)}, u32[]{:S(2)}, u32[]{:S(2)}) collective-permute-start(bf16[1,96,2432]{2,1,0:T(8,128)(2,1)S(1)} %get-tuple-element.207), channel_id=1, source_target_pairs={{0,24},{4,28},{8,16},{12,20},{16,8},{20,12},{24,0},{28,4},{1,25},{... | collective-permute-start | bytes 1400840 | tf_op jit(solution)/shard_map/ppermute | solution.py:253
  396.6 19.6 %collective-permute-start.34 = (bf16[1,96,2432]{2,1,0:T(8,128)(2,1)S(1)}, bf16[1,96,2432]{2,1,0:T(8,128)(2,1)S(1)}, u32[]{:S(2)}, u32[]{:S(2)}) collective-permute-start(bf16[1,96,2432]{2,1,0:T(8,128)(2,1)S(1)} %get-tuple-element.208), channel_id=1, source_target_pairs={{0,16},{4,20},{8,24},{12,28},{16,0},{20,4},{24,8},{28,12},{1,17},{... | collective-permute-start | bytes 1400840 | tf_op jit(solution)/shard_map/ppermute | solution.py:253
  396.7 34.9 %collective-permute-start.27 = (bf16[512,768]{1,0:T(8,128)(2,1)}, bf16[512,768]{1,0:T(8,128)(2,1)S(1)}, u32[]{:S(2)}, u32[]{:S(2)}) collective-permute-start(bf16[512,768]{1,0:T(8,128)(2,1)} %add_convert_fusion.4), channel_id=1, source_target_pairs={{0,1},{1,2},{2,3},{4,5},{5,6},{6,7},{8,9},{9,10},{10,11},{12,13},{... | collective-permute-start | bytes 2359304 | tf_op jit(solution)/shard_map/ppermute | solution.py:258
  434.0 15.2 %collective-permute-start.37 = (bf16[160,768]{1,0:T(8,128)(2,1)S(1)}, bf16[160,768]{1,0:T(8,128)(2,1)S(1)}, u32[]{:S(2)}, u32[]{:S(2)}) collective-permute-start(bf16[160,768]{1,0:T(8,128)(2,1)S(1)} %broadcast_select_fusion.11), channel_id=1, source_target_pairs={{0,1},{1,0},{2,3},{3,2},{4,5},{5,4},{6,7},{7,6},{8,9},{9,8},{10,11... | collective-permute-start | bytes 737288 | tf_op jit(solution)/shard_map/ppermute | solution.py:253
  444.5 12.8 %collective-permute-start.36 = (bf16[216,768]{1,0:T(8,128)(2,1)S(1)}, bf16[216,768]{1,0:T(8,128)(2,1)S(1)}, u32[]{:S(2)}, u32[]{:S(2)}) collective-permute-start(bf16[216,768]{1,0:T(8,128)(2,1)S(1)} %pad_maximum_fusion.15), channel_id=1, source_target_pairs={{0,2},{1,3},{2,0},{3,1},{4,6},{5,7},{6,4},{7,5},{8,10},{9,11},{10,... | collective-permute-start | bytes 995336 | tf_op jit(solution)/shard_map/ppermute | solution.py:253
  457.5 14.2 %collective-permute-start.38 = (bf16[432,768]{1,0:T(8,128)(2,1)S(1)}, bf16[432,768]{1,0:T(8,128)(2,1)S(1)}, u32[]{:S(2)}, u32[]{:S(2)}) collective-permute-start(bf16[432,768]{1,0:T(8,128)(2,1)S(1)} %pad_maximum_fusion.5), channel_id=1, source_target_pairs={{0,1},{1,0},{2,3},{3,2},{4,5},{5,4},{6,7},{7,6},{8,9},{9,8},{10,11... | collective-permute-start | bytes 1990664 | tf_op jit(solution)/shard_map/ppermute | solution.py:253
  457.6 11.2 %collective-permute-start.39 = (bf16[80,768]{1,0:T(8,128)(2,1)S(1)}, bf16[80,768]{1,0:T(8,128)(2,1)S(1)}, u32[]{:S(2)}, u32[]{:S(2)}) collective-permute-start(bf16[80,768]{1,0:T(8,128)(2,1)S(1)} %broadcast_select_fusion.19), channel_id=1, source_target_pairs={{0,2},{1,3},{2,0},{3,1},{4,6},{5,7},{6,4},{7,5},{8,10},{9,11},{10,... | collective-permute-start | bytes 368648 | tf_op jit(solution)/shard_map/ppermute | solution.py:253
  472.0 6.1 %collective-permute-start.40 = (bf16[80,768]{1,0:T(8,128)(2,1)S(1)}, bf16[80,768]{1,0:T(8,128)(2,1)S(1)}, u32[]{:S(2)}, u32[]{:S(2)}) collective-permute-start(bf16[80,768]{1,0:T(8,128)(2,1)S(1)} %add_convert_fusion.13), channel_id=1, source_target_pairs={{0,2},{1,3},{2,0},{3,1},{4,6},{5,7},{6,4},{7,5},{8,10},{9,11},{10,... | collective-permute-start | bytes 368648 | tf_op jit(solution)/shard_map/ppermute | solution.py:253
  478.2 6.3 %collective-permute-start.41 = (bf16[160,768]{1,0:T(8,128)(2,1)S(1)}, bf16[160,768]{1,0:T(8,128)(2,1)S(1)}, u32[]{:S(2)}, u32[]{:S(2)}) collective-permute-start(bf16[160,768]{1,0:T(8,128)(2,1)S(1)} %pad_maximum_fusion.20), channel_id=1, source_target_pairs={{0,1},{1,0},{2,3},{3,2},{4,5},{5,4},{6,7},{7,6},{8,9},{9,8},{10,11... | collective-permute-start | bytes 737288 | tf_op jit(solution)/shard_map/ppermute | solution.py:253
  (110 other events, 1349.0 us)
Sparse Core Ops, SparseCore 0:
  11.0 37.4 all-gather.6
  51.0 63.8 all-gather.8
  116.7 38.9 all-gather.10
  158.1 38.9 all-gather.12
  328.0 50.2 all-gather.14
